TPU v7x, 32 devices: a whole 2x2x4 slice. The times are simulated.
32 devices in a mesh: dp: 4 (over z), ctx: 8 (over y, x, core).
Axes of the slice: x: 2, y: 2, z: 4, core: 2. Of those that a mesh axis runs over, the one named last changes fastest.
Arguments:
- inputs: bfloat16 [512, 8, 2048], P('ctx', 'dp'), may hold values from -8 to 8
- lengths: int32 [4, 2], P('dp'), may hold values from 1 to 512, as said below
- w_qkv: bfloat16 [2048, 6144], P(('dp', 'ctx')), may hold values from -0.125 to 0.125
- b_qkv: bfloat16 [6144], P(('dp', 'ctx')), may hold values from -0.5 to 0.5
- w_out: bfloat16 [2048, 2048], P(('dp', 'ctx')), may hold values from -1 to 1
- w_gate: bfloat16 [2048, 5632], P(('dp', 'ctx')), may hold values from -0.125 to 0.125
- w_up: bfloat16 [2048, 5632], P(('dp', 'ctx')), may hold values from -0.125 to 0.125
- w_down: bfloat16 [5632, 2048], P(('dp', 'ctx')), may hold values from -0.078125 to 0.078125
- gain_one: bfloat16 [2048], P(('dp', 'ctx')), may hold values from 0.25 to 1.75
- shift_one: bfloat16 [2048], P(('dp', 'ctx')), may hold values from -0.5 to 0.5
- gain_two: bfloat16 [2048], P(('dp', 'ctx')), may hold values from 0.25 to 1.75
- shift_two: bfloat16 [2048], P(('dp', 'ctx')), may hold values from -0.5 to 0.5
- cotangent: bfloat16 [512, 8, 2048], P('ctx', 'dp'), may hold values from -6 to 6
Outputs:
- output: bfloat16 [512, 8, 2048], P('ctx', 'dp')
- input_grad: float32 [512, 8, 2048], P('ctx', 'dp')
- grad_qkv: float32 [2048, 6144], P(('dp', 'ctx'))
- grad_bias: float32 [6144], P(('dp', 'ctx'))
- grad_out: float32 [2048, 2048], P(('dp', 'ctx'))
- grad_gate: float32 [2048, 5632], P(('dp', 'ctx'))
- grad_up: float32 [2048, 5632], P(('dp', 'ctx'))
- grad_down: float32 [5632, 2048], P(('dp', 'ctx'))
- grad_gain_one: float32 [2048], P(('dp', 'ctx'))
- grad_shift_one: float32 [2048], P(('dp', 'ctx'))
- grad_gain_two: float32 [2048], P(('dp', 'ctx'))
- grad_shift_two: float32 [2048], P(('dp', 'ctx'))
Inputs may be any that keep to these rules, and one draw needn't show every extreme that they name: In every row one slot, drawn from the seed, has length exactly 512; the other slots' lengths are drawn evenly from 1 to 512.
All inputs are finite; a program needn't handle non-finite values.
Results may differ from a plain program's by a relative error of at most 0.018.
Values may be sent and summed in bfloat16 or wider, within the bound.
A program may use at most 448 MiB of HBM per device.

v0:
```python
import math

import jax
import jax.numpy as jnp
from jax import lax
from jax.sharding import PartitionSpec as P

HEADS = 32
HEAD_DIM = 64
ROTARY = 16


epsilon = 1e-05
masked_value = -1e30


def layer_stats(values):
    row_mean = jnp.mean(values, -1, keepdims=True)
    centred = values - row_mean
    inverse = lax.rsqrt(jnp.mean(centred * centred, -1, keepdims=True) + epsilon)
    return (centred * inverse, inverse)


def norm_back(grad_normed, scaled, inverse, gain_vec):
    grad_hat = grad_normed * gain_vec
    return inverse * (
        grad_hat
        - jnp.mean(grad_hat, -1, keepdims=True)
        - scaled * jnp.mean(grad_hat * scaled, -1, keepdims=True)
    )


def rotary_tables(positions):
    counter = jnp.arange(ROTARY // 2, dtype=jnp.float32)
    frequency = 10000.0 ** (-2.0 * counter / ROTARY)
    angles = positions.astype(jnp.float32)[:, None] * frequency[None, :]
    return (jnp.cos(angles)[:, None, None, :], jnp.sin(angles)[:, None, None, :])


def rotate(values, cos_table, sin_table):
    half_dims = ROTARY // 2
    first_half = values[..., :half_dims]
    second_half = values[..., half_dims:ROTARY]
    return jnp.concatenate(
        [
            first_half * cos_table - second_half * sin_table,
            second_half * cos_table + first_half * sin_table,
            values[..., ROTARY:],
        ],
        -1,
    )


def over_blocks(step_fn, running, gathered):
    total_rows = gathered.shape[0]
    tile_rows = math.gcd(total_rows, 512)

    def visit_block(number, current):
        block_start = number * tile_rows
        block_part = lax.dynamic_slice_in_dim(gathered, block_start, tile_rows, 0)
        return step_fn(current, block_part, block_start)

    return lax.fori_loop(0, total_rows // tile_rows, visit_block, running)


def shards(
    inputs,
    lengths,
    w_qkv,
    b_qkv,
    w_out,
    w_gate,
    w_up,
    w_down,
    gain_one,
    shift_one,
    gain_two,
    shift_two,
    cotangent,
):
    local_rows, slot_count, width = inputs.shape
    positions = lax.axis_index("ctx") * local_rows + jnp.arange(local_rows, dtype=jnp.int32)
    live_rows = positions[:, None] < lengths[0][None, :]
    live_heads = jnp.transpose(live_rows)[:, None, :, None]
    cos_table, sin_table = rotary_tables(positions)

    def allowed_mask(offset, count):
        key_pos = offset + jnp.arange(count, dtype=jnp.int32)
        causal = key_pos[None, :] <= positions[:, None]
        return causal[None, None, :, :] & live_heads

    def split_heads(block_part):
        count = block_part.shape[0]
        key_part = block_part[:, :, 0].reshape(count, slot_count, HEADS, HEAD_DIM)
        value_part = block_part[:, :, 1].reshape(count, slot_count, HEADS, HEAD_DIM)
        return (key_part, value_part)

    attn_full = (
        lax.all_gather(w_qkv, ("dp", "ctx"), axis=0, tiled=True),
        lax.all_gather(b_qkv, ("dp", "ctx"), axis=0, tiled=True),
        lax.all_gather(w_out, ("dp", "ctx"), axis=0, tiled=True),
        lax.all_gather(gain_one, ("dp", "ctx"), axis=0, tiled=True),
        lax.all_gather(shift_one, ("dp", "ctx"), axis=0, tiled=True),
    )
    qkv_full, bias_full, out_full, gain_one_full, shift_one_full = attn_full
    source = inputs.astype(jnp.float32)
    scaled_one, inverse_one = layer_stats(source)
    normed_one = (
        scaled_one * gain_one_full.astype(jnp.float32) + shift_one_full.astype(jnp.float32)
    ).astype(jnp.bfloat16)
    joined = jnp.einsum(
        "rsd,de->rse", normed_one, qkv_full, preferred_element_type=jnp.float32
    ) + bias_full.astype(jnp.float32)
    query_pre = joined[..., :width].reshape(local_rows, slot_count, HEADS, HEAD_DIM)
    key_pre = joined[..., width : 2 * width].reshape(local_rows, slot_count, HEADS, HEAD_DIM)
    queries = rotate(query_pre, cos_table, sin_table).astype(jnp.bfloat16)
    keys_rot = rotate(key_pre, cos_table, sin_table).reshape(local_rows, slot_count, width)
    key_value = jnp.stack([keys_rot, joined[..., 2 * width :]], 2).astype(jnp.bfloat16)
    block_part = lax.all_gather(key_value, "ctx", axis=0, tiled=True)
    run_peak = jnp.full((slot_count, HEADS, local_rows), masked_value, jnp.float32)
    key_part, value_part = split_heads(block_part)
    scores = (
        jnp.einsum("qshd,kshd->shqk", queries, key_part, preferred_element_type=jnp.float32) * 0.125
    )
    allowed = allowed_mask(jnp.int32(0), block_part.shape[0])
    masked = jnp.where(allowed, scores, masked_value)
    new_peak = jnp.maximum(run_peak, jnp.max(masked, -1))
    weights = jnp.where(allowed, jnp.exp(masked - new_peak[..., None]), 0.0)
    new_sum = jnp.sum(weights, -1)
    new_acc = jnp.einsum(
        "shqk,kshd->shqd",
        weights.astype(jnp.bfloat16),
        value_part,
        preferred_element_type=jnp.float32,
    )
    final_sum = jnp.maximum(new_sum, 1.0)
    log_sum = new_peak + jnp.log(final_sum)
    attended = jnp.transpose(new_acc / final_sum[..., None], (2, 0, 1, 3))
    attended_low = attended.reshape(local_rows, slot_count, width).astype(jnp.bfloat16)
    hidden_in = source + jnp.einsum(
        "rsd,de->rse", attended_low, out_full, preferred_element_type=jnp.float32
    )
    mlp_full = (
        lax.all_gather(w_gate, ("dp", "ctx"), axis=0, tiled=True),
        lax.all_gather(w_up, ("dp", "ctx"), axis=0, tiled=True),
        lax.all_gather(w_down, ("dp", "ctx"), axis=0, tiled=True),
        lax.all_gather(gain_two, ("dp", "ctx"), axis=0, tiled=True),
        lax.all_gather(shift_two, ("dp", "ctx"), axis=0, tiled=True),
    )
    gate_full, up_full, down_full, gain_two_full, shift_two_full = mlp_full
    scaled_two, inverse_two = layer_stats(hidden_in)
    normed_two = (
        scaled_two * gain_two_full.astype(jnp.float32) + shift_two_full.astype(jnp.float32)
    ).astype(jnp.bfloat16)
    gate = jnp.einsum("rsd,df->rsf", normed_two, gate_full, preferred_element_type=jnp.float32)
    upward = jnp.einsum("rsd,df->rsf", normed_two, up_full, preferred_element_type=jnp.float32)
    sigmoid = jax.nn.sigmoid(gate)
    product = (gate * sigmoid * upward).astype(jnp.bfloat16)
    result = hidden_in + jnp.einsum(
        "rsf,fd->rsd", product, down_full, preferred_element_type=jnp.float32
    )
    gate_back, up_back, down_back, gain_two_back = (
        lax.all_gather(w_gate, ("dp", "ctx"), axis=0, tiled=True),
        lax.all_gather(w_up, ("dp", "ctx"), axis=0, tiled=True),
        lax.all_gather(w_down, ("dp", "ctx"), axis=0, tiled=True),
        lax.all_gather(gain_two, ("dp", "ctx"), axis=0, tiled=True),
    )
    grad_down = jnp.einsum("rsf,rsd->fd", product, cotangent, preferred_element_type=jnp.float32)
    grad_product = jnp.einsum(
        "rsd,fd->rsf", cotangent, down_back, preferred_element_type=jnp.float32
    )
    grad_gate_act = (grad_product * upward * sigmoid * (1.0 + gate * (1.0 - sigmoid))).astype(
        jnp.bfloat16
    )
    grad_up_act = (grad_product * gate * sigmoid).astype(jnp.bfloat16)
    grad_gate = jnp.einsum(
        "rsd,rsf->df", normed_two, grad_gate_act, preferred_element_type=jnp.float32
    )
    grad_up = jnp.einsum("rsd,rsf->df", normed_two, grad_up_act, preferred_element_type=jnp.float32)
    grad_normed_two = jnp.einsum(
        "rsf,df->rsd", grad_gate_act, gate_back, preferred_element_type=jnp.float32
    ) + jnp.einsum("rsf,df->rsd", grad_up_act, up_back, preferred_element_type=jnp.float32)
    grad_gain_two = jnp.sum(grad_normed_two * scaled_two, (0, 1))
    grad_shift_two = jnp.sum(grad_normed_two, (0, 1))
    grad_hidden = cotangent.astype(jnp.float32) + norm_back(
        grad_normed_two, scaled_two, inverse_two, gain_two_back.astype(jnp.float32)
    )
    mlp_sums = (
        lax.psum_scatter(grad_gate, ("dp", "ctx"), scatter_dimension=0, tiled=True),
        lax.psum_scatter(grad_up, ("dp", "ctx"), scatter_dimension=0, tiled=True),
        lax.psum_scatter(grad_down, ("dp", "ctx"), scatter_dimension=0, tiled=True),
        lax.psum_scatter(grad_gain_two, ("dp", "ctx"), scatter_dimension=0, tiled=True),
        lax.psum_scatter(grad_shift_two, ("dp", "ctx"), scatter_dimension=0, tiled=True),
    )
    qkv_back, out_back, gain_one_back = (
        lax.all_gather(w_qkv, ("dp", "ctx"), axis=0, tiled=True),
        lax.all_gather(w_out, ("dp", "ctx"), axis=0, tiled=True),
        lax.all_gather(gain_one, ("dp", "ctx"), axis=0, tiled=True),
    )
    hidden_low = grad_hidden.astype(jnp.bfloat16)
    grad_out = jnp.einsum(
        "rsd,rse->de", attended_low, hidden_low, preferred_element_type=jnp.float32
    )
    grad_attended = jnp.einsum(
        "rse,de->rsd", hidden_low, out_back, preferred_element_type=jnp.float32
    )
    grad_heads = grad_attended.reshape(local_rows, slot_count, HEADS, HEAD_DIM).astype(jnp.bfloat16)
    delta = jnp.transpose(jnp.sum(grad_heads.astype(jnp.float32) * attended, -1), (1, 2, 0))
    key_value_all = lax.all_gather(key_value, "ctx", axis=0, tiled=True)

    def grad_parts(block_part, offset):
        key_part, value_part = split_heads(block_part)
        scores = (
            jnp.einsum("qshd,kshd->shqk", queries, key_part, preferred_element_type=jnp.float32)
            * 0.125
        )
        allowed = allowed_mask(offset, block_part.shape[0])
        probs = jnp.where(allowed, jnp.exp(scores - log_sum[..., None]), 0.0)
        grad_prob = jnp.einsum(
            "qshd,kshd->shqk", grad_heads, value_part, preferred_element_type=jnp.float32
        )
        grad_score = (probs * (grad_prob - delta[..., None])).astype(jnp.bfloat16)
        return (key_part, probs, grad_score)

    def query_step(running, block_part, offset):
        key_part, probs, grad_score = grad_parts(block_part, offset)
        return running + jnp.einsum(
            "shqk,kshd->shqd", grad_score, key_part, preferred_element_type=jnp.float32
        )

    grad_query = (
        over_blocks(
            query_step,
            jnp.zeros((slot_count, HEADS, local_rows, HEAD_DIM), jnp.float32),
            key_value_all,
        )
        * 0.125
    )
    count = local_rows * lax.axis_size("ctx")
    tile_rows = math.gcd(count, 512)

    def one_block(number):
        block_start = number * tile_rows
        block_part = lax.dynamic_slice_in_dim(key_value_all, block_start, tile_rows, 0)
        key_part, probs, grad_score = grad_parts(block_part, block_start)
        grad_key = (
            jnp.einsum("shqk,qshd->kshd", grad_score, queries, preferred_element_type=jnp.float32)
            * 0.125
        )
        grad_value = jnp.einsum(
            "shqk,qshd->kshd",
            probs.astype(jnp.bfloat16),
            grad_heads,
            preferred_element_type=jnp.float32,
        )
        return jnp.stack(
            [
                grad_key.reshape(tile_rows, slot_count, width),
                grad_value.reshape(tile_rows, slot_count, width),
            ],
            2,
        )

    blocks = lax.map(one_block, jnp.arange(count // tile_rows, dtype=jnp.int32))
    grad_key_value = lax.psum_scatter(
        blocks.reshape(count, slot_count, 2, width).astype(jnp.bfloat16),
        "ctx",
        scatter_dimension=0,
        tiled=True,
    ).astype(jnp.float32)
    grad_query_pre = rotate(jnp.transpose(grad_query, (2, 0, 1, 3)), cos_table, -sin_table)
    grad_key_pre = rotate(
        grad_key_value[:, :, 0].reshape(local_rows, slot_count, HEADS, HEAD_DIM),
        cos_table,
        -sin_table,
    )
    grad_joined = jnp.concatenate(
        [
            grad_query_pre.reshape(local_rows, slot_count, width),
            grad_key_pre.reshape(local_rows, slot_count, width),
            grad_key_value[:, :, 1],
        ],
        -1,
    ).astype(jnp.bfloat16)
    grad_qkv = jnp.einsum(
        "rsd,rse->de", normed_one, grad_joined, preferred_element_type=jnp.float32
    )
    grad_bias = jnp.sum(grad_joined.astype(jnp.float32), (0, 1))
    grad_normed_one = jnp.einsum(
        "rse,de->rsd", grad_joined, qkv_back, preferred_element_type=jnp.float32
    )
    grad_gain_one = jnp.sum(grad_normed_one * scaled_one, (0, 1))
    grad_shift_one = jnp.sum(grad_normed_one, (0, 1))
    input_grad = grad_hidden + norm_back(
        grad_normed_one, scaled_one, inverse_one, gain_one_back.astype(jnp.float32)
    )
    attn_sums = (
        lax.psum_scatter(grad_qkv, ("dp", "ctx"), scatter_dimension=0, tiled=True),
        lax.psum_scatter(grad_bias, ("dp", "ctx"), scatter_dimension=0, tiled=True),
        lax.psum_scatter(grad_out, ("dp", "ctx"), scatter_dimension=0, tiled=True),
        lax.psum_scatter(grad_gain_one, ("dp", "ctx"), scatter_dimension=0, tiled=True),
        lax.psum_scatter(grad_shift_one, ("dp", "ctx"), scatter_dimension=0, tiled=True),
    )
    return (
        result.astype(jnp.bfloat16),
        input_grad,
        attn_sums[0],
        attn_sums[1],
        attn_sums[2],
        mlp_sums[0],
        mlp_sums[1],
        mlp_sums[2],
        attn_sums[3],
        attn_sums[4],
        mlp_sums[3],
        mlp_sums[4],
    )


def solution(mesh):
    placed = (
        P("ctx", "dp", None),
        P("dp", None),
        P(("dp", "ctx"), None),
        P(("dp", "ctx")),
        P(("dp", "ctx"), None),
        P(("dp", "ctx"), None),
        P(("dp", "ctx"), None),
        P(("dp", "ctx"), None),
        P(("dp", "ctx")),
        P(("dp", "ctx")),
        P(("dp", "ctx")),
        P(("dp", "ctx")),
        P("ctx", "dp", None),
    )
    return jax.shard_map(
        shards,
        mesh=mesh,
        in_specs=placed,
        out_specs=(
            P("ctx", "dp", None),
            P("ctx", "dp", None),
            P(("dp", "ctx"), None),
            P(("dp", "ctx")),
            P(("dp", "ctx"), None),
            P(("dp", "ctx"), None),
            P(("dp", "ctx"), None),
            P(("dp", "ctx"), None),
            P(("dp", "ctx")),
            P(("dp", "ctx")),
            P(("dp", "ctx")),
            P(("dp", "ctx")),
        ),
        check_vma=False,
    )
```

profile of v0, /device:TPU:1, one launch (start us, length us, event | category | flops | bytes accessed | tf_op | source)
XLA Modules:
  0.0 3022.0 jit_solution(7482063940186944125)
XLA Ops:
  13.0 43.2 %all-reduce.11 = (bf16[6144]{0:T(1024)(128)(2,1)S(1)}, bf16[2048]{0:T(1024)(128)(2,1)S(1)}, bf16[2048]{0:T(1024)(128)(2,1)S(1)}, bf16[2048]{0:T(1024)(128)(2,1)S(1)}, bf16[2048]{0:T(1024)(128)(2,1)S(1)}) all-reduce(bf16[6144]{0:T(1024)(128)(2,1)S(1)} %dynamic-update-slice.2, ...), channel_id=1, replica_groups=mesh['dp'=4,'ctx'=8] {'dp','ctx'}, use_global_device_ids=true, to_apply=%add.2 | all-reduce | flops 14336 | bytes 57344
  57.5 1.4 fusion.72
  59.6 110.1 %all-gather.7.cloned.1.call-done = bf16[2048,6144]{1,0:T(8,128)(2,1)} async-done(((bf16[64,6144]{1,0:T(8,128)(2,1)}), bf16[2048,6144]{1,0:T(8,128)(2,1)}) %all-gather.7.cloned.1.call-update) | async-done | bytes 25165840 | tf_op jit(solution)/shard_map/all_gather | solution.py:99
  169.8 10.5 fusion.20
  180.2 1.5 fusion.93
  181.7 3.2 copy.105
  184.9 3.2 copy.106
  188.0 1.5 slice.134
  192.2 2.4 copy.107
  194.7 2.2 pad_maximum_fusion.4
  199.5 115.9 %all-gather.17.cloned.1.call-done = bf16[5632,2048]{1,0:T(8,128)(2,1)} async-done(((bf16[176,2048]{1,0:T(8,128)(2,1)}), bf16[5632,2048]{1,0:T(8,128)(2,1)}) %all-gather.17.cloned.1.call-update) | async-done | bytes 23068688 | tf_op jit(solution)/shard_map/all_gather | solution.py:146
  315.4 13.7 fusion.4
  329.1 1.5 slice.135
  330.6 39.9 %all-gather.9.cloned.1.call-done = bf16[512,2,2,2048]{3,0,1,2:T(8,128)(2,1)} async-done(((bf16[64,2,2,2048]{3,0,1,2:T(8,128)(2,1)}), bf16[512,2,2,2048]{3,0,1,2:T(8,128)(2,1)}) %all-gather.9.cloned.1.call-update) | async-done | bytes 8388624 | tf_op jit(solution)/shard_map/all_gather | solution.py:119
  370.5 6.0 fusion.92
  376.6 6.3 copy.108
  382.8 6.2 copy.110
  389.1 3.4 select_reduce_fusion
  392.5 2.5 fusion.24
  395.0 1.7 copy-done
  397.7 3.8 fusion.95
  401.5 49.3 %all-gather.11.cloned.1.call-done = bf16[2048,2048]{1,0:T(8,128)(2,1)} async-done(((bf16[64,2048]{1,0:T(8,128)(2,1)}), bf16[2048,2048]{1,0:T(8,128)(2,1)}) %all-gather.11.cloned.1.call-update) | async-done | bytes 8388624 | tf_op jit(solution)/shard_map/all_gather | solution.py:101
  450.8 4.8 fusion.96
  456.1 140.6 %all-gather.15.cloned.1.call-done = bf16[2048,5632]{1,0:T(8,128)(2,1)} async-done(((bf16[64,5632]{1,0:T(8,128)(2,1)}), bf16[2048,5632]{1,0:T(8,128)(2,1)}) %all-gather.15.cloned.1.call-update) | async-done | bytes 23068688 | tf_op jit(solution)/shard_map/all_gather | solution.py:145
  596.7 12.3 fusion.10
  609.0 133.2 %all-gather.13.cloned.1.call-done = bf16[2048,5632]{1,0:T(8,128)(2,1)} async-done(((bf16[64,5632]{1,0:T(8,128)(2,1)}), bf16[2048,5632]{1,0:T(8,128)(2,1)}) %all-gather.13.cloned.1.call-update) | async-done | bytes 23068688 | tf_op jit(solution)/shard_map/all_gather | solution.py:144
  742.2 14.7 multiply_convert_fusion.3
  756.9 12.8 fusion.8
  769.7 14.2 multiply_reduce_fusion.1
  784.0 2.0 multiply_add_fusion
  785.9 7.1 fusion.54
  793.0 1.5 copy.114
  794.5 2.2 multiply_reduce_fusion
  796.8 7.2 fusion.39
  804.0 3.2 multiply_convert_fusion.1
  807.2 3.3 multiply_convert_fusion
  810.5 6.2 copy.117
  816.7 6.2 copy.118
  823.0 7.4 pad_maximum_fusion
  831.6 10.8 convolution_bitcast_fusion.4
  842.5 5.4 multiply_bitcast_fusion
  850.3 49.3 %reduce-scatter.7.cloned.1.call-done = bf16[64,2,2,2048]{3,0,1,2:T(8,128)(2,1)} async-done(((bf16[512,2,2,2048]{3,0,1,2:T(8,128)(2,1)}), bf16[64,2,2,2048]{3,0,1,2:T(8,128)(2,1)}) %reduce-scatter.7.cloned.1.call-update) | async-done | bytes 1048592 | tf_op jit(solution)/shard_map/reduce_scatter | solution.py:265
  899.6 2.3 fusion.94
  901.9 2.5 reshape_squeeze.14
  904.4 2.0 copy.119
  907.7 1.5 reshape_squeeze.15
  911.7 1.5 copy.130
  913.2 2.3 copy.120
  915.6 2.3 copy.121
  917.9 3.8 pad_maximum_fusion.6
  921.7 2.0 reshape.293
  923.8 21.3 convolution_bitcast_fusion.3
  945.2 19.9 convolution_bitcast_fusion.2
  965.2 19.7 convolution_bitcast_fusion.1
  986.0 19.7 convolution_bitcast_fusion
  1006.9 11.5 fusion.51
  1020.1 13.9 fusion.71
  1034.0 43.5 %all-reduce.10 = (f32[6144]{0:T(1024)S(1)}, f32[2048]{0:T(1024)S(1)}, f32[2048]{0:T(1024)S(1)}, f32[2048]{0:T(1024)S(1)}, f32[2048]{0:T(1024)S(1)}) all-reduce(f32[6144]{0:T(1024)S(1)} %convert_reduce_fusion, f32[2048]{0:T(1024)S(1)} %get-tuple-element.119, ...), channel_id=4, replica_groups=mesh['dp'=4,'ctx'=8] {'dp','ctx'}, use_global_device_ids=true, to_apply=%region_14.15.clone | all-reduce | flops 14336 | bytes 114688
  1080.4 1.8 copy.125
  1082.8 4.7 reduce-scatter.11.cloned.1.call-done
  1087.5 440.9 %reduce-scatter.9.cloned.1.call-done = f32[64,6144]{1,0:T(8,128)} async-done(((f32[2048,6144]{1,0:T(8,128)}), f32[64,6144]{1,0:T(8,128)}) %reduce-scatter.9.cloned.1.call-update) | async-done | bytes 1572880 | tf_op jit(solution)/shard_map/reduce_scatter | solution.py:298
  1528.4 494.5 %reduce-scatter.13.cloned.1.call-done = f32[64,5632]{1,0:T(8,128)} async-done(((f32[2048,5632]{1,0:T(8,128)}), f32[64,5632]{1,0:T(8,128)}) %reduce-scatter.13.cloned.1.call-update) | async-done | bytes 1441808 | tf_op jit(solution)/shard_map/reduce_scatter | solution.py:189
  2022.9 496.1 %reduce-scatter.15.cloned.1.call-done = f32[64,5632]{1,0:T(8,128)} async-done(((f32[2048,5632]{1,0:T(8,128)}), f32[64,5632]{1,0:T(8,128)}) %reduce-scatter.15.cloned.1.call-update) | async-done | bytes 1441808 | tf_op jit(solution)/shard_map/reduce_scatter | solution.py:190
  2519.0 495.9 %reduce-scatter.17.cloned.1.call-done = f32[176,2048]{1,0:T(8,128)} async-done(((f32[5632,2048]{1,0:T(8,128)}), f32[176,2048]{1,0:T(8,128)}) %reduce-scatter.17.cloned.1.call-update) | async-done | bytes 1441808 | tf_op jit(solution)/shard_map/reduce_scatter | solution.py:191
  (133 shorter events, 29.5 us)
Async XLA Ops:
  7.2 162.6 %all-gather.7.cloned.1.call-start = ((), (), s32[]{:S(2)}) async-start(), calls=%async_computation.6 | async-start | bytes 25952256 | tf_op jit(solution)/shard_map/all_gather | solution.py:99
  7.9 307.5 %all-gather.17.cloned.1.call-start = ((), (), s32[]{:S(2)}) async-start(), calls=%async_computation.11 | async-start | bytes 23789568 | tf_op jit(solution)/shard_map/all_gather | solution.py:146
  8.7 361.9 %all-gather.9.cloned.1.call-start = ((), (), s32[]{:S(2)}) async-start(), calls=%async_computation.7 | async-start | bytes 9437184 | tf_op jit(solution)/shard_map/all_gather | solution.py:119
  192.2 7.0 copy-start.27
  194.7 120.8 %copy-start.11 = (bf16[64,2,2048]{2,1,0:T(2,128)(2,1)S(1)}, bf16[64,2,2048]{2,1,0:T(2,128)(2,1)}, u32[]{:S(2)}) copy-start(bf16[64,2,2048]{2,1,0:T(2,128)(2,1)} %param.25) | copy-start | bytes 1572868
  196.9 253.9 %all-gather.11.cloned.1.call-start = ((), (), s32[]{:S(2)}) async-start(), calls=%async_computation.8 | async-start | bytes 8650752 | tf_op jit(solution)/shard_map/all_gather | solution.py:101
  197.4 399.2 %all-gather.15.cloned.1.call-start = ((), (), s32[]{:S(2)}) async-start(), calls=%async_computation.10 | async-start | bytes 23789568 | tf_op jit(solution)/shard_map/all_gather | solution.py:145
  198.0 544.2 %all-gather.13.cloned.1.call-start = ((), (), s32[]{:S(2)}) async-start(), calls=%async_computation.9 | async-start | bytes 23789568 | tf_op jit(solution)/shard_map/all_gather | solution.py:144
  198.6 701.0 %reduce-scatter.7.cloned.1.call-start = ((), (), s32[]{:S(2)}) async-start(), calls=%async_computation.12 | async-start | bytes 9437184 | tf_op jit(solution)/shard_map/reduce_scatter | solution.py:265
  330.6 58.4 %copy-start.9 = (bf16[64,2,32,48]{0,3,2,1:T(8,128)(2,1)}, bf16[64,2,32,48]{0,3,2,1:T(8,128)(2,1)S(1)}, u32[]{:S(2)}) copy-start(bf16[64,2,32,48]{0,3,2,1:T(8,128)(2,1)S(1)} %slice.135) | copy-start | bytes 1179652
  392.5 4.3 copy-start
  392.5 5.2 copy-start.5
  397.7 53.1 %copy-start.4 = (bf16[64,2,2048]{2,1,0:T(2,128)(2,1)S(1)}, bf16[64,2,2048]{2,1,0:T(2,128)(2,1)}, u32[]{:S(2)}) copy-start(bf16[64,2,2048]{2,1,0:T(2,128)(2,1)} %param.13) | copy-start | bytes 1572868
  401.5 54.1 %copy-start.14 = (bf16[64,2,32,64]{0,3,2,1:T(8,128)(2,1)}, bf16[64,2,32,64]{0,3,2,1:T(8,128)(2,1)S(1)}, u32[]{:S(2)}) copy-start(bf16[64,2,32,64]{0,3,2,1:T(8,128)(2,1)S(1)} %get-tuple-element.163) | copy-start | bytes 1572868
  455.5 328.4 %copy-start.2 = (f32[64,2,2048]{2,0,1:T(8,128)}, f32[64,2,2048]{2,0,1:T(8,128)S(1)}, u32[]{:S(2)}) copy-start(f32[64,2,2048]{2,0,1:T(8,128)S(1)} %get-tuple-element.166) | copy-start | bytes 3145732
  455.8 153.2 %copy-start.24 = (f32[64,2]{0,1:T(2,128)}, f32[64,2]{0,1:T(2,128)S(1)}, u32[]{:S(2)}) copy-start(f32[64,2]{0,1:T(2,128)S(1)} %add_rsqrt_fusion) | copy-start | bytes 1540
  756.9 12.8 copy-start.8
  756.9 12.8 copy-start.7
  756.9 12.9 copy-start.25
  794.5 9.4 slice-start
  796.7 7.2 slice-start.1
  796.8 7.2 copy-start.6
  804.0 3.2 copy-start.10
  807.2 3.3 copy-start.1
  830.4 1.2 copy-start.15
  830.4 257.1 %reduce-scatter.11.cloned.1.call-start = ((), (), s32[]{:S(2)}) async-start(), calls=%async_computation.14 | async-start | bytes 17301504 | tf_op jit(solution)/shard_map/reduce_scatter | solution.py:300
  842.4 686.0 %reduce-scatter.9.cloned.1.call-start = ((), (), s32[]{:S(2)}) async-start(), calls=%async_computation.13 | async-start | bytes 51904512 | tf_op jit(solution)/shard_map/reduce_scatter | solution.py:298
  847.9 1.4 copy-start.13
  901.9 7.3 copy-start.26
  906.4 4.0 copy-start.21
  913.2 31.9 %copy-start.16 = (bf16[64,2,2048]{2,0,1:T(8,128)(2,1)}, bf16[64,2,2048]{2,0,1:T(8,128)(2,1)S(1)}, u32[]{:S(2)}) copy-start(bf16[64,2,2048]{2,0,1:T(8,128)(2,1)S(1)} %copy.130) | copy-start | bytes 1572868
  923.8 21.3 copy-start.18
  945.2 1077.7 %reduce-scatter.13.cloned.1.call-start = ((), (), s32[]{:S(2)}) async-start(), calls=%async_computation.15 | async-start | bytes 47579136 | tf_op jit(solution)/shard_map/reduce_scatter | solution.py:189
  965.2 1553.8 %reduce-scatter.15.cloned.1.call-start = ((), (), s32[]{:S(2)}) async-start(), calls=%async_computation.16 | async-start | bytes 47579136 | tf_op jit(solution)/shard_map/reduce_scatter | solution.py:190
  984.9 1.0 copy-start.12
  985.0 2029.9 %reduce-scatter.17.cloned.1.call-start = ((), (), s32[]{:S(2)}) async-start(), calls=%async_computation.17 | async-start | bytes 47579136 | tf_op jit(solution)/shard_map/reduce_scatter | solution.py:191
  1005.7 1.2 copy-start.3
  1006.9 12.9 copy-start.17
  1006.9 12.9 copy-start.19
  1006.9 12.9 copy-start.20
  1020.1 13.9 copy-start.22
  1020.1 13.9 copy-start.23
Sparse Core Ops, SparseCore 0:
  10.9 158.8 all-gather.6
  172.6 142.7 all-gather.16
  317.9 52.6 all-gather.8
  373.3 77.4 all-gather.10
  453.4 143.1 all-gather.14
  599.4 142.7 all-gather.12
  830.6 69.0 reduce-scatter.6
  902.6 184.8 reduce-scatter.10
  1095.7 432.6 reduce-scatter.8
  1531.2 491.6 reduce-scatter.12
  2025.9 493.0 reduce-scatter.14
  2521.8 493.0 reduce-scatter.16
where the time goes:
time: 3030 us; the launch traced here: 3020 us
  waiting for transfers between devices  2570 us (85%)
  matrix products  233 us (8%)
  blocking collectives  86.6 us (3%)
  local copies, waits for them, and re-layouts  80.9 us (3%)
  other arithmetic  31.7 us (1%)
    reduce_scatter x1, waiting for transfers between devices, shards(): lax.psum_scatter(grad_up, ('dp', 'ctx'), scatter_dimension=0, tiled=True)  496 us
    reduce_scatter x1, waiting for transfers between devices, shards(): lax.psum_scatter(grad_down, ('dp', 'ctx'), scatter_dimension=0, tiled=True)  496 us
    reduce_scatter x1, waiting for transfers between devices, shards(): lax.psum_scatter(grad_gate, ('dp', 'ctx'), scatter_dimension=0, tiled=True)  495 us
    reduce_scatter x1, waiting for transfers between devices, shards(): lax.psum_scatter(grad_qkv, ('dp', 'ctx'), scatter_dimension=0, tiled=True)  441 us
    all_gather x1, waiting for transfers between devices, shards(): lax.all_gather(w_up, ('dp', 'ctx'), axis=0, tiled=True)  141 us
    all_gather x1, waiting for transfers between devices, shards(): lax.all_gather(w_gate, ('dp', 'ctx'), axis=0, tiled=True)  133 us
    all_gather x1, waiting for transfers between devices, shards(): lax.all_gather(w_down, ('dp', 'ctx'), axis=0, tiled=True)  116 us
    all_gather x1, waiting for transfers between devices, shards(): lax.all_gather(w_qkv, ('dp', 'ctx'), axis=0, tiled=True)  110 us
  transfers between devices with their start and end apart: 12, of which 12 were waited for; matrix products, arithmetic and copies ran while one was open for 8% of the time, Pallas kernels for 0%

commit v1 on v0

--- a/solution.py
+++ b/solution.py
@@ -63,7 +63,7 @@
     return lax.fori_loop(0, total_rows // tile_rows, visit_block, running)
 
 
-def shards(
+def gathered_shards(
     inputs,
     lengths,
     w_qkv,
@@ -317,7 +317,222 @@
     )
 
 
+def tensor_shards(
+    inputs,
+    lengths,
+    w_qkv,
+    b_qkv,
+    w_out,
+    w_gate,
+    w_up,
+    w_down,
+    gain_one,
+    shift_one,
+    gain_two,
+    shift_two,
+    cotangent,
+):
+    rows, slots, width = inputs.shape
+    f32, b16 = jnp.float32, jnp.bfloat16
+    zs, n = lax.axis_size("dp"), lax.axis_size("ctx")
+    me = lax.axis_index("ctx")
+    local = rows * slots
+    tokens = local * n
+    seq = rows * n
+    wrows = w_qkv.shape[0]
+    ff_block = w_down.shape[0]
+    heads = HEADS // n
+    hc = heads * HEAD_DIM
+    ffc = ff_block * zs
+
+    def dot(a, b, dims):
+        return lax.dot_general(a, b, (dims, ((), ())), preferred_element_type=f32)
+
+    def local_tokens(v):
+        return jnp.transpose(v, (1, 0, 2)).reshape(local, width)
+
+    def back_tokens(v):
+        return jnp.transpose(v.reshape(slots, rows, width), (1, 0, 2))
+
+    def exchange(v):
+        return lax.all_to_all(v, "ctx", 0, 0, tiled=True)
+
+    def gather_ctx(v):
+        return lax.all_gather(v, "ctx", axis=0, tiled=True)
+
+    def scatter_ctx(v):
+        return lax.psum_scatter(v.astype(b16), "ctx", scatter_dimension=0, tiled=True).astype(f32)
+
+    def gather_dp(v):
+        return lax.all_gather(v, "dp", axis=0, tiled=True)
+
+    def scatter_dp(v):
+        return lax.psum_scatter(v.astype(b16), "dp", scatter_dimension=0, tiled=True)
+
+    xs = local_tokens(inputs)
+    dy = local_tokens(cotangent)
+    qkv_send = jnp.transpose(w_qkv.reshape(wrows, 3, zs, n, HEAD_DIM), (3, 0, 1, 2, 4)).reshape(
+        n, wrows, 3 * hc
+    )
+
+    def ff_send(w):
+        return jnp.transpose(w.reshape(wrows, zs, n, ff_block), (2, 0, 1, 3)).reshape(
+            n, wrows, ffc
+        )
+
+    gu_send = jnp.concatenate([ff_send(w_gate), ff_send(w_up)], -1)
+    small = lax.all_gather(
+        jnp.concatenate([b_qkv, gain_one, shift_one, gain_two, shift_two]), ("dp", "ctx"), axis=0
+    ).astype(f32)
+    nb = b_qkv.shape[0]
+    bias_full = small[:, :nb].reshape(3, zs, n, HEAD_DIM)
+    bias_own = lax.dynamic_index_in_dim(bias_full, me, 2, keepdims=False).reshape(1, 3 * hc)
+    g1, s1, g2, s2 = [
+        small[:, nb + i * wrows : nb + (i + 1) * wrows].reshape(1, width) for i in range(4)
+    ]
+
+    w_qkv_c = gather_dp(exchange(qkv_send).reshape(n * wrows, 3 * hc))
+    w_gu_c = gather_dp(exchange(gu_send).reshape(n * wrows, 2 * ffc))
+    w_out_c = gather_dp(w_out)
+    w_down_c = gather_dp(w_down)
+
+    counter = jnp.arange(ROTARY // 2, dtype=f32)
+    angles = jnp.arange(seq, dtype=f32)[:, None] * (10000.0 ** (-2.0 * counter / ROTARY))[None, :]
+    cos_t, sin_t = jnp.cos(angles), jnp.sin(angles)
+    zero = jnp.zeros_like(sin_t)
+    rest = jnp.ones((seq, HEAD_DIM - ROTARY), f32)
+    table_c = jnp.tile(jnp.concatenate([cos_t, cos_t, rest], -1), (1, heads))
+    table_l = jnp.tile(jnp.concatenate([-sin_t, zero, 0 * rest], -1), (1, heads))
+    table_r = jnp.tile(jnp.concatenate([zero, sin_t, 0 * rest], -1), (1, heads))
+
+    def by_slot(v):
+        return v.reshape(n, slots, rows, v.shape[-1]).transpose(1, 0, 2, 3).reshape(
+            slots, seq, v.shape[-1]
+        )
+
+    def by_device(v):
+        return v.reshape(slots, n, rows, v.shape[-1]).transpose(1, 0, 2, 3).reshape(
+            tokens, v.shape[-1]
+        )
+
+    def turn(v, sign):
+        half = ROTARY // 2
+        return (
+            v * table_c
+            + sign * jnp.roll(v, -half, -1) * table_l
+            + sign * jnp.roll(v, half, -1) * table_r
+        )
+
+    x32 = xs.astype(f32)
+    n1, r1 = layer_stats(x32)
+    a1 = (n1 * g1 + s1).astype(b16)
+    a1_all = gather_ctx(a1)
+    joined = by_slot(dot(a1_all, w_qkv_c, ((1,), (0,))) + bias_own)
+    q = turn(joined[..., :hc], 1.0).astype(b16)
+    k = turn(joined[..., hc : 2 * hc], 1.0).astype(b16)
+    v = joined[..., 2 * hc :].astype(b16)
+
+    def heads_of(t):
+        return t.reshape(slots, seq, heads, HEAD_DIM)
+
+    at = jnp.arange(seq, dtype=jnp.int32)
+    allowed = (at[None, :] <= at[:, None])[None] & (at[None, :, None] < lengths[0][:, None, None])
+    scores = jnp.einsum("sqhd,skhd->shqk", heads_of(q), heads_of(k), preferred_element_type=f32)
+    scores = jnp.where(allowed[:, None], scores * 0.125, masked_value)
+    peak = jnp.max(scores, -1, keepdims=True)
+    weights = jnp.where(allowed[:, None], jnp.exp(scores - peak), 0.0)
+    probs = (weights / jnp.maximum(jnp.sum(weights, -1, keepdims=True), 1.0)).astype(b16)
+    attended = jnp.einsum("shqk,skhd->sqhd", probs, heads_of(v), preferred_element_type=f32)
+    ob = by_device(attended.reshape(slots, seq, hc).astype(b16))
+    hidden = x32 + scatter_ctx(dot(ob, w_out_c, ((1,), (0,))))
+    n2, r2 = layer_stats(hidden)
+    a2_all = gather_ctx((n2 * g2 + s2).astype(b16))
+
+    gu = dot(a2_all, w_gu_c, ((1,), (0,)))
+    gate, up = gu[:, :ffc], gu[:, ffc:]
+    sig = jax.nn.sigmoid(gate)
+    z = (gate * sig * up).astype(b16)
+    result = hidden + scatter_ctx(dot(z, w_down_c, ((1,), (0,))))
+    dy_all = gather_ctx(dy)
+    grad_down = scatter_dp(dot(z, dy_all, ((0,), (0,)))).astype(f32)
+    dz = dot(dy_all, w_down_c, ((1,), (1,)))
+    dg = (dz * up * sig * (1.0 + gate * (1.0 - sig))).astype(b16)
+    du = (dz * gate * sig).astype(b16)
+    dgu = jnp.concatenate([dg, du], -1)
+    grad_gu = exchange(scatter_dp(dot(a2_all, dgu, ((0,), (0,)))).reshape(n, wrows, 2 * ffc))
+    da2 = scatter_ctx(dot(dgu, w_gu_c, ((1,), (1,))))
+    gain_two_part = jnp.sum(da2 * n2, 0)
+    shift_two_part = jnp.sum(da2, 0)
+    dh = dy.astype(f32) + norm_back(da2, n2, r2, g2)
+    dh_all = gather_ctx(dh.astype(b16))
+
+    grad_out = scatter_dp(dot(ob, dh_all, ((0,), (0,)))).astype(f32)
+    do = heads_of(by_slot(dot(dh_all, w_out_c, ((1,), (1,))).astype(b16)))
+    dp = jnp.einsum("sqhd,skhd->shqk", do, heads_of(v), preferred_element_type=f32)
+    p32 = probs.astype(f32)
+    ds = (p32 * (dp - jnp.sum(p32 * dp, -1, keepdims=True))).astype(b16)
+    dq = jnp.einsum("shqk,skhd->sqhd", ds, heads_of(k), preferred_element_type=f32) * 0.125
+    dk = jnp.einsum("shqk,sqhd->skhd", ds, heads_of(q), preferred_element_type=f32) * 0.125
+    dv = jnp.einsum("shqk,sqhd->skhd", probs, do, preferred_element_type=f32)
+    dj = by_device(
+        jnp.concatenate(
+            [
+                turn(dq.reshape(slots, seq, hc), -1.0),
+                turn(dk.reshape(slots, seq, hc), -1.0),
+                dv.reshape(slots, seq, hc),
+            ],
+            -1,
+        ).astype(b16)
+    )
+    grad_qkv = exchange(scatter_dp(dot(a1_all, dj, ((0,), (0,)))).reshape(n, wrows, 3 * hc))
+    bias_part = jnp.sum(dj.astype(f32), 0).reshape(3, zs, 1, HEAD_DIM)
+    da1 = scatter_ctx(dot(dj, w_qkv_c, ((1,), (1,))))
+    gain_one_part = jnp.sum(da1 * n1, 0)
+    shift_one_part = jnp.sum(da1, 0)
+    input_grad = dh + norm_back(da1, n1, r1, g1)
+
+    own = (jnp.arange(n) == me)[None, None, :, None]
+    devices = zs * n
+    pieces = jnp.concatenate(
+        [
+            jnp.where(own, bias_part, 0.0).reshape(devices, nb),
+            gain_one_part.reshape(devices, wrows),
+            shift_one_part.reshape(devices, wrows),
+            gain_two_part.reshape(devices, wrows),
+            shift_two_part.reshape(devices, wrows),
+        ],
+        -1,
+    )
+    summed = lax.psum_scatter(pieces, ("dp", "ctx"), scatter_dimension=0, tiled=True)[0]
+
+    def ff_back(part):
+        return jnp.transpose(part.reshape(n, wrows, zs, ff_block), (1, 2, 0, 3)).reshape(
+            wrows, zs * n * ff_block
+        ).astype(f32)
+
+    grad_qkv = jnp.transpose(grad_qkv.reshape(n, wrows, 3, zs, HEAD_DIM), (1, 2, 3, 0, 4)).reshape(
+        wrows, 3 * width
+    ).astype(f32)
+    return (
+        back_tokens(result.astype(b16)),
+        back_tokens(input_grad),
+        grad_qkv,
+        summed[:nb],
+        grad_out,
+        ff_back(grad_gu[..., :ffc]),
+        ff_back(grad_gu[..., ffc:]),
+        grad_down,
+        summed[nb : nb + wrows],
+        summed[nb + wrows : nb + 2 * wrows],
+        summed[nb + 2 * wrows : nb + 3 * wrows],
+        summed[nb + 3 * wrows :],
+    )
+
+
 def solution(mesh):
+    zs, n = mesh.shape["dp"], mesh.shape["ctx"]
+    shards = tensor_shards if HEADS == zs * n else gathered_shards
+
     placed = (
         P("ctx", "dp", None),
         P("dp", None),

time: 3030 us -> 1030 us (0.34)
  waiting for transfers between devices: 2570 us -> 597 us
  matrix products: 233 us -> 115 us
  blocking collectives: 86.6 us -> 135 us
    reduce_scatter x6 -> x8, waiting for transfers between devices: 1980 us -> 306 us  [the longest x4 162 us: scatter_ctx(): lax.psum_scatter(v.astype(b16), 'ctx', scatter_dimension=0, tiled=True)]
    all_gather x6 -> x8, waiting for transfers between devices: 589 us -> 289 us  [the longest x4 161 us: gather_dp(): return lax.all_gather(v, 'dp', axis=0, tiled=True)]
    dot_general x21 -> x17, matrix products: 233 us -> 107 us  [the longest x12 93 us: dot(): return lax.dot_general(a, b, (dims, ((), ())), preferred_element_type=f32)]
    all_to_all x0 -> x2, blocking collectives: none -> 49.8 us  [exchange(): return lax.all_to_all(v, 'ctx', 0, 0, tiled=True)]
  transfers between devices with their start and end apart: 12 -> 18, of which waited for: 12 -> 15; matrix products, arithmetic and copies ran while one was open for 8% -> 21% of each run, Pallas kernels for 0% -> 0%
where the time goes in v1:
time: 1030 us; the launch traced here: 1020 us
  waiting for transfers between devices  597 us (58%)
  blocking collectives  135 us (13%)
  matrix products  115 us (11%)
  local copies, waits for them, and re-layouts  98.5 us (10%)
  other arithmetic  45 us (4%)
  between operations  15.2 us (1%)
  starting transfers between devices  10.5 us (1%)
    reduce_scatter x4, waiting for transfers between devices, scatter_ctx(): lax.psum_scatter(v.astype(b16), 'ctx', scatter_dimension=0, tiled=True)  162 us
    all_gather x4, waiting for transfers between devices, gather_dp(): return lax.all_gather(v, 'dp', axis=0, tiled=True)  161 us
    reduce_scatter x4, waiting for transfers between devices, scatter_dp(): lax.psum_scatter(v.astype(b16), 'dp', scatter_dimension=0, tiled=True)  145 us
    all_gather x4, waiting for transfers between devices, gather_ctx(): return lax.all_gather(v, 'ctx', axis=0, tiled=True)  129 us
    dot_general x12, matrix products, dot(): return lax.dot_general(a, b, (dims, ((), ())), preferred_element_type=f32)  93 us
    unnamed x2, blocking collectives  85.7 us
    all_to_all x2, blocking collectives, exchange(): return lax.all_to_all(v, 'ctx', 0, 0, tiled=True)  49.8 us
  transfers between devices with their start and end apart: 18, of which 15 were waited for; matrix products, arithmetic and copies ran while one was open for 21% of the time, Pallas kernels for 0%

profile of v1, /device:TPU:1, one launch (start us, length us, event | category | flops | bytes accessed | tf_op | source)
XLA Modules:
  0.0 1017.4 jit_solution(7689406156359768548)
XLA Ops:
  7.2 2.5 reshape.328
  11.4 16.4 %all_to_all.20 = bf16[8,64,768]{2,1,0:T(8,128)(2,1)} all-to-all(bf16[8,64,768]{2,1,0:T(8,128)(2,1)S(1)} %reshape.329), channel_id=1, replica_groups=mesh['dp'=4,'ctx'=8] {'ctx'}, dimensions={0} | all-to-all | bytes 1572864 | tf_op jit(solution)/shard_map/all_to_all | solution.py:358
  28.2 44.7 %all-reduce = bf16[14336]{0:T(1024)(128)(2,1)S(1)} all-reduce(bf16[14336]{0:T(1024)(128)(2,1)S(1)} %dynamic-update-slice), channel_id=2, replica_groups=mesh['dp'=4,'ctx'=8] {'dp','ctx'}, use_global_device_ids=true, to_apply=%add | all-reduce | flops 14336 | bytes 57344
  84.3 8.1 all-gather.12.cloned.1.call-done
  92.4 38.2 %all-gather.10.cloned.1.call-done = bf16[1024,2048]{1,0:T(8,128)(2,1)} async-done(((bf16[128,2048]{1,0:T(8,128)(2,1)}), bf16[1024,2048]{1,0:T(8,128)(2,1)}) %all-gather.10.cloned.1.call-update) | async-done | bytes 4194320 | tf_op jit(solution)/shard_map/all_gather | solution.py:361
  130.6 6.7 convolution_add_fusion
  139.6 2.1 fusion.33
  141.7 2.0 copy.158
  145.2 8.6 fusion.58
  153.8 4.6 divide_convert_fusion
  158.5 2.0 copy-done
  162.6 4.6 convolution_convert_fusion.3
  168.3 3.0 reshape.338
  173.9 3.9 reshape.340
  182.9 33.4 %all_to_all.21 = bf16[8,64,1408]{2,1,0:T(8,128)(2,1)} all-to-all(bf16[8,64,1408]{2,1,0:T(8,128)(2,1)S(1)} %pad_maximum_fusion.3), channel_id=1, replica_groups=mesh['dp'=4,'ctx'=8] {'ctx'}, dimensions={0} | all-to-all | bytes 2883584 | tf_op jit(solution)/shard_map/all_to_all | solution.py:358
  216.5 14.4 %reduce-scatter.9.cloned.1.call-done = bf16[128,2048]{1,0:T(8,128)(2,1)} async-done(((bf16[1024,2048]{1,0:T(8,128)(2,1)}), bf16[128,2048]{1,0:T(8,128)(2,1)}) %reduce-scatter.9.cloned.1.call-update) | async-done | bytes 524304 | tf_op jit(solution)/shard_map/reduce_scatter | solution.py:364
  235.6 103.8 %all-gather.18.cloned.1.call-done = bf16[2048,1408]{1,0:T(8,128)(2,1)} async-done(((bf16[512,1408]{1,0:T(8,128)(2,1)}), bf16[2048,1408]{1,0:T(8,128)(2,1)}) %all-gather.18.cloned.1.call-update) | async-done | bytes 5767184 | tf_op jit(solution)/shard_map/all_gather | solution.py:367
  339.4 37.7 %all-gather.16.cloned.1.call-done = bf16[1024,2048]{1,0:T(8,128)(2,1)} async-done(((bf16[128,2048]{1,0:T(8,128)(2,1)}), bf16[1024,2048]{1,0:T(8,128)(2,1)}) %all-gather.16.cloned.1.call-update) | async-done | bytes 4194320 | tf_op jit(solution)/shard_map/all_gather | solution.py:361
  377.1 11.7 %fusion.59 = f32[1024,1408]{1,0:T(8,128)} fusion(bf16[1024,2048]{1,0:T(8,128)(2,1)} %all-gather.16.cloned.1.call-done, bf16[2048,1408]{1,0:T(8,128)(2,1)} %all-gather.18.cloned.1.call-done), kind=kOutput, calls=%fused_computation.147 | convolution fusion | flops 5905580032 | bytes 15728640 | tf_op jit(solution)/shard_map/dot_general | solution.py:349
  388.8 48.7 %all-gather.20.cloned.1.call-done = bf16[704,2048]{1,0:T(8,128)(2,1)} async-done(((bf16[176,2048]{1,0:T(8,128)(2,1)}), bf16[704,2048]{1,0:T(8,128)(2,1)}) %all-gather.20.cloned.1.call-update) | async-done | bytes 2883600 | tf_op jit(solution)/shard_map/all_gather | solution.py:367
  437.5 38.5 %all-gather.22.cloned.1.call-done = bf16[1024,2048]{1,0:T(8,128)(2,1)} async-done(((bf16[128,2048]{1,0:T(8,128)(2,1)}), bf16[1024,2048]{1,0:T(8,128)(2,1)}) %all-gather.22.cloned.1.call-update) | async-done | bytes 4194320 | tf_op jit(solution)/shard_map/all_gather | solution.py:361
  476.1 10.2 %multiply_convert_fusion.1 = (bf16[1024,704]{1,0:T(8,128)(2,1)S(1)}, bf16[1024,704]{1,0:T(8,128)(2,1)S(1)}, bf16[1024,704]{1,0:T(8,128)(2,1)}) fusion(f32[1024,1408]{1,0:T(8,128)} %fusion.59, bf16[1024,2048]{1,0:T(8,128)(2,1)} %all-gather.22.cloned.1.call-done, bf16[704,2048]{1,0:T(8,128)(2,1)} %all-gather.20.cloned.1.call-done), kind=kOutput, calls=%fused_computation.23 | convolution fusion | flops 2964324352 | bytes 17170432 | tf_op jit(solution)/shard_map/dot_general | solution.py:349
  487.9 11.0 %convolution_convert_fusion.1 = bf16[1024,2048]{1,0:T(8,128)(2,1)} fusion(bf16[2048,1408]{1,0:T(8,128)(2,1)} %all-gather.18.cloned.1.call-done, bf16[1024,704]{1,0:T(8,128)(2,1)S(1)} %get-tuple-element.27, bf16[1024,704]{1,0:T(8,128)(2,1)S(1)} %get-tuple-element.26), kind=kOutput, calls=%fused_computation.14 | convolution fusion | flops 5913444352 | bytes 12845056 | tf_op jit(solution)/shard_map/dot_general | solution.py:349
  498.9 7.7 convolution_convert_fusion.2
  506.7 43.2 %reduce-scatter.13.cloned.1.call-done = bf16[128,2048]{1,0:T(8,128)(2,1)} async-done(((bf16[1024,2048]{1,0:T(8,128)(2,1)}), bf16[128,2048]{1,0:T(8,128)(2,1)}) %reduce-scatter.13.cloned.1.call-update) | async-done | bytes 524304 | tf_op jit(solution)/shard_map/reduce_scatter | solution.py:364
  550.0 2.1 fusion.29
  552.1 52.5 %reduce-scatter.11.cloned.1.call-done = bf16[128,2048]{1,0:T(8,128)(2,1)} async-done(((bf16[1024,2048]{1,0:T(8,128)(2,1)}), bf16[128,2048]{1,0:T(8,128)(2,1)}) %reduce-scatter.11.cloned.1.call-update) | async-done | bytes 524304 | tf_op jit(solution)/shard_map/reduce_scatter | solution.py:364
  604.5 3.2 fusion.48
  608.2 11.3 %convolution_convert_fusion = bf16[2048,1408]{1,0:T(8,128)(2,1)} fusion(bf16[1024,2048]{1,0:T(8,128)(2,1)} %all-gather.16.cloned.1.call-done, bf16[1024,704]{1,0:T(8,128)(2,1)} %copy-done.40, bf16[1024,704]{1,0:T(8,128)(2,1)} %copy-done.39), kind=kOutput, calls=%fused_computation.8 | convolution fusion | flops 5914230784 | bytes 12845056 | tf_op jit(solution)/shard_map/dot_general | solution.py:349
  619.6 7.4 convolution_convert_fusion.6
  630.7 14.3 %all-gather.24.cloned.1.call-done = bf16[1024,2048]{1,0:T(8,128)(2,1)} async-done(((bf16[128,2048]{1,0:T(8,128)(2,1)}), bf16[1024,2048]{1,0:T(8,128)(2,1)}) %all-gather.24.cloned.1.call-update) | async-done | bytes 4194320 | tf_op jit(solution)/shard_map/all_gather | solution.py:361
  645.0 3.8 convolution_convert_fusion.10
  650.0 3.7 fusion.1
  653.7 5.1 fusion.2
  663.4 2.0 copy.176
  666.9 2.0 copy.178
  670.9 3.1 convolution_multiply_fusion.1
  677.1 2.0 copy.171
  684.4 4.4 convolution_convert_fusion.7
  689.1 4.7 fusion.20
  693.8 2.6 concatenate.96
  696.3 5.9 fusion.9
  702.2 4.3 convert_reduce_fusion
  706.6 3.7 copy.180
  710.3 6.9 convolution_convert_fusion.4
  717.3 7.3 convolution_convert_fusion.5
  724.7 24.5 %reduce-scatter.21.cloned.1.call-done = bf16[512,1408]{1,0:T(8,128)(2,1)} async-done(((bf16[2048,1408]{1,0:T(8,128)(2,1)}), bf16[512,1408]{1,0:T(8,128)(2,1)}) %reduce-scatter.21.cloned.1.call-update) | async-done | bytes 1441808 | tf_op jit(solution)/shard_map/reduce_scatter | solution.py:370
  749.2 4.5 all-to-all-start.3
  753.8 54.4 %reduce-scatter.23.cloned.1.call-done = bf16[176,2048]{1,0:T(8,128)(2,1)} async-done(((bf16[704,2048]{1,0:T(8,128)(2,1)}), bf16[176,2048]{1,0:T(8,128)(2,1)}) %reduce-scatter.23.cloned.1.call-update) | async-done | bytes 720912 | tf_op jit(solution)/shard_map/reduce_scatter | solution.py:370
  808.1 2.4 convert_element_type.202
  812.0 2.2 slice_convert_fusion.1
  814.2 3.0 reshape.363
  817.2 2.6 copy.206
  819.7 3.3 reshape.360
  823.0 3.0 reshape.364
  826.1 2.6 copy.205
  828.6 3.4 reshape.361
  832.2 5.2 reduce-scatter.19.cloned.1.call-done
  839.2 51.6 %reduce-scatter.15.cloned.1.call-done = bf16[128,2048]{1,0:T(8,128)(2,1)} async-done(((bf16[1024,2048]{1,0:T(8,128)(2,1)}), bf16[128,2048]{1,0:T(8,128)(2,1)}) %reduce-scatter.15.cloned.1.call-update) | async-done | bytes 524304 | tf_op jit(solution)/shard_map/reduce_scatter | solution.py:364
  892.5 60.7 %reduce-scatter.17.cloned.1.call-done = bf16[512,768]{1,0:T(8,128)(2,1)} async-done(((bf16[2048,768]{1,0:T(8,128)(2,1)}), bf16[512,768]{1,0:T(8,128)(2,1)}) %reduce-scatter.17.cloned.1.call-update) | async-done | bytes 786448 | tf_op jit(solution)/shard_map/reduce_scatter | solution.py:370
  953.2 4.5 all-to-all-start.2
  960.1 40.9 %all-reduce.1 = f32[32,448]{1,0:T(8,128)S(1)} all-reduce(f32[32,448]{1,0:T(8,128)S(1)} %concatenate.98), channel_id=8, replica_groups=mesh['dp'=4,'ctx'=8] {'dp','ctx'}, use_global_device_ids=true, to_apply=%region_21.22.clone | all-reduce | flops 14336 | bytes 114688
  1002.2 2.5 reshape.362
  1004.7 3.7 copy.204
  (224 shorter events, 67.3 us)
Async XLA Ops:
  7.2 85.2 %all-gather.12.cloned.1.call-start = ((), (), s32[]{:S(2)}) async-start(), calls=%async_computation.13 | async-start | bytes 3932160 | tf_op jit(solution)/shard_map/all_gather | solution.py:367
  10.4 17.5 %copy-start.33 = (bf16[192]{0:T(256)(128)(2,1)S(1)}, bf16[192]{0:T(256)(128)(2,1)}, u32[]{:S(2)}) copy-start(bf16[192]{0:T(256)(128)(2,1)} %param.16) | copy-start | bytes 1156
  10.4 17.5 %copy-start.34 = (bf16[64]{0:T(256)(128)(2,1)S(1)}, bf16[64]{0:T(256)(128)(2,1)}, u32[]{:S(2)}) copy-start(bf16[64]{0:T(256)(128)(2,1)} %param.21) | copy-start | bytes 388
  10.4 17.5 %copy-start.35 = (bf16[64]{0:T(256)(128)(2,1)S(1)}, bf16[64]{0:T(256)(128)(2,1)}, u32[]{:S(2)}) copy-start(bf16[64]{0:T(256)(128)(2,1)} %param.22) | copy-start | bytes 388
  10.4 17.5 %copy-start.36 = (bf16[64]{0:T(256)(128)(2,1)S(1)}, bf16[64]{0:T(256)(128)(2,1)}, u32[]{:S(2)}) copy-start(bf16[64]{0:T(256)(128)(2,1)} %param.23) | copy-start | bytes 388
  10.4 17.5 %copy-start.37 = (bf16[64]{0:T(256)(128)(2,1)S(1)}, bf16[64]{0:T(256)(128)(2,1)}, u32[]{:S(2)}) copy-start(bf16[64]{0:T(256)(128)(2,1)} %param.24) | copy-start | bytes 388
  10.4 63.5 %copy-start.3 = (bf16[64,2,2048]{2,1,0:T(2,128)(2,1)S(1)}, bf16[64,2,2048]{2,1,0:T(2,128)(2,1)}, u32[]{:S(2)}) copy-start(bf16[64,2,2048]{2,1,0:T(2,128)(2,1)} %param.13) | copy-start | bytes 1572868
  27.8 102.9 %all-gather.10.cloned.1.call-start = ((), (), s32[]{:S(2)}) async-start(), calls=%async_computation.12 | async-start | bytes 4718592 | tf_op jit(solution)/shard_map/all_gather | solution.py:361
  73.8 4.0 copy-start.23
  76.7 1.9 copy-start.29
  76.7 1.8 copy-start.31
  77.8 84.8 %all-gather.14.cloned.1.call-start = ((), (), s32[]{:S(2)}) async-start(), calls=%async_computation.14 | async-start | bytes 1310720 | tf_op jit(solution)/shard_map/all_gather | solution.py:367
  78.6 152.4 %reduce-scatter.9.cloned.1.call-start = ((), (), s32[]{:S(2)}) async-start(), calls=%async_computation.15 | async-start | bytes 4718592 | tf_op jit(solution)/shard_map/reduce_scatter | solution.py:364
  78.7 4.5 copy-start.38
  138.2 1.1 copy-start.17
  138.2 1.2 copy-start.18
  138.2 1.4 copy-start.19
  145.0 8.9 copy-start.14
  145.2 13.3 %copy-start.6 = (bf16[2,512,256]{1,2,0:T(8,128)(2,1)}, bf16[2,512,256]{1,2,0:T(8,128)(2,1)S(1)}, u32[]{:S(2)}) copy-start(bf16[2,512,256]{1,2,0:T(8,128)(2,1)S(1)} %copy.154) | copy-start | bytes 1572868
  158.5 2.0 copy-start
  162.6 4.7 copy-start.10
  167.2 1.1 copy-start.20
  167.2 172.2 %all-gather.18.cloned.1.call-start = ((), (), s32[]{:S(2)}) async-start(), calls=%async_computation.17 | async-start | bytes 7208960 | tf_op jit(solution)/shard_map/all_gather | solution.py:367
  181.2 35.1 %copy-start.26 = (f32[32,64]{1,0:T(8,128)S(1)}, f32[32,64]{1,0:T(8,128)}, u32[]{:S(2)}) copy-start(f32[32,64]{1,0:T(8,128)} %get-tuple-element.56) | copy-start | bytes 24580
  181.2 35.2 %copy-start.25 = (f32[32,64]{1,0:T(8,128)S(1)}, f32[32,64]{1,0:T(8,128)}, u32[]{:S(2)}) copy-start(f32[32,64]{1,0:T(8,128)} %get-tuple-element.57) | copy-start | bytes 24580
  216.3 160.8 %all-gather.16.cloned.1.call-start = ((), (), s32[]{:S(2)}) async-start(), calls=%async_computation.16 | async-start | bytes 4718592 | tf_op jit(solution)/shard_map/all_gather | solution.py:361
  216.5 17.8 %copy-start.21 = (bf16[64,2,2048]{2,1,0:T(2,128)(2,1)S(1)}, bf16[64,2,2048]{2,1,0:T(2,128)(2,1)}, u32[]{:S(2)}) copy-start(bf16[64,2,2048]{2,1,0:T(2,128)(2,1)} %param.25) | copy-start | bytes 1572868
  233.5 204.0 %all-gather.20.cloned.1.call-start = ((), (), s32[]{:S(2)}) async-start(), calls=%async_computation.18 | async-start | bytes 3604480 | tf_op jit(solution)/shard_map/all_gather | solution.py:367
  234.3 241.8 %all-gather.22.cloned.1.call-start = ((), (), s32[]{:S(2)}) async-start(), calls=%async_computation.20 | async-start | bytes 4718592 | tf_op jit(solution)/shard_map/all_gather | solution.py:361
  235.3 314.6 %reduce-scatter.13.cloned.1.call-start = ((), (), s32[]{:S(2)}) async-start(), calls=%async_computation.21 | async-start | bytes 4718592 | tf_op jit(solution)/shard_map/reduce_scatter | solution.py:364
  486.2 1.2 copy-start.39
  486.2 1.7 copy-start.40
  498.9 105.6 %reduce-scatter.11.cloned.1.call-start = ((), (), s32[]{:S(2)}) async-start(), calls=%async_computation.19 | async-start | bytes 4718592 | tf_op jit(solution)/shard_map/reduce_scatter | solution.py:364
  506.7 97.9 %copy-start.4 = (bf16[2,64,2048]{2,1,0:T(8,128)(2,1)S(1)}, bf16[2,64,2048]{2,1,0:T(8,128)(2,1)}, u32[]{:S(2)}) copy-start(bf16[2,64,2048]{2,1,0:T(8,128)(2,1)} %copy.165) | copy-start | bytes 1572868
  506.7 138.3 %all-gather.24.cloned.1.call-start = ((), (), s32[]{:S(2)}) async-start(), calls=%async_computation.22 | async-start | bytes 4718592 | tf_op jit(solution)/shard_map/all_gather | solution.py:361
  607.7 141.5 %reduce-scatter.21.cloned.1.call-start = ((), (), s32[]{:S(2)}) async-start(), calls=%async_computation.26 | async-start | bytes 7208960 | tf_op jit(solution)/shard_map/reduce_scatter | solution.py:370
  619.5 188.6 %reduce-scatter.23.cloned.1.call-start = ((), (), s32[]{:S(2)}) async-start(), calls=%async_computation.27 | async-start | bytes 3604480 | tf_op jit(solution)/shard_map/reduce_scatter | solution.py:370
  627.0 1.3 copy-start.22
  627.0 210.4 %reduce-scatter.19.cloned.1.call-start = ((), (), s32[]{:S(2)}) async-start(), calls=%async_computation.25 | async-start | bytes 1310720 | tf_op jit(solution)/shard_map/reduce_scatter | solution.py:370
  648.8 1.2 copy-start.7
  650.0 3.7 copy-start.5
  653.7 5.1 copy-start.16
  658.8 3.0 copy-start.1
  668.9 2.0 copy-start.15
  682.6 1.8 copy-start.11
  688.8 201.9 %reduce-scatter.15.cloned.1.call-start = ((), (), s32[]{:S(2)}) async-start(), calls=%async_computation.23 | async-start | bytes 4718592 | tf_op jit(solution)/shard_map/reduce_scatter | solution.py:364
  689.1 7.3 copy-start.2
  696.3 5.9 copy-start.9
  717.2 235.9 %reduce-scatter.17.cloned.1.call-start = ((), (), s32[]{:S(2)}) async-start(), calls=%async_computation.24 | async-start | bytes 3932160 | tf_op jit(solution)/shard_map/reduce_scatter | solution.py:370
  724.7 85.8 %copy-start.28 = (f32[2048]{0:T(1024)S(1)}, f32[2048]{0:T(1024)}, u32[]{:S(2)}) copy-start(f32[2048]{0:T(1024)} %get-tuple-element.12) | copy-start | bytes 24580
  724.7 85.9 %copy-start.27 = (f32[2048]{0:T(1024)S(1)}, f32[2048]{0:T(1024)}, u32[]{:S(2)}) copy-start(f32[2048]{0:T(1024)} %get-tuple-element.18) | copy-start | bytes 24580
  724.7 86.0 %copy-start.12 = (bf16[128,2048]{1,0:T(8,128)(2,1)S(1)}, bf16[128,2048]{1,0:T(8,128)(2,1)}, u32[]{:S(2)}) copy-start(bf16[128,2048]{1,0:T(8,128)(2,1)} %get-tuple-element.51) | copy-start | bytes 1572868
  749.2 62.8 %all-to-all-start.3 = ((bf16[8,64,1408]{2,1,0:T(8,128)(2,1)}), bf16[8,64,1408]{2,1,0:T(8,128)(2,1)S(1)}, u32[]{:S(2)}, u32[]{:S(2)}) async-start(bf16[8,64,1408]{2,1,0:T(8,128)(2,1)} %bitcast.215), calls=%async_computation.10 | async-start | bytes 2883584 | tf_op jit(solution)/shard_map/all_to_all | solution.py:358
  828.6 62.1 %copy-start.24 = (f32[2048]{0:T(1024)S(1)}, f32[2048]{0:T(1024)}, u32[]{:S(2)}) copy-start(f32[2048]{0:T(1024)} %copy-done.23) | copy-start | bytes 24580
  828.6 62.1 %copy-start.30 = (f32[128]{0:T(128)S(1)}, f32[128]{0:T(128)}, u32[]{:S(2)}) copy-start(f32[128]{0:T(128)} %copy-done.29) | copy-start | bytes 1540
  828.6 62.1 %copy-start.32 = (f32[128]{0:T(128)S(1)}, f32[128]{0:T(128)}, u32[]{:S(2)}) copy-start(f32[128]{0:T(128)} %copy-done.31) | copy-start | bytes 1540
  828.6 129.0 %copy-start.8 = (f32[128,2048]{1,0:T(8,128)S(1)}, f32[128,2048]{1,0:T(8,128)}, u32[]{:S(2)}) copy-start(f32[128,2048]{1,0:T(8,128)} %get-tuple-element.23) | copy-start | bytes 3145732
  890.8 66.9 %copy-start.13 = (bf16[128,2048]{1,0:T(8,128)(2,1)S(1)}, bf16[128,2048]{1,0:T(8,128)(2,1)}, u32[]{:S(2)}) copy-start(bf16[128,2048]{1,0:T(8,128)(2,1)} %reduce-scatter.15.cloned.1.call-done) | copy-start | bytes 1572868
  953.2 49.0 %all-to-all-start.2 = ((bf16[8,64,768]{2,1,0:T(8,128)(2,1)}), bf16[8,64,768]{2,1,0:T(8,128)(2,1)S(1)}, u32[]{:S(2)}, u32[]{:S(2)}) async-start(bf16[8,64,768]{2,1,0:T(8,128)(2,1)} %bitcast.217), calls=%async_computation.7 | async-start | bytes 1572864 | tf_op jit(solution)/shard_map/all_to_all | solution.py:358
Sparse Core Ops, SparseCore 0:
  27.9 64.4 all-gather.11
  94.9 35.7 all-gather.9
  132.2 27.3 all-gather.13
  167.4 63.5 reduce-scatter.8
  232.5 106.9 all-gather.17
  341.9 35.2 all-gather.15
  378.8 58.7 all-gather.19
  440.2 35.8 all-gather.21
  499.0 50.8 reduce-scatter.12
  553.2 51.3 reduce-scatter.10
  607.8 37.1 all-gather.23
  647.3 101.8 reduce-scatter.20
  751.6 56.4 reduce-scatter.22
  810.4 26.9 reduce-scatter.18
  840.6 50.1 reduce-scatter.14
  893.0 60.0 reduce-scatter.16

commit v2 on v1

--- a/solution.py
+++ b/solution.py
@@ -1,8 +1,12 @@
+import functools
+import itertools
 import math
 
 import jax
 import jax.numpy as jnp
 from jax import lax
+from jax.experimental import pallas as pl
+from jax.experimental.pallas import tpu as pltpu
 from jax.sharding import PartitionSpec as P
 
 HEADS = 32
@@ -315,6 +319,257 @@
         mlp_sums[3],
         mlp_sums[4],
     )
+
+
+MESH = pl.DeviceIdType.MESH
+HBM = pl.BlockSpec(memory_space=pltpu.HBM)
+VMEM = pl.BlockSpec(memory_space=pltpu.VMEM)
+
+
+def flip(index, mask):
+    for bit in (1, 2, 4):
+        if mask & bit:
+            index = index + bit - 2 * bit * ((index // bit) % 2)
+    return index
+
+
+class Wires:
+    def __init__(self, send, recv):
+        self.send, self.recv = send, recv
+        self.z, self.c = lax.axis_index("dp"), lax.axis_index("ctx")
+        self.inner = (self.z == 1) | (self.z == 2)
+        self.outer = (self.z == 0) | (self.z == 3)
+        self.number = itertools.count()
+
+    def put(self, src, dst, z_mask, c_mask):
+        i = next(self.number)
+        return pltpu.make_async_remote_copy(
+            src_ref=src,
+            dst_ref=dst,
+            send_sem=self.send.at[i],
+            recv_sem=self.recv.at[i],
+            device_id=(flip(self.z, z_mask), flip(self.c, c_mask)),
+            device_id_type=MESH,
+        )
+
+    def greet(self, zs, n):
+        barrier = pltpu.get_barrier_semaphore()
+        for m in range(1, zs):
+            pl.semaphore_signal(
+                barrier, inc=1, device_id=(flip(self.z, m), self.c), device_id_type=MESH
+            )
+        for m in range(1, n):
+            pl.semaphore_signal(
+                barrier, inc=1, device_id=(self.z, flip(self.c, m)), device_id_type=MESH
+            )
+        pl.semaphore_wait(barrier, zs + n - 2)
+
+
+class DepthGather:
+    def __init__(self, wires, part):
+        z = wires.z
+        self.wires = wires
+        self.near = wires.put(part(z), part(z), 1, 0)
+        self.skip = wires.put(part(z), part(z), 2, 0)
+        self.mid = wires.put(part(z), part(z), 3, 0)
+        far = flip(z, 2)
+        self.on = wires.put(part(far), part(far), 1, 0)
+
+    def start(self):
+        self.skip.start()
+        pl.when(self.wires.inner)(self.mid.start)
+        self.near.start()
+
+    def forward(self):
+        @pl.when(self.wires.inner)
+        def _():
+            self.skip.wait_recv()
+            self.on.start()
+
+    def finish(self):
+        self.near.wait_recv()
+        self.near.wait_send()
+        self.skip.wait_send()
+
+        @pl.when(self.wires.inner)
+        def _():
+            self.mid.wait_recv()
+            self.mid.wait_send()
+            self.on.wait_send()
+
+        @pl.when(self.wires.outer)
+        def _():
+            self.skip.wait_recv()
+            self.on.wait_recv()
+
+
+class LayerGather:
+    def __init__(self, wires, buf, source=None):
+        c = wires.c
+        mine = buf.at[c] if source is None else source
+        self.direct = {m: wires.put(mine, buf.at[c], 0, m) for m in (2, 4, 6, 1)}
+        self.on = {
+            m: wires.put(buf.at[flip(c, m)], buf.at[flip(c, m)], 0, 1) for m in (2, 4, 6)
+        }
+
+    def start(self):
+        for m in (2, 4, 6, 1):
+            self.direct[m].start()
+
+    def forward(self, m):
+        self.direct[m].wait_recv()
+        self.on[m].start()
+
+    def arrived(self, m):
+        (self.direct[1] if m == 1 else self.on[m - 1]).wait_recv()
+
+    def sent(self):
+        for copy in (*self.direct.values(), *self.on.values()):
+            copy.wait_send()
+
+
+def pack_columns(dst, refs, n, zs):
+    for i in range(n):
+        pieces = []
+        for ref, block in refs:
+            pieces += [ref[:, block * (j * n + i) : block * (j * n + i + 1)] for j in range(zs)]
+        dst[i] = jnp.concatenate(pieces, -1)
+
+
+def spread_kernel(
+    zs,
+    n,
+    w_qkv,
+    w_gate,
+    w_up,
+    w_out,
+    xs,
+    dy,
+    small,
+    qkv_all,
+    out_all,
+    gu_own,
+    xs_all,
+    dy_all,
+    small_all,
+    qkv_send,
+    gu_send,
+    send,
+    recv,
+    local,
+):
+    wires = Wires(send, recv)
+    z, c = wires.z, wires.c
+    hc = HEAD_DIM * HEADS // n
+    width = HEADS * HEAD_DIM
+    ff_block = w_gate.shape[1] // (zs * n)
+
+    own = [
+        pltpu.make_async_copy(w_out, out_all.at[z], local.at[0]),
+        pltpu.make_async_copy(qkv_send.at[c], qkv_all.at[z, c], local.at[1]),
+        pltpu.make_async_copy(gu_send.at[c], gu_own.at[c], local.at[2]),
+        pltpu.make_async_copy(xs, xs_all.at[c], local.at[3]),
+        pltpu.make_async_copy(dy, dy_all.at[c], local.at[4]),
+        pltpu.make_async_copy(small, small_all.at[z, c], local.at[5]),
+    ]
+    for i in (0, 3, 4, 5):
+        own[i].start()
+    pack_columns(
+        qkv_send, [(w_qkv.at[:, i * width : (i + 1) * width], HEAD_DIM) for i in range(3)], n, zs
+    )
+    own[1].start()
+    wires.greet(zs, n)
+    for i in (0, 5):
+        own[i].wait()
+
+    out_z = DepthGather(wires, lambda i: out_all.at[i])
+    out_z.start()
+    qkv_x = [
+        wires.put(qkv_send.at[flip(c, m)], qkv_all.at[z, c], 0, m) for m in range(1, n)
+    ]
+    for copy in qkv_x:
+        copy.start()
+    small_z = [wires.put(small_all.at[z, c], small_all.at[z, c], m, 0) for m in range(1, zs)]
+    for copy in small_z:
+        copy.start()
+    xs_g = LayerGather(wires, xs_all, xs)
+    xs_g.start()
+    pack_columns(gu_send, [(w_gate, ff_block), (w_up, ff_block)], n, zs)
+    own[2].start()
+    for copy in small_z:
+        copy.wait_recv()
+    small_x = [
+        wires.put(small_all.at[:, c], small_all.at[:, c], 0, m) for m in range(1, n)
+    ]
+    for copy in small_x:
+        copy.start()
+    own[1].wait()
+    for copy in qkv_x:
+        copy.wait_recv()
+    half = n // 2
+    qkv_z = [
+        DepthGather(wires, lambda i, p=p: qkv_all.at[i, p * half : (p + 1) * half])
+        for p in range(2)
+    ]
+    for part in qkv_z:
+        part.start()
+    out_z.forward()
+    gu_x = [wires.put(gu_send.at[flip(c, m)], gu_own.at[c], 0, m) for m in range(1, n)]
+    for copy in gu_x:
+        copy.start()
+    for m in (2, 4, 6):
+        xs_g.forward(m)
+    dy_g = LayerGather(wires, dy_all, dy)
+    dy_g.start()
+    qkv_z[0].forward()
+    for m in (2, 4, 6):
+        dy_g.forward(m)
+    qkv_z[1].forward()
+
+    for i in (2, 3, 4):
+        own[i].wait()
+    for group in (xs_g, dy_g):
+        for m in (1, 3, 5, 7):
+            group.arrived(m)
+        group.sent()
+    for copy in small_z:
+        copy.wait_send()
+    for copy in qkv_x:
+        copy.wait_send()
+    for copy in (*small_x, *gu_x):
+        copy.wait()
+    for part in (out_z, *qkv_z):
+        part.finish()
+
+
+def spread(zs, n, w_qkv, w_gate, w_up, w_out, xs, dy, small):
+    wrows, width = w_out.shape
+    qc, gc = w_qkv.shape[1] // n, 2 * w_gate.shape[1] // n
+    b16 = jnp.bfloat16
+    return pl.pallas_call(
+        functools.partial(spread_kernel, zs, n),
+        out_shape=[
+            jax.ShapeDtypeStruct((zs, n, wrows, qc), b16),
+            jax.ShapeDtypeStruct((zs, wrows, width), b16),
+            jax.ShapeDtypeStruct((n, wrows, gc), b16),
+            jax.ShapeDtypeStruct((n, *xs.shape), b16),
+            jax.ShapeDtypeStruct((n, *dy.shape), b16),
+            jax.ShapeDtypeStruct((zs, n, *small.shape), small.dtype),
+        ],
+        in_specs=[VMEM, VMEM, VMEM, HBM, HBM, HBM, HBM],
+        out_specs=[HBM] * 6,
+        scratch_shapes=[
+            pltpu.VMEM((n, wrows, qc), b16),
+            pltpu.VMEM((n, wrows, gc), b16),
+            pltpu.SemaphoreType.DMA((64,)),
+            pltpu.SemaphoreType.DMA((64,)),
+            pltpu.SemaphoreType.DMA((6,)),
+        ],
+        compiler_params=pltpu.CompilerParams(
+            collective_id=1, has_side_effects=True, vmem_limit_bytes=32 << 20
+        ),
+        name="spread",
+    )(w_qkv, w_gate, w_up, w_out, xs, dy, small)
 
 
 def tensor_shards(
@@ -371,19 +626,15 @@
 
     xs = local_tokens(inputs)
     dy = local_tokens(cotangent)
-    qkv_send = jnp.transpose(w_qkv.reshape(wrows, 3, zs, n, HEAD_DIM), (3, 0, 1, 2, 4)).reshape(
-        n, wrows, 3 * hc
-    )
-
-    def ff_send(w):
-        return jnp.transpose(w.reshape(wrows, zs, n, ff_block), (2, 0, 1, 3)).reshape(
-            n, wrows, ffc
-        )
-
-    gu_send = jnp.concatenate([ff_send(w_gate), ff_send(w_up)], -1)
-    small = lax.all_gather(
-        jnp.concatenate([b_qkv, gain_one, shift_one, gain_two, shift_two]), ("dp", "ctx"), axis=0
-    ).astype(f32)
+    small = jnp.concatenate([b_qkv, gain_one, shift_one, gain_two, shift_two]).astype(f32)
+    small = jnp.pad(small, (0, 1024 - small.shape[0])).reshape(8, 128)
+    w_qkv_c, w_out_c, gu_own, a_all, dy_all, small = spread(
+        zs, n, w_qkv, w_gate, w_up, w_out, xs, dy, small
+    )
+    small = small.reshape(zs * n, 1024)
+    dy_all = dy_all.reshape(tokens, width)
+    w_qkv_c = w_qkv_c.reshape(width, 3 * hc)
+    w_out_c = w_out_c.reshape(hc, width)
     nb = b_qkv.shape[0]
     bias_full = small[:, :nb].reshape(3, zs, n, HEAD_DIM)
     bias_own = lax.dynamic_index_in_dim(bias_full, me, 2, keepdims=False).reshape(1, 3 * hc)
@@ -391,9 +642,7 @@
         small[:, nb + i * wrows : nb + (i + 1) * wrows].reshape(1, width) for i in range(4)
     ]
 
-    w_qkv_c = gather_dp(exchange(qkv_send).reshape(n * wrows, 3 * hc))
-    w_gu_c = gather_dp(exchange(gu_send).reshape(n * wrows, 2 * ffc))
-    w_out_c = gather_dp(w_out)
+    w_gu_c = gather_dp(gu_own.reshape(n * wrows, 2 * ffc))
     w_down_c = gather_dp(w_down)
 
     counter = jnp.arange(ROTARY // 2, dtype=f32)
@@ -425,8 +674,7 @@
 
     x32 = xs.astype(f32)
     n1, r1 = layer_stats(x32)
-    a1 = (n1 * g1 + s1).astype(b16)
-    a1_all = gather_ctx(a1)
+    a1_all = (layer_stats(a_all.reshape(tokens, width).astype(f32))[0] * g1 + s1).astype(b16)
     joined = by_slot(dot(a1_all, w_qkv_c, ((1,), (0,))) + bias_own)
     q = turn(joined[..., :hc], 1.0).astype(b16)
     k = turn(joined[..., hc : 2 * hc], 1.0).astype(b16)
@@ -453,7 +701,6 @@
     sig = jax.nn.sigmoid(gate)
     z = (gate * sig * up).astype(b16)
     result = hidden + scatter_ctx(dot(z, w_down_c, ((1,), (0,))))
-    dy_all = gather_ctx(dy)
     grad_down = scatter_dp(dot(z, dy_all, ((0,), (0,)))).astype(f32)
     dz = dot(dy_all, w_down_c, ((1,), (1,)))
     dg = (dz * up * sig * (1.0 + gate * (1.0 - sig))).astype(b16)
@@ -531,7 +778,7 @@
 
 def solution(mesh):
     zs, n = mesh.shape["dp"], mesh.shape["ctx"]
-    shards = tensor_shards if HEADS == zs * n else gathered_shards
+    shards = tensor_shards if (zs, n) == (4, 8) and HEADS == 32 else gathered_shards
 
     placed = (
         P("ctx", "dp", None),

time: 1030 us -> 891 us (0.87)
  waiting for transfers between devices: 597 us -> 445 us
  blocking collectives: 135 us -> 38.9 us
  Pallas kernels: 0 us -> 86.6 us
  local copies, waits for them, and re-layouts: 98.5 us -> 120 us
  other arithmetic: 45 us -> 55.5 us
    pallas_call x0 -> x1, Pallas kernels: none -> 86.6 us  [spread(): pl.pallas_call(functools.partial(spread_kernel, zs, n), out_shape=[jax.Sh...]
    all_gather x4 -> x2, waiting for transfers between devices: 129 us -> 52 us  [gather_ctx(): return lax.all_gather(v, 'ctx', axis=0, tiled=True)]
    all_gather x4 -> x2, waiting for transfers between devices: 161 us -> 100 us  [gather_dp(): return lax.all_gather(v, 'dp', axis=0, tiled=True)]
    reduce_scatter x4, waiting for transfers between devices: 145 us -> 88.4 us  [scatter_dp(): lax.psum_scatter(v.astype(b16), 'dp', scatter_dimension=0, tiled=True)]
    all_to_all x2 -> x0, blocking collectives: 49.8 us -> none  [exchange(): return lax.all_to_all(v, 'ctx', 0, 0, tiled=True)]
    unnamed x2 -> x1, blocking collectives: 85.7 us -> 38.9 us
    reduce_scatter x4, waiting for transfers between devices: 162 us -> 203 us  [scatter_ctx(): lax.psum_scatter(v.astype(b16), 'ctx', scatter_dimension=0, tiled=True)]
    reshape x9 -> x0, local copies, waits for them, and re-layouts: 16.9 us -> none  [the longest x4 10.2 us: ff_send(): w.reshape(wrows, zs, n, ff_block)]
  transfers between devices with their start and end apart: 18 -> 14, of which waited for: 15 -> 10; matrix products, arithmetic and copies ran while one was open for 21% -> 20% of each run, Pallas kernels for 0% -> 0%
where the time goes in v2:
time: 891 us; the launch traced here: 883 us
  waiting for transfers between devices  445 us (50%)
  local copies, waits for them, and re-layouts  120 us (13%)
  matrix products  110 us (12%)
  Pallas kernels  86.6 us (10%)
  other arithmetic  55.5 us (6%)
  blocking collectives  38.9 us (4%)
  between operations  16.3 us (2%)
  starting transfers between devices  10.9 us (1%)
    reduce_scatter x4, waiting for transfers between devices, scatter_ctx(): lax.psum_scatter(v.astype(b16), 'ctx', scatter_dimension=0, tiled=True)  203 us
    all_gather x2, waiting for transfers between devices, gather_dp(): return lax.all_gather(v, 'dp', axis=0, tiled=True)  100 us
    reduce_scatter x4, waiting for transfers between devices, scatter_dp(): lax.psum_scatter(v.astype(b16), 'dp', scatter_dimension=0, tiled=True)  88.4 us
    dot_general x12, matrix products, dot(): return lax.dot_general(a, b, (dims, ((), ())), preferred_element_type=f32)  88 us
    pallas_call x1, Pallas kernels, spread(): pl.pallas_call(functools.partial(spread_kernel, zs, n), out_shape=[jax.Sh...  86.6 us
    all_gather x2, waiting for transfers between devices, gather_ctx(): return lax.all_gather(v, 'ctx', axis=0, tiled=True)  52 us
    unnamed x1, blocking collectives  38.9 us
    convert_element_type x6, local copies, waits for them, and re-layouts, ff_back(): return jnp.transpose(part.reshape(n, wrows, zs, ff_block), (1, 2, 0, 3))....  22.9 us
  transfers between devices with their start and end apart: 14, of which 10 were waited for; matrix products, arithmetic and copies ran while one was open for 20% of the time, Pallas kernels for 0%

profile of v2, /device:TPU:1, one launch (start us, length us, event | category | flops | bytes accessed | tf_op | source)
XLA Modules:
  0.0 883.4 jit_solution(8736749176064186748)
XLA Ops:
  10.5 3.4 concatenate.71
  18.2 86.6 %spread.1 = (bf16[4,8,64,768]{3,2,1,0:T(8,128)(2,1)S(1)}, bf16[4,64,2048]{2,1,0:T(8,128)(2,1)S(1)}, bf16[8,64,1408]{2,1,0:T(8,128)(2,1)}, bf16[8,128,2048]{2,1,0...) custom-call(bf16[64,6144]{1,0:T(8,128)(2,1)S(1)} %copy-done.1, ...), custom_call_target="tpu_custom_call" | custom-call | tf_op jit(solution)/shard_map/spread/pallas_call | solution.py:549
  110.2 3.7 fusion.6
  113.9 3.4 convolution_add_fusion
  117.7 3.0 fusion.59
  129.5 5.6 fusion.43
  138.5 8.4 fusion.65
  148.1 4.8 divide_convert_fusion
  156.5 2.6 convert_element_type.167
  161.0 3.2 convolution_convert_fusion.3
  165.1 51.5 %reduce-scatter.9.cloned.1.call-done = bf16[128,2048]{1,0:T(8,128)(2,1)} async-done(((bf16[1024,2048]{1,0:T(8,128)(2,1)}), bf16[128,2048]{1,0:T(8,128)(2,1)}) %reduce-scatter.9.cloned.1.call-update) | async-done | bytes 524304 | tf_op jit(solution)/shard_map/reduce_scatter | solution.py:619
  219.2 2.1 add_convert_fusion.1
  222.0 51.9 %all-gather.7.cloned.1.call-done = bf16[2048,1408]{1,0:T(8,128)(2,1)} async-done(((bf16[512,1408]{1,0:T(8,128)(2,1)}), bf16[2048,1408]{1,0:T(8,128)(2,1)}) %all-gather.7.cloned.1.call-update) | async-done | bytes 5767184 | tf_op jit(solution)/shard_map/all_gather | solution.py:622
  274.0 37.6 %all-gather.5.cloned.1.call-done = bf16[1024,2048]{1,0:T(8,128)(2,1)} async-done(((bf16[128,2048]{1,0:T(8,128)(2,1)}), bf16[1024,2048]{1,0:T(8,128)(2,1)}) %all-gather.5.cloned.1.call-update) | async-done | bytes 4194320 | tf_op jit(solution)/shard_map/all_gather | solution.py:616
  311.5 11.7 %fusion.66 = f32[1024,1408]{1,0:T(8,128)} fusion(bf16[1024,2048]{1,0:T(8,128)(2,1)} %all-gather.5.cloned.1.call-done, bf16[2048,1408]{1,0:T(8,128)(2,1)} %all-gather.7.cloned.1.call-done), kind=kOutput, calls=%fused_computation.156 | convolution fusion | flops 5905580032 | bytes 15728640 | tf_op jit(solution)/shard_map/dot_general | solution.py:604
  323.2 48.3 %all-gather.9.cloned.1.call-done = bf16[704,2048]{1,0:T(8,128)(2,1)} async-done(((bf16[176,2048]{1,0:T(8,128)(2,1)}), bf16[704,2048]{1,0:T(8,128)(2,1)}) %all-gather.9.cloned.1.call-update) | async-done | bytes 2883600 | tf_op jit(solution)/shard_map/all_gather | solution.py:622
  371.5 10.3 %multiply_convert_fusion.1 = (bf16[1024,704]{1,0:T(8,128)(2,1)S(1)}, bf16[1024,704]{1,0:T(8,128)(2,1)S(1)}, bf16[1024,704]{1,0:T(8,128)(2,1)}) fusion(f32[1024,1408]{1,0:T(8,128)} %fusion.66, bf16[1024,2048]{1,0:T(8,128)(2,1)} %bitcast.184, bf16[704,2048]{1,0:T(8,128)(2,1)} %all-gather.9.cloned.1.call-done), kind=kOutput, calls=%fused_computation.31 | convolution fusion | flops 2964324352 | bytes 17170432 | tf_op jit(solution)/shard_map/dot_general | solution.py:604
  383.5 8.3 convolution_convert_fusion.1
  392.3 49.9 %reduce-scatter.13.cloned.1.call-done = bf16[128,2048]{1,0:T(8,128)(2,1)} async-done(((bf16[1024,2048]{1,0:T(8,128)(2,1)}), bf16[128,2048]{1,0:T(8,128)(2,1)}) %reduce-scatter.13.cloned.1.call-update) | async-done | bytes 524304 | tf_op jit(solution)/shard_map/reduce_scatter | solution.py:619
  442.2 2.2 fusion.39
  444.4 2.5 fusion.57
  447.0 11.3 %convolution_convert_fusion = bf16[2048,1408]{1,0:T(8,128)(2,1)} fusion(bf16[1024,2048]{1,0:T(8,128)(2,1)} %all-gather.5.cloned.1.call-done, bf16[1024,704]{1,0:T(8,128)(2,1)} %copy-done.41, bf16[1024,704]{1,0:T(8,128)(2,1)} %copy-done.40), kind=kOutput, calls=%fused_computation.16 | convolution fusion | flops 5914230784 | bytes 12845056 | tf_op jit(solution)/shard_map/dot_general | solution.py:604
  458.4 7.7 convolution_convert_fusion.6
  469.8 14.4 %all-gather.11.cloned.1.call-done = bf16[1024,2048]{1,0:T(8,128)(2,1)} async-done(((bf16[128,2048]{1,0:T(8,128)(2,1)}), bf16[1024,2048]{1,0:T(8,128)(2,1)}) %all-gather.11.cloned.1.call-update) | async-done | bytes 4194320 | tf_op jit(solution)/shard_map/all_gather | solution.py:616
  484.2 3.5 convolution_convert_fusion.10
  491.2 3.5 fusion.7
  494.8 4.7 fusion.8
  502.5 2.5 copy.180
  505.0 3.2 copy.164
  508.1 2.5 copy.181
  510.7 3.2 copy.166
  515.8 3.1 convolution_multiply_fusion.1
  520.5 2.5 copy.178
  523.0 3.2 copy.159
  526.2 2.5 copy.179
  528.7 3.2 copy.161
  533.7 4.6 convolution_convert_fusion.7
  538.6 4.5 fusion.26
  543.1 2.6 concatenate.92
  545.6 6.1 fusion.15
  551.7 4.3 convert_reduce_fusion.1
  556.0 4.7 copy.168
  560.8 7.8 convolution_convert_fusion.4
  568.6 8.4 convolution_convert_fusion.5
  577.2 7.7 convolution_convert_fusion.2
  584.9 5.1 all-to-all-start.1
  591.6 27.8 %reduce-scatter.23.cloned.1.call-done = bf16[176,2048]{1,0:T(8,128)(2,1)} async-done(((bf16[704,2048]{1,0:T(8,128)(2,1)}), bf16[176,2048]{1,0:T(8,128)(2,1)}) %reduce-scatter.23.cloned.1.call-update) | async-done | bytes 720912 | tf_op jit(solution)/shard_map/reduce_scatter | solution.py:625
  619.4 2.4 convert_element_type.205
  621.9 3.5 slice_convert_fusion.1
  625.5 4.0 reshape.426
  629.5 4.1 copy.193
  633.6 3.3 reshape.423
  636.9 4.0 reshape.427
  640.9 4.1 copy.192
  645.0 3.4 reshape.424
  650.4 51.8 %reduce-scatter.15.cloned.1.call-done = bf16[128,2048]{1,0:T(8,128)(2,1)} async-done(((bf16[1024,2048]{1,0:T(8,128)(2,1)}), bf16[128,2048]{1,0:T(8,128)(2,1)}) %reduce-scatter.15.cloned.1.call-update) | async-done | bytes 524304 | tf_op jit(solution)/shard_map/reduce_scatter | solution.py:619
  704.0 60.5 %reduce-scatter.17.cloned.1.call-done = bf16[512,768]{1,0:T(8,128)(2,1)} async-done(((bf16[2048,768]{1,0:T(8,128)(2,1)}), bf16[512,768]{1,0:T(8,128)(2,1)}) %reduce-scatter.17.cloned.1.call-update) | async-done | bytes 786448 | tf_op jit(solution)/shard_map/reduce_scatter | solution.py:625
  764.5 4.9 all-to-all-start
  769.4 49.7 %reduce-scatter.11.cloned.1.call-done = bf16[128,2048]{1,0:T(8,128)(2,1)} async-done(((bf16[1024,2048]{1,0:T(8,128)(2,1)}), bf16[128,2048]{1,0:T(8,128)(2,1)}) %reduce-scatter.11.cloned.1.call-update) | async-done | bytes 524304 | tf_op jit(solution)/shard_map/reduce_scatter | solution.py:619
  819.1 2.2 fusion.31
  824.6 38.9 %all-reduce.1 = f32[32,448]{1,0:T(8,128)S(1)} all-reduce(f32[32,448]{1,0:T(8,128)S(1)} %concatenate.94), channel_id=7, replica_groups=mesh['dp'=4,'ctx'=8] {'dp','ctx'}, use_global_device_ids=true, to_apply=%region_23.24.clone | all-reduce | flops 14336 | bytes 114688
  864.6 2.5 reshape.425
  867.2 5.4 copy.191
  872.6 3.3 reshape.422
  (204 shorter events, 63.5 us)
Async XLA Ops:
  8.0 208.6 %reduce-scatter.9.cloned.1.call-start = ((), (), s32[]{:S(2)}) async-start(), calls=%async_computation.10 | async-start | bytes 4718592 | tf_op jit(solution)/shard_map/reduce_scatter | solution.py:619
  13.9 1.1 copy-start.1
  15.0 1.1 copy-start.2
  16.1 1.1 copy-start.3
  17.3 0.9 copy-start.4
  104.8 1.7 copy-start.6
  106.5 2.7 copy-start
  106.5 3.4 copy-start.5
  109.9 4.0 copy-start.23
  110.2 3.7 copy-start.7
  113.9 3.5 copy-start.16
  117.7 4.7 copy-start.9
  129.4 7.9 copy-start.38
  137.3 9.5 %copy-start.20 = (bf16[2,512,256]{1,2,0:T(8,128)(2,1)}, bf16[2,512,256]{1,2,0:T(8,128)(2,1)S(1)}, u32[]{:S(2)}) copy-start(bf16[2,512,256]{1,2,0:T(8,128)(2,1)S(1)} %copy.147) | copy-start | bytes 1572868
  148.1 4.8 copy-start.14
  152.9 2.0 copy-start.8
  161.0 3.2 copy-start.19
  164.2 0.7 copy-start.26
  164.2 0.8 copy-start.25
  164.2 109.7 %all-gather.7.cloned.1.call-start = ((), (), s32[]{:S(2)}) async-start(), calls=%async_computation.12 | async-start | bytes 7208960 | tf_op jit(solution)/shard_map/all_gather | solution.py:622
  164.8 146.7 %all-gather.5.cloned.1.call-start = ((), (), s32[]{:S(2)}) async-start(), calls=%async_computation.11 | async-start | bytes 4718592 | tf_op jit(solution)/shard_map/all_gather | solution.py:616
  217.9 226.5 %copy-start.28 = (f32[128]{0:T(128)}, f32[128]{0:T(128)S(1)}, u32[]{:S(2)}) copy-start(f32[128]{0:T(128)S(1)} %broadcast_multiply_fusion.8) | copy-start | bytes 1540
  219.2 225.2 %copy-start.30 = (f32[128]{0:T(128)}, f32[128]{0:T(128)S(1)}, u32[]{:S(2)}) copy-start(f32[128]{0:T(128)S(1)} %add_rsqrt_fusion.2) | copy-start | bytes 1540
  221.4 150.1 %all-gather.9.cloned.1.call-start = ((), (), s32[]{:S(2)}) async-start(), calls=%async_computation.13 | async-start | bytes 3604480 | tf_op jit(solution)/shard_map/all_gather | solution.py:622
  222.0 220.2 %reduce-scatter.13.cloned.1.call-start = ((), (), s32[]{:S(2)}) async-start(), calls=%async_computation.15 | async-start | bytes 4718592 | tf_op jit(solution)/shard_map/reduce_scatter | solution.py:619
  371.5 12.0 %copy-start.39 = (bf16[2048,1408]{1,0:T(8,128)(2,1)S(1)}, bf16[2048,1408]{1,0:T(8,128)(2,1)}, u32[]{:S(2)}) copy-start(bf16[2048,1408]{1,0:T(8,128)(2,1)} %all-gather.7.cloned.1.call-done) | copy-start | bytes 17301508
  381.9 1.2 copy-start.40
  381.9 1.7 copy-start.41
  391.9 50.3 %copy-start.11 = (bf16[128,2048]{1,0:T(8,128)(2,1)S(1)}, bf16[128,2048]{1,0:T(8,128)(2,1)}, u32[]{:S(2)}) copy-start(bf16[128,2048]{1,0:T(8,128)(2,1)} %reduce-scatter.9.cloned.1.call-done) | copy-start | bytes 1572868
  391.9 92.3 %all-gather.11.cloned.1.call-start = ((), (), s32[]{:S(2)}) async-start(), calls=%async_computation.16 | async-start | bytes 4718592 | tf_op jit(solution)/shard_map/all_gather | solution.py:616
  444.4 13.9 %copy-start.32 = (f32[128]{0:T(128)}, f32[128]{0:T(128)S(1)}, u32[]{:S(2)}) copy-start(f32[128]{0:T(128)S(1)} %broadcast_multiply_fusion.6) | copy-start | bytes 1540
  444.4 13.9 %copy-start.34 = (f32[128]{0:T(128)}, f32[128]{0:T(128)S(1)}, u32[]{:S(2)}) copy-start(f32[128]{0:T(128)S(1)} %broadcast_multiply_fusion.7) | copy-start | bytes 1540
  446.9 137.9 %reduce-scatter.21.cloned.1.call-start = ((), (), s32[]{:S(2)}) async-start(), calls=%async_computation.20 | async-start | bytes 7208960 | tf_op jit(solution)/shard_map/reduce_scatter | solution.py:625
  458.4 161.1 %reduce-scatter.23.cloned.1.call-start = ((), (), s32[]{:S(2)}) async-start(), calls=%async_computation.21 | async-start | bytes 3604480 | tf_op jit(solution)/shard_map/reduce_scatter | solution.py:625
  466.1 1.3 copy-start.22
  466.1 182.6 %reduce-scatter.19.cloned.1.call-start = ((), (), s32[]{:S(2)}) async-start(), calls=%async_computation.19 | async-start | bytes 1310720 | tf_op jit(solution)/shard_map/reduce_scatter | solution.py:625
  487.7 3.5 copy-start.15
  494.8 4.7 copy-start.21
  499.5 3.0 copy-start.10
  538.4 163.9 %reduce-scatter.15.cloned.1.call-start = ((), (), s32[]{:S(2)}) async-start(), calls=%async_computation.17 | async-start | bytes 4718592 | tf_op jit(solution)/shard_map/reduce_scatter | solution.py:619
  538.6 7.0 copy-start.17
  545.6 6.1 copy-start.18
  568.6 195.9 %reduce-scatter.17.cloned.1.call-start = ((), (), s32[]{:S(2)}) async-start(), calls=%async_computation.18 | async-start | bytes 3932160 | tf_op jit(solution)/shard_map/reduce_scatter | solution.py:625
  577.1 242.0 %reduce-scatter.11.cloned.1.call-start = ((), (), s32[]{:S(2)}) async-start(), calls=%async_computation.14 | async-start | bytes 4718592 | tf_op jit(solution)/shard_map/reduce_scatter | solution.py:619
  584.8 5.1 copy-start.12
  584.9 36.9 %copy-start.27 = (f32[2048]{0:T(1024)S(1)}, f32[2048]{0:T(1024)}, u32[]{:S(2)}) copy-start(f32[2048]{0:T(1024)} %get-tuple-element.24) | copy-start | bytes 24580
  584.9 37.1 %all-to-all-start.1 = ((bf16[8,64,1408]{2,1,0:T(8,128)(2,1)}), bf16[8,64,1408]{2,1,0:T(8,128)(2,1)}, u32[]{:S(2)}, u32[]{:S(2)}) async-start(bf16[8,64,1408]{2,1,0:T(8,128)(2,1)} %bitcast.226), calls=%async_computation.8 | async-start | bytes 2883584 | tf_op jit(solution)/shard_map/all_to_all | solution.py:613
  591.5 110.7 %copy-start.36 = (f32[128]{0:T(128)}, f32[128]{0:T(128)S(1)}, u32[]{:S(2)}) copy-start(f32[128]{0:T(128)S(1)} %rsqrt.30) | copy-start | bytes 1540
  591.6 110.6 %copy-start.37 = (f32[128]{0:T(128)}, f32[128]{0:T(128)S(1)}, u32[]{:S(2)}) copy-start(f32[128]{0:T(128)S(1)} %div.68) | copy-start | bytes 1540
  645.0 57.3 %copy-start.24 = (f32[2048]{0:T(1024)S(1)}, f32[2048]{0:T(1024)}, u32[]{:S(2)}) copy-start(f32[2048]{0:T(1024)} %copy-done.23) | copy-start | bytes 24580
  645.0 174.1 %copy-start.13 = (bf16[128,2048]{1,0:T(8,128)(2,1)S(1)}, bf16[128,2048]{1,0:T(8,128)(2,1)}, u32[]{:S(2)}) copy-start(bf16[128,2048]{1,0:T(8,128)(2,1)} %reduce-scatter.13.cloned.1.call-done) | copy-start | bytes 1572868
  645.0 174.1 %copy-start.29 = (f32[128]{0:T(128)S(1)}, f32[128]{0:T(128)}, u32[]{:S(2)}) copy-start(f32[128]{0:T(128)} %copy-done.28) | copy-start | bytes 1540
  645.0 174.1 %copy-start.31 = (f32[128]{0:T(128)S(1)}, f32[128]{0:T(128)}, u32[]{:S(2)}) copy-start(f32[128]{0:T(128)} %copy-done.30) | copy-start | bytes 1540
  645.0 174.1 %copy-start.33 = (f32[128]{0:T(128)S(1)}, f32[128]{0:T(128)}, u32[]{:S(2)}) copy-start(f32[128]{0:T(128)} %copy-done.32) | copy-start | bytes 1540
  645.0 174.1 %copy-start.35 = (f32[128]{0:T(128)S(1)}, f32[128]{0:T(128)}, u32[]{:S(2)}) copy-start(f32[128]{0:T(128)} %copy-done.34) | copy-start | bytes 1540
  764.5 100.2 %all-to-all-start = ((bf16[8,64,768]{2,1,0:T(8,128)(2,1)}), bf16[8,64,768]{2,1,0:T(8,128)(2,1)S(1)}, u32[]{:S(2)}, u32[]{:S(2)}) async-start(bf16[8,64,768]{2,1,0:T(8,128)(2,1)} %bitcast.228), calls=%async_computation.5 | async-start | bytes 1572864 | tf_op jit(solution)/shard_map/all_to_all | solution.py:613
Sparse Core Ops, SparseCore 0:
  164.4 52.2 reduce-scatter.8
  392.0 50.1 reduce-scatter.12
  447.0 37.1 all-gather.10
Sparse Core Ops, SparseCore 1:
  166.3 107.6 all-gather.6
  276.5 35.0 all-gather.4
  313.1 58.4 all-gather.8
  458.4 102.1 reduce-scatter.20
  563.0 56.4 reduce-scatter.22
  621.7 26.9 reduce-scatter.18
  652.3 49.9 reduce-scatter.14
  704.4 60.0 reduce-scatter.16
  767.7 51.3 reduce-scatter.10

commit v3 on v2

--- a/solution.py
+++ b/solution.py
@@ -572,6 +572,741 @@
     )(w_qkv, w_gate, w_up, w_out, xs, dy, small)
 
 
+class LayerScatter:
+    def __init__(self, wires, part, near, far):
+        c = wires.c
+        self.c, self.part, self.near, self.far = c, part, near, far
+        self.pair = {
+            m: wires.put(part.at[flip(c, m + 1)], near.at[m // 2], 0, 1) for m in (6, 4, 2, 0)
+        }
+        self.chips = {
+            m: wires.put(part.at[flip(c, m)], far.at[m // 2 - 1], 0, m) for m in (6, 4, 2)
+        }
+
+    def start(self):
+        for copy in self.pair.values():
+            copy.start()
+
+    def step(self, m):
+        self.pair[m].wait_recv()
+        to = flip(self.c, m)
+        self.part[to] = (
+            self.part[to].astype(jnp.float32) + self.near[m // 2].astype(jnp.float32)
+        ).astype(self.part.dtype)
+        self.chips[m].start()
+
+    def total(self):
+        self.pair[0].wait_recv()
+        result = self.part[self.c].astype(jnp.float32) + self.near[0].astype(jnp.float32)
+        for m in (2, 4, 6):
+            self.chips[m].wait_recv()
+            result = result + self.far[m // 2 - 1].astype(jnp.float32)
+        return result
+
+    def sent(self):
+        for copy in (*self.pair.values(), *self.chips.values()):
+            copy.wait_send()
+
+
+def dot(a, b, dims=((1,), (0,))):
+    return lax.dot_general(a, b, (dims, ((), ())), preferred_element_type=jnp.float32)
+
+
+def turn_pair(values, table, sign):
+    half = ROTARY // 2
+    columns = values.shape[-1]
+    return (
+        values * table[0]
+        + sign * (pltpu.roll(values, columns - half, 1) * table[1])
+        + sign * (pltpu.roll(values, half, 1) * table[2])
+    )
+
+
+def head_mask(rows, columns, head):
+    return lax.broadcasted_iota(jnp.int32, (rows, columns), 1) // HEAD_DIM == head
+
+
+def forward_kernel(
+    zs,
+    n,
+    lengths,
+    norms,
+    bias,
+    tables,
+    xs_all,
+    w_qkv,
+    w_out,
+    gu_own,
+    a1_out,
+    qkv_out,
+    probs_out,
+    ob_out,
+    hidden_out,
+    a2_out,
+    w_gu_out,
+    gu_out,
+    zz_out,
+    xs_v,
+    a1_v,
+    w_qkv_v,
+    w_out_v,
+    qkv_v,
+    probs_v,
+    ob_v,
+    part,
+    near,
+    far,
+    hidden_v,
+    a2_v,
+    w_gu_v,
+    gu_v,
+    zz_v,
+    send,
+    recv,
+    local,
+    drain,
+):
+    f32, b16 = jnp.float32, jnp.bfloat16
+    wires = Wires(send, recv)
+    z, c = wires.z, wires.c
+    _, slots, rows, hc = ob_v.shape
+    tokens, width = n * slots * rows, a1_v.shape[-1]
+    seq = n * rows
+    heads = hc // HEAD_DIM
+    ffc = zz_v.shape[-1]
+    chunks = 4
+    chunk = w_gu_v.shape[1] // chunks
+
+    loads = [
+        pltpu.make_async_copy(gu_own, w_gu_v.at[z], local.at[0]),
+        pltpu.make_async_copy(xs_all, xs_v, local.at[1]),
+        pltpu.make_async_copy(w_qkv, w_qkv_v, local.at[2]),
+        pltpu.make_async_copy(w_out, w_out_v, local.at[3]),
+    ]
+    for copy in loads:
+        copy.start()
+    wires.greet(zs, n)
+    loads[0].wait()
+    gu_z = [
+        DepthGather(wires, lambda i, p=p: w_gu_v.at[i, p * chunk : (p + 1) * chunk])
+        for p in range(chunks)
+    ]
+    for part_z in gu_z:
+        part_z.start()
+    stores = []
+
+    def store(src, dst):
+        copy = pltpu.make_async_copy(src, dst, drain.at[len(stores)])
+        copy.start()
+        stores.append(copy)
+
+    for copy in loads[1:]:
+        copy.wait()
+
+    def project(i, carry):
+        x = xs_v[pl.ds(2 * i, 2)].reshape(2 * slots * rows, width).astype(f32)
+        a1 = (layer_stats(x)[0] * norms[0:1] + norms[1:2]).astype(b16)
+        a1_v[pl.ds(2 * i, 2)] = a1.reshape(2, slots * rows, width)
+        joined = dot(a1, w_qkv_v[...].reshape(width, 3 * hc)) + bias[...]
+        for j in range(2):
+            table = tables[:, 2 * i + j]
+            for s in range(slots):
+                at = (j * slots + s) * rows
+                piece = joined[at : at + rows]
+                qkv_v[0, s, 2 * i + j] = turn_pair(piece[:, :hc], table, 1.0).astype(b16)
+                qkv_v[1, s, 2 * i + j] = turn_pair(piece[:, hc : 2 * hc], table, 1.0).astype(b16)
+                qkv_v[2, s, 2 * i + j] = piece[:, 2 * hc :].astype(b16)
+        return carry
+
+    lax.fori_loop(0, n // 2, project, 0)
+    store(a1_v, a1_out)
+    store(qkv_v, qkv_out)
+
+    half = seq // 2
+
+    def attend(s, carry):
+        q, k, v = [qkv_v[i, s].reshape(seq, hc) for i in range(3)]
+        length = lengths[0, s]
+        for part_q in range(2):
+            keys = (part_q + 1) * half
+            at = part_q * half
+            query = q[at : at + half]
+            row = lax.broadcasted_iota(jnp.int32, (half, keys), 0) + at
+            key = lax.broadcasted_iota(jnp.int32, (half, keys), 1)
+            allowed = (key <= row) & (row < length)
+            out = jnp.zeros((half, hc), f32)
+            for h in range(heads):
+                mask = head_mask(half, hc, h)
+                scores = dot(jnp.where(mask, query, 0).astype(b16), k[:keys], ((1,), (1,)))
+                scores = jnp.where(allowed, scores * 0.125, masked_value)
+                peak = jnp.max(scores, -1, keepdims=True)
+                weights = jnp.where(allowed, jnp.exp(scores - peak), 0.0)
+                total = jnp.maximum(jnp.sum(weights, -1, keepdims=True), 1.0)
+                probs = (weights * (1.0 / total)).astype(b16)
+                probs_v[s, h, at : at + half, 0:keys] = probs
+                out = jnp.where(mask, dot(probs, v[:keys]), out)
+            ob_v[part_q * n // 2 : (part_q + 1) * n // 2, s] = out.astype(b16).reshape(
+                n // 2, rows, hc
+            )
+        return carry
+
+    lax.fori_loop(0, slots, attend, 0)
+    store(probs_v, probs_out)
+    store(ob_v, ob_out)
+
+    def to_hidden(i, carry):
+        part[i] = dot(
+            ob_v[i].reshape(slots * rows, hc), w_out_v[...].reshape(hc, width)
+        ).astype(b16)
+        return carry
+
+    lax.fori_loop(0, n, to_hidden, 0)
+    sums = LayerScatter(wires, part, near, far)
+    sums.start()
+    for m in (6, 4, 2):
+        sums.step(m)
+    gu_z[0].forward()
+    hidden = xs_v[c].astype(f32) + sums.total()
+    hidden_v[...] = hidden
+    store(hidden_v, hidden_out)
+    a2_v[c] = (layer_stats(hidden)[0] * norms[2:3] + norms[3:4]).astype(b16)
+    a2_g = LayerGather(wires, a2_v)
+    a2_g.start()
+    gu_z[1].forward()
+    for m in (2, 4, 6):
+        a2_g.forward(m)
+    gu_z[2].forward()
+    for m in (1, 3, 5, 7):
+        a2_g.arrived(m)
+    gu_z[3].forward()
+    store(a2_v, a2_out)
+    for part_z in gu_z:
+        part_z.finish()
+    store(w_gu_v, w_gu_out)
+
+    def feed(i, carry):
+        a2 = a2_v[pl.ds(2 * i, 2)].reshape(2 * slots * rows, width)
+        gu = dot(a2, w_gu_v[...].reshape(width, 2 * ffc))
+        gu_v[i] = gu
+        gate = gu[:, :ffc]
+        zz_v[i] = (gate * jax.nn.sigmoid(gate) * gu[:, ffc:]).astype(b16)
+        return carry
+
+    lax.fori_loop(0, n // 2, feed, 0)
+    store(gu_v, gu_out)
+    store(zz_v, zz_out)
+    sums.sent()
+    a2_g.sent()
+    for copy in stores:
+        copy.wait()
+
+
+def forward(zs, n, slots, lengths, norms, bias, tables, xs_all, w_qkv, w_out, gu_own):
+    _, local, width = xs_all.shape
+    rows = local // slots
+    seq = rows * n
+    heads = HEADS // n
+    hc = heads * HEAD_DIM
+    gc = gu_own.shape[-1]
+    f32, b16 = jnp.float32, jnp.bfloat16
+    kept = [
+        ((n, local, width), b16),
+        ((3, slots, n, rows, hc), b16),
+        ((slots, heads, seq, seq), b16),
+        ((n, slots, rows, hc), b16),
+        ((local, width), f32),
+        ((n, local, width), b16),
+        ((zs, *gu_own.shape), b16),
+        ((n // 2, 2 * local, gc), f32),
+        ((n // 2, 2 * local, gc // 2), b16),
+    ]
+    a1, qkv, probs, ob, hidden, a2, w_gu, gu, zz = [pltpu.VMEM(*k) for k in kept]
+    return pl.pallas_call(
+        functools.partial(forward_kernel, zs, n),
+        out_shape=[jax.ShapeDtypeStruct(*k) for k in kept],
+        in_specs=[pl.BlockSpec(memory_space=pltpu.SMEM)] + [VMEM] * 3 + [HBM] * 4,
+        out_specs=[HBM] * len(kept),
+        scratch_shapes=[
+            pltpu.VMEM(xs_all.shape, b16),
+            a1,
+            pltpu.VMEM(w_qkv.shape, b16),
+            pltpu.VMEM(w_out.shape, b16),
+            qkv,
+            probs,
+            ob,
+            pltpu.VMEM((n, local, width), b16),
+            pltpu.VMEM((n // 2, local, width), b16),
+            pltpu.VMEM((n // 2 - 1, local, width), b16),
+            hidden,
+            a2,
+            w_gu,
+            gu,
+            zz,
+            pltpu.SemaphoreType.DMA((40,)),
+            pltpu.SemaphoreType.DMA((40,)),
+            pltpu.SemaphoreType.DMA((4,)),
+            pltpu.SemaphoreType.DMA((len(kept),)),
+        ],
+        compiler_params=pltpu.CompilerParams(
+            collective_id=2, has_side_effects=True, vmem_limit_bytes=60 << 20
+        ),
+        name="forward",
+    )(lengths, norms, bias, tables, xs_all, w_qkv, w_out, gu_own)
+
+
+class DepthScatter:
+    def __init__(self, wires, part, relay, boxes):
+        z = wires.z
+        self.wires, self.part, self.relay_box, self.boxes = wires, part, relay, boxes
+        self.far = wires.put(part(flip(z, 3)), relay, 1, 0)
+        self.skip = wires.put(part(flip(z, 2)), boxes[1], 2, 0)
+        self.near = wires.put(part(flip(z, 1)), boxes[0], 1, 0)
+        self.mid = wires.put(part(flip(z, 3)), boxes[2], 3, 0)
+
+    def start(self):
+        @pl.when(self.wires.outer)
+        def _():
+            self.far.start()
+            self.skip.start()
+            self.boxes[2][...] = jnp.zeros_like(self.boxes[2])
+
+        pl.when(self.wires.inner)(self.mid.start)
+        self.near.start()
+
+    def relay(self):
+        @pl.when(self.wires.inner)
+        def _():
+            self.far.wait_recv()
+            to = self.part(flip(self.wires.z, 2))
+            to[...] = (
+                to[...].astype(jnp.float32) + self.relay_box[...].astype(jnp.float32)
+            ).astype(to.dtype)
+            self.skip.start()
+
+    def total(self):
+        self.near.wait_recv()
+        self.skip.wait_recv()
+        pl.when(self.wires.inner)(self.mid.wait_recv)
+        result = self.part(self.wires.z)[...].astype(jnp.float32)
+        for box in self.boxes:
+            result = result + box[...].astype(jnp.float32)
+        return result
+
+    def sent(self):
+        self.near.wait_send()
+        self.skip.wait_send()
+        pl.when(self.wires.outer)(self.far.wait_send)
+        pl.when(self.wires.inner)(self.mid.wait_send)
+
+
+class Moves:
+    def __init__(self, sems):
+        self.sems, self.number, self.stores = sems, itertools.count(), []
+
+    def load(self, src, dst):
+        copy = pltpu.make_async_copy(src, dst, self.sems.at[next(self.number)])
+        copy.start()
+        return copy
+
+    def store(self, src, dst):
+        self.stores.append(self.load(src, dst))
+
+    def finish(self):
+        for copy in self.stores:
+            copy.wait()
+
+
+def pieces_of(total, number, unit):
+    units = total // unit
+    cuts = [units * i // number * unit for i in range(number + 1)]
+    return [(a, b - a) for a, b in zip(cuts[:-1], cuts[1:])]
+
+
+def middle_kernel(
+    zs,
+    n,
+    zz,
+    gu,
+    dy_all,
+    w_down,
+    dgu_out,
+    w_down_out,
+    grad_down_out,
+    zz_v,
+    gu_v,
+    dy_v,
+    w_down_v,
+    dgu_v,
+    gd_v,
+    relay_v,
+    box_v,
+    total_v,
+    send,
+    recv,
+    local,
+):
+    f32, b16 = jnp.float32, jnp.bfloat16
+    wires = Wires(send, recv)
+    moves = Moves(local)
+    z = wires.z
+    _, block, width = w_down_v.shape
+    ffc = zs * block
+    tokens = n * dy_v.shape[1]
+    wait_down = moves.load(w_down, w_down_v.at[z])
+    wait_zz = moves.load(zz, zz_v)
+    wait_dy = moves.load(dy_all, dy_v)
+    wait_gu = moves.load(gu, gu_v)
+    wires.greet(zs, n)
+    wait_down.wait()
+    down_z = [
+        DepthGather(wires, lambda i, a=a, s=s: w_down_v.at[i, a : a + s])
+        for a, s in pieces_of(block, 4, 16)
+    ]
+    for part in down_z:
+        part.start()
+    wait_zz.wait()
+    wait_dy.wait()
+    number = 4
+    tile = width // number
+    sums = [
+        DepthScatter(
+            wires,
+            lambda i, a=p * tile: gd_v.at[i, :, a : a + tile],
+            relay_v.at[:, p * tile : (p + 1) * tile],
+            [box_v.at[j, :, p * tile : (p + 1) * tile] for j in range(3)],
+        )
+        for p in range(number)
+    ]
+    for p in range(number):
+        gd = dot(
+            zz_v[...].reshape(tokens, ffc),
+            dy_v[:, :, p * tile : (p + 1) * tile].reshape(tokens, tile),
+            ((0,), (0,)),
+        )
+        gd_v[:, :, p * tile : (p + 1) * tile] = gd.astype(b16).reshape(zs, block, tile)
+        sums[p].start()
+    for p in range(number):
+        down_z[p].forward()
+        sums[p].relay()
+    for part in down_z:
+        part.finish()
+    moves.store(w_down_v, w_down_out)
+    wait_gu.wait()
+
+    def back(i, carry):
+        dz = dot(
+            dy_v[pl.ds(2 * i, 2)].reshape(tokens // (n // 2), width),
+            w_down_v[...].reshape(ffc, width),
+            ((1,), (1,)),
+        )
+        gu_block = gu_v[i]
+        gate, up = gu_block[:, :ffc], gu_block[:, ffc:]
+        sig = jax.nn.sigmoid(gate)
+        dg = dz * up * sig * (1.0 + gate * (1.0 - sig))
+        du = dz * gate * sig
+        dgu_v[i] = jnp.concatenate([dg, du], -1).astype(b16)
+        return carry
+
+    lax.fori_loop(0, n // 2, back, 0)
+    moves.store(dgu_v, dgu_out)
+    for p in range(number):
+        total_v[:, p * tile : (p + 1) * tile] = sums[p].total()
+    moves.store(total_v, grad_down_out)
+    for part in sums:
+        part.sent()
+    moves.finish()
+
+
+def middle(zs, n, zz, gu, dy_all, w_down):
+    f32, b16 = jnp.float32, jnp.bfloat16
+    block, width = w_down.shape
+    return pl.pallas_call(
+        functools.partial(middle_kernel, zs, n),
+        out_shape=[
+            jax.ShapeDtypeStruct(gu.shape, b16),
+            jax.ShapeDtypeStruct((zs, block, width), b16),
+            jax.ShapeDtypeStruct((block, width), f32),
+        ],
+        in_specs=[HBM] * 4,
+        out_specs=[HBM] * 3,
+        scratch_shapes=[
+            pltpu.VMEM(zz.shape, b16),
+            pltpu.VMEM(gu.shape, f32),
+            pltpu.VMEM(dy_all.shape, b16),
+            pltpu.VMEM((zs, block, width), b16),
+            pltpu.VMEM(gu.shape, b16),
+            pltpu.VMEM((zs, block, width), b16),
+            pltpu.VMEM((block, width), b16),
+            pltpu.VMEM((3, block, width), b16),
+            pltpu.VMEM((block, width), f32),
+            pltpu.SemaphoreType.DMA((40,)),
+            pltpu.SemaphoreType.DMA((40,)),
+            pltpu.SemaphoreType.DMA((8,)),
+        ],
+        compiler_params=pltpu.CompilerParams(
+            collective_id=3, has_side_effects=True, vmem_limit_bytes=60 << 20
+        ),
+        name="middle",
+    )(zz, gu, dy_all, w_down)
+
+
+def backward_kernel(
+    zs,
+    n,
+    norms,
+    tables,
+    a2_all,
+    dgu,
+    w_gu,
+    w_out,
+    qkv,
+    probs,
+    ob,
+    hidden,
+    dy_all,
+    ggu_out,
+    grad_out_out,
+    dh_out,
+    dj_out,
+    gains_out,
+    bias_out,
+    a2_v,
+    dgu_v,
+    w_gu_v,
+    w_out_v,
+    qkv_v,
+    probs_v,
+    ob_v,
+    hidden_v,
+    dy_v,
+    ggu_v,
+    relay_v,
+    box_v,
+    part,
+    near,
+    far,
+    dh_v,
+    dh_all,
+    go_v,
+    go_relay,
+    go_box,
+    go_total,
+    do_v,
+    dqkv_v,
+    dj_v,
+    send,
+    recv,
+    local,
+):
+    f32, b16 = jnp.float32, jnp.bfloat16
+    wires = Wires(send, recv)
+    moves = Moves(local)
+    z, c = wires.z, wires.c
+    _, slots, rows, hc = ob_v.shape
+    width = dh_v.shape[-1]
+    tokens, seq, local_rows = n * slots * rows, n * rows, slots * rows
+    heads = hc // HEAD_DIM
+    depth, gc = ggu_v.shape[1:]
+
+    wait_a2 = moves.load(a2_all, a2_v)
+    wait_dgu = moves.load(dgu, dgu_v)
+    wait_w = moves.load(w_gu, w_gu_v)
+    waits = [
+        moves.load(hidden, hidden_v),
+        moves.load(dy_all.at[c], dy_v),
+        moves.load(w_out, w_out_v),
+        moves.load(qkv, qkv_v),
+        moves.load(probs, probs_v),
+        moves.load(ob, ob_v),
+    ]
+    wires.greet(zs, n)
+    wait_a2.wait()
+    wait_dgu.wait()
+
+    number = 4
+    size = depth // number
+    sums = [
+        DepthScatter(
+            wires,
+            lambda i, a=p * size: ggu_v.at[i, a : a + size],
+            relay_v.at[p * size : (p + 1) * size],
+            [box_v.at[j, p * size : (p + 1) * size] for j in range(3)],
+        )
+        for p in range(number)
+    ]
+    step = 2 * size
+    for p in range(number // 2):
+
+        def weigh(i, carry, p=p):
+            at = pl.multiple_of(i * depth + p * step, step)
+            left = a2_v[:, :, pl.ds(at, step)].reshape(tokens, step)
+            ggu_v[i, p * step : (p + 1) * step] = dot(
+                left, dgu_v[...].reshape(tokens, gc), ((0,), (0,))
+            ).astype(b16)
+            return carry
+
+        lax.fori_loop(0, zs, weigh, 0)
+        sums[2 * p].start()
+        sums[2 * p + 1].start()
+
+    wait_w.wait()
+
+    def normed(i, carry):
+        part[pl.ds(2 * i, 2)] = (
+            dot(dgu_v[i], w_gu_v[...].reshape(width, gc), ((1,), (1,)))
+            .astype(b16)
+            .reshape(2, local_rows, width)
+        )
+        return carry
+
+    lax.fori_loop(0, n // 2, normed, 0)
+    sums[0].relay()
+    da2_sums = LayerScatter(wires, part, near, far)
+    da2_sums.start()
+    for m in (6, 4, 2):
+        da2_sums.step(m)
+    for copy in waits:
+        copy.wait()
+    n2, r2 = layer_stats(hidden_v[...])
+    sums[1].relay()
+    da2 = da2_sums.total()
+    gains_out[0:1] = jnp.sum(da2 * n2, 0, keepdims=True)
+    gains_out[1:2] = jnp.sum(da2, 0, keepdims=True)
+    dh = dy_v[...].astype(f32) + norm_back(da2, n2, r2, norms[2:3])
+    dh_v[...] = dh
+    moves.store(dh_v, dh_out)
+    dh_all[c] = dh.astype(b16)
+    dh_g = LayerGather(wires, dh_all)
+    dh_g.start()
+    for m in (2, 4, 6):
+        dh_g.forward(m)
+    sums[2].relay()
+    for m in (1, 3, 5, 7):
+        dh_g.arrived(m)
+
+    def heads_back(i, carry):
+        do_v[i] = (
+            dot(dh_all[i], w_out_v[...].reshape(hc, width), ((1,), (1,)))
+            .astype(b16)
+            .reshape(slots, rows, hc)
+        )
+        return carry
+
+    lax.fori_loop(0, n, heads_back, 0)
+
+    half = seq // 2
+
+    def attend(s, carry):
+        q, k, v = [qkv_v[i, s].reshape(seq, hc) for i in range(3)]
+        do_s = do_v[:, s].reshape(seq, hc)
+        dqkv_v[...] = jnp.zeros_like(dqkv_v)
+        for part_q in range(2):
+            keys = (part_q + 1) * half
+            at = part_q * half
+            query, do_q = q[at : at + half], do_s[at : at + half]
+            dq = jnp.zeros((half, hc), f32)
+            for h in range(heads):
+                mask, mask_k = head_mask(half, hc, h), head_mask(keys, hc, h)
+                do_h = jnp.where(mask, do_q, 0).astype(b16)
+                low = probs_v[s, h, at : at + half, 0:keys]
+                p32 = low.astype(f32)
+                t = p32 * dot(do_h, v[:keys], ((1,), (1,)))
+                ds = (t - p32 * jnp.sum(t, -1, keepdims=True)).astype(b16)
+                dq = jnp.where(mask, dot(ds, k[:keys]), dq)
+                dk = dot(ds, query, ((0,), (0,)))
+                dv = dot(low, do_h, ((0,), (0,)))
+                dqkv_v[1, 0:keys] += jnp.where(mask_k, dk, 0.0)
+                dqkv_v[2, 0:keys] += dv
+            dqkv_v[0, at : at + half] = dq
+        dq, dk = dqkv_v[0] * 0.125, dqkv_v[1] * 0.125
+        table = [tables[i].reshape(seq, hc) for i in range(3)]
+        dj = [turn_pair(dq, table, -1.0), turn_pair(dk, table, -1.0), dqkv_v[2]]
+        for i in range(3):
+            dj_v[:, s, :, i * hc : (i + 1) * hc] = dj[i].astype(b16).reshape(n, rows, hc)
+        return carry
+
+    lax.fori_loop(0, slots, attend, 0)
+    moves.store(dj_v, dj_out)
+    sums[3].relay()
+    dj_all = dj_v[...].reshape(tokens, 3 * hc).astype(f32)
+    bias_out[...] = jnp.sum(dj_all, 0, keepdims=True)
+
+    go_sums = DepthScatter(
+        wires, lambda i: go_v.at[i], go_relay, [go_box.at[j] for j in range(3)]
+    )
+    tile = width // 4
+    for p in range(4):
+        go = dot(
+            ob_v[...].reshape(tokens, hc),
+            dh_all[:, :, p * tile : (p + 1) * tile].reshape(tokens, tile),
+            ((0,), (0,)),
+        )
+        go_v[:, :, p * tile : (p + 1) * tile] = go.astype(b16).reshape(zs, hc // zs, tile)
+    go_sums.start()
+    for p in range(number):
+        a = p * size
+        ggu_v[z, a : a + size] = sums[p].total().astype(b16)
+        moves.store(ggu_v.at[z, a : a + size], ggu_out.at[a : a + size])
+    go_sums.relay()
+    go_total[...] = go_sums.total()
+    moves.store(go_total, grad_out_out)
+    for group in (*sums, go_sums, da2_sums, dh_g):
+        group.sent()
+    moves.finish()
+
+
+def backward(zs, n, norms, tables, a2_all, dgu, w_gu, w_out, qkv, probs, ob, hidden, dy_all):
+    f32, b16 = jnp.float32, jnp.bfloat16
+    _, slots, rows, hc = ob.shape
+    local, width = hidden.shape
+    _, depth, gc = w_gu.shape
+    seq = n * rows
+    wide = (n, local, width)
+
+    def buf(like):
+        return pltpu.VMEM(like.shape, like.dtype)
+
+    return pl.pallas_call(
+        functools.partial(backward_kernel, zs, n),
+        out_shape=[
+            jax.ShapeDtypeStruct((depth, gc), b16),
+            jax.ShapeDtypeStruct((hc // zs, width), f32),
+            jax.ShapeDtypeStruct((local, width), f32),
+            jax.ShapeDtypeStruct((n, slots, rows, 3 * hc), b16),
+            jax.ShapeDtypeStruct((2, width), f32),
+            jax.ShapeDtypeStruct((1, 3 * hc), f32),
+        ],
+        in_specs=[VMEM] * 2 + [HBM] * 9,
+        out_specs=[HBM] * 4 + [VMEM] * 2,
+        scratch_shapes=[
+            *[buf(v) for v in (a2_all, dgu, w_gu, w_out, qkv, probs, ob, hidden)],
+            pltpu.VMEM((local, width), b16),
+            pltpu.VMEM((zs, depth, gc), b16),
+            pltpu.VMEM((depth, gc), b16),
+            pltpu.VMEM((3, depth, gc), b16),
+            pltpu.VMEM(wide, b16),
+            pltpu.VMEM((n // 2, local, width), b16),
+            pltpu.VMEM((n // 2 - 1, local, width), b16),
+            pltpu.VMEM((local, width), f32),
+            pltpu.VMEM(wide, b16),
+            pltpu.VMEM((zs, hc // zs, width), b16),
+            pltpu.VMEM((hc // zs, width), b16),
+            pltpu.VMEM((3, hc // zs, width), b16),
+            pltpu.VMEM((hc // zs, width), f32),
+            pltpu.VMEM(ob.shape, b16),
+            pltpu.VMEM((3, seq, hc), f32),
+            pltpu.VMEM((n, slots, rows, 3 * hc), b16),
+            pltpu.SemaphoreType.DMA((48,)),
+            pltpu.SemaphoreType.DMA((48,)),
+            pltpu.SemaphoreType.DMA((24,)),
+        ],
+        compiler_params=pltpu.CompilerParams(
+            collective_id=4, has_side_effects=True, vmem_limit_bytes=62 << 20
+        ),
+        name="backward",
+    )(norms, tables, a2_all, dgu, w_gu, w_out, qkv, probs, ob, hidden, dy_all)
+
+
 def tensor_shards(
     inputs,
     lengths,
@@ -633,8 +1368,6 @@
     )
     small = small.reshape(zs * n, 1024)
     dy_all = dy_all.reshape(tokens, width)
-    w_qkv_c = w_qkv_c.reshape(width, 3 * hc)
-    w_out_c = w_out_c.reshape(hc, width)
     nb = b_qkv.shape[0]
     bias_full = small[:, :nb].reshape(3, zs, n, HEAD_DIM)
     bias_own = lax.dynamic_index_in_dim(bias_full, me, 2, keepdims=False).reshape(1, 3 * hc)
@@ -642,8 +1375,6 @@
         small[:, nb + i * wrows : nb + (i + 1) * wrows].reshape(1, width) for i in range(4)
     ]
 
-    w_gu_c = gather_dp(gu_own.reshape(n * wrows, 2 * ffc))
-    w_down_c = gather_dp(w_down)
 
     counter = jnp.arange(ROTARY // 2, dtype=f32)
     angles = jnp.arange(seq, dtype=f32)[:, None] * (10000.0 ** (-2.0 * counter / ROTARY))[None, :]
@@ -672,67 +1403,28 @@
             + sign * jnp.roll(v, half, -1) * table_r
         )
 
-    x32 = xs.astype(f32)
-    n1, r1 = layer_stats(x32)
-    a1_all = (layer_stats(a_all.reshape(tokens, width).astype(f32))[0] * g1 + s1).astype(b16)
-    joined = by_slot(dot(a1_all, w_qkv_c, ((1,), (0,))) + bias_own)
-    q = turn(joined[..., :hc], 1.0).astype(b16)
-    k = turn(joined[..., hc : 2 * hc], 1.0).astype(b16)
-    v = joined[..., 2 * hc :].astype(b16)
-
-    def heads_of(t):
-        return t.reshape(slots, seq, heads, HEAD_DIM)
-
-    at = jnp.arange(seq, dtype=jnp.int32)
-    allowed = (at[None, :] <= at[:, None])[None] & (at[None, :, None] < lengths[0][:, None, None])
-    scores = jnp.einsum("sqhd,skhd->shqk", heads_of(q), heads_of(k), preferred_element_type=f32)
-    scores = jnp.where(allowed[:, None], scores * 0.125, masked_value)
-    peak = jnp.max(scores, -1, keepdims=True)
-    weights = jnp.where(allowed[:, None], jnp.exp(scores - peak), 0.0)
-    probs = (weights / jnp.maximum(jnp.sum(weights, -1, keepdims=True), 1.0)).astype(b16)
-    attended = jnp.einsum("shqk,skhd->sqhd", probs, heads_of(v), preferred_element_type=f32)
-    ob = by_device(attended.reshape(slots, seq, hc).astype(b16))
-    hidden = x32 + scatter_ctx(dot(ob, w_out_c, ((1,), (0,))))
-    n2, r2 = layer_stats(hidden)
-    a2_all = gather_ctx((n2 * g2 + s2).astype(b16))
-
-    gu = dot(a2_all, w_gu_c, ((1,), (0,)))
-    gate, up = gu[:, :ffc], gu[:, ffc:]
-    sig = jax.nn.sigmoid(gate)
-    z = (gate * sig * up).astype(b16)
+    tables = jnp.stack([table_c, table_l, table_r]).reshape(3, n, rows, hc)
+    norms = jnp.concatenate([g1, s1, g2, s2])
+    a1_all, qkv, probs, ob, hidden, a2_all, w_gu_c, gu, z = forward(
+        zs, n, slots, lengths, norms, bias_own, tables, a_all, w_qkv_c, w_out_c,
+        gu_own.reshape(n * wrows, 2 * ffc),
+    )
+    dgu, w_down_c, grad_down = middle(zs, n, z, gu, dy_all.reshape(n, local, width), w_down)
+    ggu, grad_out, dh, dj, gains_two, bias_part = backward(
+        zs, n, norms, tables, a2_all, dgu, w_gu_c, w_out_c, qkv, probs, ob, hidden,
+        dy_all.reshape(n, local, width),
+    )
+    grad_gu = exchange(ggu.reshape(n, wrows, 2 * ffc))
+    gain_two_part, shift_two_part = gains_two[0], gains_two[1]
+    bias_part = bias_part.reshape(3, zs, 1, HEAD_DIM)
+    w_qkv_c = w_qkv_c.reshape(width, 3 * hc)
+    a1_all = a1_all.reshape(tokens, width)
+    dj = dj.reshape(tokens, 3 * hc)
+    n1, r1 = layer_stats(xs.astype(f32))
+    z = z.reshape(tokens, ffc)
+    w_down_c = w_down_c.reshape(ffc, width)
     result = hidden + scatter_ctx(dot(z, w_down_c, ((1,), (0,))))
-    grad_down = scatter_dp(dot(z, dy_all, ((0,), (0,)))).astype(f32)
-    dz = dot(dy_all, w_down_c, ((1,), (1,)))
-    dg = (dz * up * sig * (1.0 + gate * (1.0 - sig))).astype(b16)
-    du = (dz * gate * sig).astype(b16)
-    dgu = jnp.concatenate([dg, du], -1)
-    grad_gu = exchange(scatter_dp(dot(a2_all, dgu, ((0,), (0,)))).reshape(n, wrows, 2 * ffc))
-    da2 = scatter_ctx(dot(dgu, w_gu_c, ((1,), (1,))))
-    gain_two_part = jnp.sum(da2 * n2, 0)
-    shift_two_part = jnp.sum(da2, 0)
-    dh = dy.astype(f32) + norm_back(da2, n2, r2, g2)
-    dh_all = gather_ctx(dh.astype(b16))
-
-    grad_out = scatter_dp(dot(ob, dh_all, ((0,), (0,)))).astype(f32)
-    do = heads_of(by_slot(dot(dh_all, w_out_c, ((1,), (1,))).astype(b16)))
-    dp = jnp.einsum("sqhd,skhd->shqk", do, heads_of(v), preferred_element_type=f32)
-    p32 = probs.astype(f32)
-    ds = (p32 * (dp - jnp.sum(p32 * dp, -1, keepdims=True))).astype(b16)
-    dq = jnp.einsum("shqk,skhd->sqhd", ds, heads_of(k), preferred_element_type=f32) * 0.125
-    dk = jnp.einsum("shqk,sqhd->skhd", ds, heads_of(q), preferred_element_type=f32) * 0.125
-    dv = jnp.einsum("shqk,sqhd->skhd", probs, do, preferred_element_type=f32)
-    dj = by_device(
-        jnp.concatenate(
-            [
-                turn(dq.reshape(slots, seq, hc), -1.0),
-                turn(dk.reshape(slots, seq, hc), -1.0),
-                dv.reshape(slots, seq, hc),
-            ],
-            -1,
-        ).astype(b16)
-    )
     grad_qkv = exchange(scatter_dp(dot(a1_all, dj, ((0,), (0,)))).reshape(n, wrows, 3 * hc))
-    bias_part = jnp.sum(dj.astype(f32), 0).reshape(3, zs, 1, HEAD_DIM)
     da1 = scatter_ctx(dot(dj, w_qkv_c, ((1,), (1,))))
     gain_one_part = jnp.sum(da1 * n1, 0)
     shift_one_part = jnp.sum(da1, 0)

time: 891 us -> 659 us (0.74)
  waiting for transfers between devices: 445 us -> 71.9 us
  Pallas kernels: 86.6 us -> 426 us
  matrix products: 110 us -> 21.6 us
  local copies, waits for them, and re-layouts: 120 us -> 55.7 us
  other arithmetic: 55.5 us -> 10 us
    pallas_call x0 -> x3, Pallas kernels: none -> 339 us  [the longest x1 131 us: backward(): pl.pallas_call(functools.partial(backward_kernel, zs, n), out_shape=[jax....]
    reduce_scatter x4 -> x2, waiting for transfers between devices: 203 us -> 50.5 us  [scatter_ctx(): lax.psum_scatter(v.astype(b16), 'ctx', scatter_dimension=0, tiled=True)]
    all_gather x4 -> x0, waiting for transfers between devices: 152 us -> none  [the longest x2 100 us: gather_dp(): return lax.all_gather(v, 'dp', axis=0, tiled=True)]
    reduce_scatter x4 -> x1, waiting for transfers between devices: 88.4 us -> 7.47 us  [scatter_dp(): lax.psum_scatter(v.astype(b16), 'dp', scatter_dimension=0, tiled=True)]
    dot_general x12 -> x3, matrix products: 88 us -> 21.6 us  [dot(): return lax.dot_general(a, b, (dims, ((), ())), preferred_element_type=f32)]
    convert_element_type x8 -> x1, other arithmetic: 27.5 us -> 1.14 us  [tensor_shards(): result.astype(b16)]
    concatenate x9 -> x0, local copies, waits for them, and re-layouts: 15.6 us -> none  [the longest x4 6.56 us: turn(): jnp.roll(v, half, -1)]
    dot_general x5 -> x0, matrix products: 14 us -> none  [the longest x1 4.45 us: tensor_shards(): dv = jnp.einsum('shqk,sqhd->skhd', probs, do, preferred_element_type=f32)]
  transfers between devices with their start and end apart: 14 -> 5, of which waited for: 10 -> 3; matrix products, arithmetic and copies ran while one was open for 20% -> 7% of each run, Pallas kernels for 0% -> 20%
where the time goes in v3:
time: 659 us; the launch traced here: 648 us
  Pallas kernels  426 us (65%)
  waiting for transfers between devices  71.9 us (11%)
  local copies, waits for them, and re-layouts  55.7 us (8%)
  blocking collectives  38.8 us (6%)
  matrix products  21.6 us (3%)
  between operations  14.6 us (2%)
  other arithmetic  10 us (2%)
  starting transfers between devices  9.42 us (1%)
    pallas_call x1, Pallas kernels, backward(): pl.pallas_call(functools.partial(backward_kernel, zs, n), out_shape=[jax....  131 us
    pallas_call x1, Pallas kernels, forward(): pl.pallas_call(functools.partial(forward_kernel, zs, n), out_shape=[jax.S...  111 us
    pallas_call x1, Pallas kernels, middle(): pl.pallas_call(functools.partial(middle_kernel, zs, n), out_shape=[jax.Sh...  97.8 us
    pallas_call x1, Pallas kernels, spread(): pl.pallas_call(functools.partial(spread_kernel, zs, n), out_shape=[jax.Sh...  86.6 us
    reduce_scatter x2, waiting for transfers between devices, scatter_ctx(): lax.psum_scatter(v.astype(b16), 'ctx', scatter_dimension=0, tiled=True)  50.5 us
    unnamed x1, blocking collectives  38.8 us
    dot_general x3, matrix products, dot(): return lax.dot_general(a, b, (dims, ((), ())), preferred_element_type=f32)  21.6 us
    convert_element_type x6, local copies, waits for them, and re-layouts, ff_back(): return jnp.transpose(part.reshape(n, wrows, zs, ff_block), (1, 2, 0, 3))....  17.8 us
  transfers between devices with their start and end apart: 5, of which 3 were waited for; matrix products, arithmetic and copies ran while one was open for 7% of the time, Pallas kernels for 20%

profile of v3, /device:TPU:1, one launch (start us, length us, event | category | flops | bytes accessed | tf_op | source)
XLA Modules:
  0.0 647.9 jit_solution(3219136518657353531)
XLA Ops:
  7.3 3.5 concatenate.19
  10.8 1.2 copy.59
  12.0 1.2 copy.60
  13.3 1.1 copy-done.7
  14.4 86.6 %spread.1 = (bf16[4,8,64,768]{3,2,1,0:T(8,128)(2,1)S(1)}, bf16[4,64,2048]{2,1,0:T(8,128)(2,1)S(1)}, bf16[8,64,1408]{2,1,0:T(8,128)(2,1)S(1)}, bf16[8,128,2048]{2...) custom-call(bf16[64,6144]{1,0:T(8,128)(2,1)S(1)} %copy-done.5, ...), custom_call_target="tpu_custom_call" | custom-call | tf_op jit(solution)/shard_map/spread/pallas_call | solution.py:549
  101.0 2.0 copy-done
  103.1 1.0 copy-done.1
  104.0 2.0 copy-done.2
  106.1 1.7 copy-done.3
  107.7 1.1 copy-done.4
  108.9 0.1 pad.17.clone
  109.1 0.1 fusion.11
  109.2 0.1 maximum_maximum_fusion.1
  109.4 0.2 tile.27
  109.6 0.4 copy.63
  110.1 0.2 tile.29
  110.3 0.4 copy.64
  110.7 0.2 tile.25
  110.9 0.4 copy.62
  111.3 0.1 reshape.203
  111.4 0.1 reshape.200
  111.5 0.1 reshape.202
  111.5 0.1 reshape.201
  111.7 0.7 reshape.205.bias
  112.4 1.3 pad_maximum_fusion.tables
  113.7 0.6 pad_maximum_fusion.1.norms
  114.3 110.8 %forward.1 = (bf16[8,128,2048]{2,1,0:T(8,128)(2,1)}, bf16[3,2,8,64,256]{4,3,2,1,0:T(8,128)(2,1)}, bf16[2,4,512,512]{3,2,1,0:T(8,128)(2,1)}, bf16[8,2,64,256]{3,2...) custom-call(s32[1,2]{1,0:T(1,128)} %lengths.1, ...), custom_call_target="tpu_custom_call" | custom-call | tf_op jit(solution)/shard_map/forward/pallas_call | solution.py:824
  225.1 97.8 %middle.1 = (bf16[4,256,1408]{2,1,0:T(8,128)(2,1)}, bf16[4,176,2048]{2,1,0:T(8,128)(2,1)}, f32[176,2048]{1,0:T(8,128)}) custom-call(bf16[4,256,704]{2,1,0:T(8,128)(2,1)} %get-tuple-element.42.zz, f32[4,256,1408]{2,1,0:T(8,128)} %get-tuple-element.43.gu, bf16[8,128,2048]{2,1,0:T(8,128)(2,1)} %copy-done, bf16[176,2048]{1,0:T(8,128)(2,1)} %w_down.1), custom_call_target="tpu_custom_call" | custom-call | tf_op jit(solution)/shard_map/middle/pallas_call | solution.py:1023
  322.9 6.9 %convolution_convert_fusion = bf16[1024,2048]{1,0:T(8,128)(2,1)} fusion(bf16[1024,704]{1,0:T(8,128)(2,1)S(1)} %bitcast.84, bf16[704,2048]{1,0:T(8,128)(2,1)} %bitcast.95), kind=kOutput, calls=%fused_computation | convolution fusion | flops 2954887168 | bytes 8519680 | tf_op jit(solution)/shard_map/dot_general | solution.py:1339
  329.8 130.7 %backward.1 = (bf16[512,1408]{1,0:T(8,128)(2,1)}, f32[64,2048]{1,0:T(8,128)}, f32[128,2048]{1,0:T(8,128)}, bf16[8,2,64,768]{3,2,1,0:T(8,128)(2,1)}, f32[2,2048]{1,0:T(2,128)}, /*index=5*/f32[1,768]{1,0:T(1,128)}) custom-call(f32[4,2048]{1,0:T(4,128)} %pad_maximum_fusion.1.norms, f32[3,8,64,256]{3,2,1,0:T(8,128)} %pad_maximum_fusion.tables, ...), custom_call_target="tpu_custom_call" | custom-call | tf_op jit(solution)/shard_map/backward/pallas_call | solution.py:1269
  460.5 7.9 %convolution_convert_fusion.2 = bf16[2048,768]{1,0:T(8,128)(2,1)} fusion(bf16[1024,2048]{1,0:T(8,128)(2,1)} %bitcast.94, bf16[1024,768]{1,0:T(8,128)(2,1)} %bitcast.96), kind=kOutput, calls=%fused_computation.2 | convolution fusion | flops 3222798336 | bytes 8912896 | tf_op jit(solution)/shard_map/dot_general | solution.py:1339
  468.5 1.3 copy-done.17
  469.8 6.9 %convolution_convert_fusion.1 = bf16[1024,2048]{1,0:T(8,128)(2,1)} fusion(bf16[1024,768]{1,0:T(8,128)(2,1)S(1)} %bitcast.97, bf16[2048,768]{1,0:T(8,128)(2,1)} %bitcast.75), kind=kOutput, calls=%fused_computation.1 | convolution fusion | flops 3223322624 | bytes 8912896 | tf_op jit(solution)/shard_map/dot_general | solution.py:1339
  476.7 4.5 all-to-all-start.1
  481.3 0.5 convert_reduce_fusion.1
  481.9 0.1 div.30
  482.0 0.8 fusion.4
  482.9 0.1 rsqrt.12
  483.3 0.1 broadcast_select_fusion
  483.4 13.9 %all-to-all-done.1 = bf16[8,64,1408]{2,1,0:T(8,128)(2,1)S(1)} async-done(((bf16[8,64,1408]{2,1,0:T(8,128)(2,1)}), bf16[8,64,1408]{2,1,0:T(8,128)(2,1)S(1)}, u32[]{:S(2)}, u32[]{:S(2)}) %all-to-all-start.1) | async-done | bytes 1441824 | tf_op jit(solution)/shard_map/all_to_all | solution.py:1348
  497.3 2.2 slice_convert_fusion
  499.5 3.0 reshape.225
  502.5 2.5 copy.84
  505.1 3.3 reshape.222
  508.3 3.0 reshape.224
  511.4 2.5 copy.85
  513.9 3.4 reshape.221
  517.3 1.1 add_convert_fusion
  518.5 1.3 copy.87
  519.8 7.5 %reduce-scatter.8.cloned.1.call-done = bf16[512,768]{1,0:T(8,128)(2,1)} async-done(((bf16[2048,768]{1,0:T(8,128)(2,1)}), bf16[512,768]{1,0:T(8,128)(2,1)}) %reduce-scatter.8.cloned.1.call-update) | async-done | bytes 786448 | tf_op jit(solution)/shard_map/reduce_scatter | solution.py:1360
  527.3 4.8 all-to-all-start
  532.1 50.5 %reduce-scatter.6.cloned.1.call-done = bf16[128,2048]{1,0:T(8,128)(2,1)} async-done(((bf16[1024,2048]{1,0:T(8,128)(2,1)}), bf16[128,2048]{1,0:T(8,128)(2,1)}) %reduce-scatter.6.cloned.1.call-update) | async-done | bytes 524304 | tf_op jit(solution)/shard_map/reduce_scatter | solution.py:1354
  582.6 1.5 fusion.9
  584.1 1.5 fusion.7
  585.7 1.8 copy.86
  587.6 0.1 concatenate.24
  587.7 38.8 %all-reduce.1 = f32[32,448]{1,0:T(8,128)S(1)} all-reduce(f32[32,448]{1,0:T(8,128)S(1)} %concatenate.24), channel_id=5, replica_groups=mesh['dp'=4,'ctx'=8] {'dp','ctx'}, use_global_device_ids=true, to_apply=%region_9.10.clone | all-reduce | flops 14336 | bytes 114688
  626.5 0.6 constant_dynamic-slice_fusion
  627.0 0.6 dynamic-slice_bitcast_fusion
  627.7 2.5 reshape.223
  630.2 5.4 copy.83
  635.6 3.5 reshape.220
  639.0 0.8 copy.91
  639.8 1.1 copy.92
  (67 shorter events, 1.4 us)
Async XLA Ops:
  7.2 6.1 copy-start.6
  7.2 6.1 copy-start.8
  7.2 6.1 copy-start.5
  7.2 510.1 %reduce-scatter.4.cloned.1.call-start = ((), (), s32[]{:S(2)}) async-start(), calls=%async_computation.5 | async-start | bytes 4718592 | tf_op jit(solution)/shard_map/reduce_scatter | solution.py:1354
  13.3 1.1 copy-start.7
  101.0 2.0 copy-start
  103.0 1.0 copy-start.1
  104.0 2.0 copy-start.2
  106.1 1.7 copy-start.3
  107.7 1.1 copy-start.4
  225.1 97.8 %copy-start.11 = (bf16[4,256,704]{2,1,0:T(8,128)(2,1)S(1)}, bf16[4,256,704]{2,1,0:T(8,128)(2,1)}, u32[]{:S(2)}) copy-start(bf16[4,256,704]{2,1,0:T(8,128)(2,1)} %get-tuple-element.42.zz) | copy-start | bytes 4325380
  329.8 197.5 %reduce-scatter.8.cloned.1.call-start = ((), (), s32[]{:S(2)}) async-start(), calls=%async_computation.7 | async-start | bytes 3932160 | tf_op jit(solution)/shard_map/reduce_scatter | solution.py:1360
  468.4 1.4 copy-start.17
  468.4 114.1 %reduce-scatter.6.cloned.1.call-start = ((), (), s32[]{:S(2)}) async-start(), calls=%async_computation.6 | async-start | bytes 4718592 | tf_op jit(solution)/shard_map/reduce_scatter | solution.py:1354
  476.7 4.6 copy-start.9
  476.7 6.3 copy-start.16
  476.7 6.4 copy-start.15
  476.7 20.6 %all-to-all-start.1 = ((bf16[8,64,1408]{2,1,0:T(8,128)(2,1)}), bf16[8,64,1408]{2,1,0:T(8,128)(2,1)S(1)}, u32[]{:S(2)}, u32[]{:S(2)}) async-start(bf16[8,64,1408]{2,1,0:T(8,128)(2,1)} %bitcast.85), calls=%async_computation.4 | async-start | bytes 2883584 | tf_op jit(solution)/shard_map/all_to_all | solution.py:1348
  513.9 3.4 copy-start.10
  518.5 65.7 %copy-start.13 = (f32[128,2048]{1,0:T(8,128)S(1)}, f32[128,2048]{1,0:T(8,128)}, u32[]{:S(2)}) copy-start(f32[128,2048]{1,0:T(8,128)} %get-tuple-element.52) | copy-start | bytes 3145732
  527.3 100.4 %all-to-all-start = ((bf16[8,64,768]{2,1,0:T(8,128)(2,1)}), bf16[8,64,768]{2,1,0:T(8,128)(2,1)S(1)}, u32[]{:S(2)}, u32[]{:S(2)}) async-start(bf16[8,64,768]{2,1,0:T(8,128)(2,1)} %bitcast.87), calls=%async_computation.3 | async-start | bytes 1572864 | tf_op jit(solution)/shard_map/all_to_all | solution.py:1348
  635.6 3.5 copy-start.14
  635.6 4.3 copy-start.12
Sparse Core Ops, SparseCore 0:
  329.9 77.7 reduce-scatter.3
  468.6 58.6 reduce-scatter.7
  531.0 51.5 reduce-scatter.5

commit v4 on v3

--- a/solution.py
+++ b/solution.py
@@ -1306,6 +1306,291 @@
         name="backward",
     )(norms, tables, a2_all, dgu, w_gu, w_out, qkv, probs, ob, hidden, dy_all)
 
+def unpack_columns(dst, src, at, block, n, zs):
+    dst[...] = jnp.concatenate(
+        [
+            src[i, :, at + block * j : at + block * (j + 1)]
+            for j in range(zs)
+            for i in range(n)
+        ],
+        -1,
+    )
+
+
+def last_kernel(
+    zs,
+    n,
+    norms,
+    gains_two,
+    bias_part,
+    a1_all,
+    dj,
+    w_qkv,
+    ggu,
+    zz,
+    w_down,
+    hidden,
+    xs,
+    dh,
+    result_out,
+    input_grad_out,
+    qkv_out,
+    gate_out,
+    up_out,
+    small_out,
+    a1_v,
+    dj_v,
+    w_qkv_v,
+    zz_v,
+    w_down_v,
+    hidden_v,
+    xs_v,
+    dh_v,
+    gq_v,
+    relay_v,
+    box_v,
+    part,
+    near,
+    far,
+    part_y,
+    near_y,
+    far_y,
+    gu_box,
+    gq_box,
+    small_v,
+    small_x,
+    small_r,
+    small_z,
+    send,
+    recv,
+    local,
+):
+    f32, b16 = jnp.float32, jnp.bfloat16
+    wires = Wires(send, recv)
+    moves = Moves(local)
+    z, c = wires.z, wires.c
+    _, local_rows, width = a1_v.shape
+    tokens = n * local_rows
+    _, depth, qc = gq_v.shape
+    hc = qc // 3
+    wrows = depth // n
+    ffc = zz_v.shape[-1]
+    ff_block = ffc // zs
+
+    wait_a1 = moves.load(a1_all, a1_v)
+    wait_dj = moves.load(dj, dj_v)
+    wait_gu = moves.load(ggu.at[c], gu_box.at[c])
+    wait_w = moves.load(w_qkv, w_qkv_v)
+    wait_y = [moves.load(zz, zz_v), moves.load(w_down, w_down_v)]
+    waits = [moves.load(hidden, hidden_v), moves.load(xs, xs_v), moves.load(dh, dh_v)]
+    wires.greet(zs, n)
+    wait_a1.wait()
+    wait_dj.wait()
+
+    number = 4
+    size = depth // number
+    sums = [
+        DepthScatter(
+            wires,
+            lambda i, a=p * size: gq_v.at[i, a : a + size],
+            relay_v.at[p * size : (p + 1) * size],
+            [box_v.at[j, p * size : (p + 1) * size] for j in range(3)],
+        )
+        for p in range(number)
+    ]
+    step = 2 * size
+    for p in range(number // 2):
+
+        def weigh(i, carry, p=p):
+            at = pl.multiple_of(i * depth + p * step, step)
+            left = a1_v[:, :, pl.ds(at, step)].reshape(tokens, step)
+            gq_v[i, p * step : (p + 1) * step] = dot(
+                left, dj_v[...].reshape(tokens, qc), ((0,), (0,))
+            ).astype(b16)
+            return carry
+
+        lax.fori_loop(0, zs, weigh, 0)
+        sums[2 * p].start()
+        sums[2 * p + 1].start()
+
+    wait_w.wait()
+
+    def normed(i, carry):
+        part[pl.ds(2 * i, 2)] = (
+            dot(
+                dj_v[pl.ds(2 * i, 2)].reshape(2 * local_rows, qc),
+                w_qkv_v[...].reshape(width, qc),
+                ((1,), (1,)),
+            )
+            .astype(b16)
+            .reshape(2, local_rows, width)
+        )
+        return carry
+
+    lax.fori_loop(0, n // 2, normed, 0)
+    da1_sums = LayerScatter(wires, part, near, far)
+    da1_sums.start()
+    for m in (6, 4, 2):
+        da1_sums.step(m)
+    gu_x = [wires.put(ggu.at[flip(c, m)], gu_box.at[c], 0, m) for m in range(1, n)]
+    for copy in gu_x:
+        copy.start()
+
+    for copy in wait_y:
+        copy.wait()
+
+    def down(i, carry):
+        part_y[pl.ds(2 * i, 2)] = (
+            dot(zz_v[i], w_down_v[...].reshape(ffc, width))
+            .astype(b16)
+            .reshape(2, local_rows, width)
+        )
+        return carry
+
+    lax.fori_loop(0, n // 2, down, 0)
+    sums[0].relay()
+    y_sums = LayerScatter(wires, part_y, near_y, far_y)
+    y_sums.start()
+    for m in (6, 4, 2):
+        y_sums.step(m)
+
+    for copy in waits:
+        copy.wait()
+    n1, r1 = layer_stats(xs_v[...].astype(f32))
+    da1 = da1_sums.total()
+    input_grad_out[...] = dh_v[...] + norm_back(da1, n1, r1, norms[0:1])
+    gains = [
+        jnp.sum(da1 * n1, 0, keepdims=True),
+        jnp.sum(da1, 0, keepdims=True),
+        gains_two[0:1],
+        gains_two[1:2],
+    ]
+    sums[1].relay()
+    chips = n // 2
+    lane_half = lax.broadcasted_iota(jnp.int32, (1, 2 * HEAD_DIM), 1) // HEAD_DIM
+    lanes = 2 * HEAD_DIM
+    for j in range(zs):
+        for chip in range(chips):
+            k = j * chips + chip
+            for r in range(4):
+                small_v[j, chip, r : r + 1] = gains[r][:, k * lanes : (k + 1) * lanes]
+            small_v[j, chip, 7:8] = jnp.zeros((1, lanes), f32)
+    for i in range(3):
+        for j in range(zs):
+            at = i * hc + j * HEAD_DIM
+            piece = bias_part[:, at : at + HEAD_DIM]
+            both = jnp.concatenate([piece, piece], -1)
+            for chip in range(chips):
+                tile = (i * zs + j) * chips + chip
+                pair, row = tile // 3, tile % 3
+                small_v[pair // chips, pair % chips, 4 + row : 5 + row] = jnp.where(
+                    (lane_half == c % 2) & (c // 2 == chip), both, 0.0
+                )
+    small_v_x = [
+        wires.put(small_v.at[:, flip(c, m) // 2], small_x.at[m], 0, m) for m in range(1, n)
+    ]
+    for copy in small_v_x:
+        copy.start()
+    for copy in gu_x:
+        copy.wait_recv()
+    wait_gu.wait()
+    unpack_columns(gate_out, gu_box, 0, ff_block, n, zs)
+    unpack_columns(up_out, gu_box, ffc, ff_block, n, zs)
+    small_sum = small_v[:, c // 2]
+    for m in range(1, n):
+        small_v_x[m - 1].wait_recv()
+        small_sum = small_sum + small_x[m]
+    small_r[...] = small_sum
+    small_z_x = [wires.put(small_r.at[flip(z, m)], small_z.at[m], m, 0) for m in range(1, zs)]
+    for copy in small_z_x:
+        copy.start()
+    sums[2].relay()
+    result_out[...] = (hidden_v[...] + y_sums.total()).astype(b16)
+    small_sum = small_r[z]
+    for m in range(1, zs):
+        small_z_x[m - 1].wait_recv()
+        small_sum = small_sum + small_z[m]
+    small_out[...] = small_sum
+    sums[3].relay()
+    for p in range(number):
+        a = p * size
+        gq_v[z, a : a + size] = sums[p].total().astype(b16)
+    gq_x = [
+        wires.put(
+            gq_v.at[z, pl.ds(pl.multiple_of(flip(c, m) * wrows, wrows), wrows)],
+            gq_box.at[c],
+            0,
+            m,
+        )
+        for m in range(1, n)
+    ]
+    for copy in gq_x:
+        copy.start()
+    gq_box[c] = gq_v[z, pl.ds(pl.multiple_of(c * wrows, wrows), wrows)]
+    for group in (*sums, da1_sums, y_sums):
+        group.sent()
+    for copy in (*gu_x, *small_v_x, *small_z_x):
+        copy.wait_send()
+    for copy in gq_x:
+        copy.wait()
+    for i in range(3):
+        unpack_columns(
+            qkv_out.at[:, i * width : (i + 1) * width], gq_box, i * hc, HEAD_DIM, n, zs
+        )
+
+
+def last(
+    zs, n, norms, gains_two, bias_part, a1_all, dj, w_qkv, ggu, zz, w_down, hidden, xs, dh
+):
+    f32, b16 = jnp.float32, jnp.bfloat16
+    local, width = hidden.shape
+    _, wrows, gc = ggu.shape
+    qc = dj.shape[-1]
+    depth = n * wrows
+    wide = (n, local, width)
+
+    def buf(like):
+        return pltpu.VMEM(like.shape, like.dtype)
+
+    return pl.pallas_call(
+        functools.partial(last_kernel, zs, n),
+        out_shape=[
+            jax.ShapeDtypeStruct((local, width), b16),
+            jax.ShapeDtypeStruct((local, width), f32),
+            jax.ShapeDtypeStruct((wrows, n * qc), b16),
+            jax.ShapeDtypeStruct((wrows, n * gc // 2), b16),
+            jax.ShapeDtypeStruct((wrows, n * gc // 2), b16),
+            jax.ShapeDtypeStruct((8, 2 * HEAD_DIM), f32),
+        ],
+        in_specs=[VMEM] * 3 + [HBM] * 9,
+        out_specs=[VMEM] * 6,
+        scratch_shapes=[
+            *[buf(v) for v in (a1_all, dj, w_qkv, zz, w_down, hidden, xs, dh)],
+            pltpu.VMEM((zs, depth, qc), b16),
+            pltpu.VMEM((depth, qc), b16),
+            pltpu.VMEM((3, depth, qc), b16),
+            pltpu.VMEM(wide, b16),
+            pltpu.VMEM((n // 2, local, width), b16),
+            pltpu.VMEM((n // 2 - 1, local, width), b16),
+            pltpu.VMEM(wide, b16),
+            pltpu.VMEM((n // 2, local, width), b16),
+            pltpu.VMEM((n // 2 - 1, local, width), b16),
+            pltpu.VMEM(ggu.shape, b16),
+            pltpu.VMEM((n, wrows, qc), b16),
+            pltpu.VMEM((zs, n // 2, 8, 2 * HEAD_DIM), f32),
+            pltpu.VMEM((n, zs, 8, 2 * HEAD_DIM), f32),
+            pltpu.VMEM((zs, 8, 2 * HEAD_DIM), f32),
+            pltpu.VMEM((zs, 8, 2 * HEAD_DIM), f32),
+            pltpu.SemaphoreType.DMA((64,)),
+            pltpu.SemaphoreType.DMA((64,)),
+            pltpu.SemaphoreType.DMA((16,)),
+        ],
+        compiler_params=pltpu.CompilerParams(
+            collective_id=5, has_side_effects=True, vmem_limit_bytes=60 << 20
+        ),
+        name="last",
+    )(norms, gains_two, bias_part, a1_all, dj, w_qkv, ggu, zz, w_down, hidden, xs, dh)
+
 
 def tensor_shards(
     inputs,
@@ -1414,57 +1699,25 @@
         zs, n, norms, tables, a2_all, dgu, w_gu_c, w_out_c, qkv, probs, ob, hidden,
         dy_all.reshape(n, local, width),
     )
-    grad_gu = exchange(ggu.reshape(n, wrows, 2 * ffc))
-    gain_two_part, shift_two_part = gains_two[0], gains_two[1]
-    bias_part = bias_part.reshape(3, zs, 1, HEAD_DIM)
-    w_qkv_c = w_qkv_c.reshape(width, 3 * hc)
-    a1_all = a1_all.reshape(tokens, width)
-    dj = dj.reshape(tokens, 3 * hc)
-    n1, r1 = layer_stats(xs.astype(f32))
-    z = z.reshape(tokens, ffc)
-    w_down_c = w_down_c.reshape(ffc, width)
-    result = hidden + scatter_ctx(dot(z, w_down_c, ((1,), (0,))))
-    grad_qkv = exchange(scatter_dp(dot(a1_all, dj, ((0,), (0,)))).reshape(n, wrows, 3 * hc))
-    da1 = scatter_ctx(dot(dj, w_qkv_c, ((1,), (1,))))
-    gain_one_part = jnp.sum(da1 * n1, 0)
-    shift_one_part = jnp.sum(da1, 0)
-    input_grad = dh + norm_back(da1, n1, r1, g1)
-
-    own = (jnp.arange(n) == me)[None, None, :, None]
-    devices = zs * n
-    pieces = jnp.concatenate(
-        [
-            jnp.where(own, bias_part, 0.0).reshape(devices, nb),
-            gain_one_part.reshape(devices, wrows),
-            shift_one_part.reshape(devices, wrows),
-            gain_two_part.reshape(devices, wrows),
-            shift_two_part.reshape(devices, wrows),
-        ],
-        -1,
-    )
-    summed = lax.psum_scatter(pieces, ("dp", "ctx"), scatter_dimension=0, tiled=True)[0]
-
-    def ff_back(part):
-        return jnp.transpose(part.reshape(n, wrows, zs, ff_block), (1, 2, 0, 3)).reshape(
-            wrows, zs * n * ff_block
-        ).astype(f32)
-
-    grad_qkv = jnp.transpose(grad_qkv.reshape(n, wrows, 3, zs, HEAD_DIM), (1, 2, 3, 0, 4)).reshape(
-        wrows, 3 * width
-    ).astype(f32)
+    result, input_grad, grad_qkv, grad_gate, grad_up, sums = last(
+        zs, n, norms, gains_two, bias_part, a1_all, dj.reshape(n, local, 3 * hc), w_qkv_c,
+        ggu.reshape(n, wrows, 2 * ffc), z, w_down_c, hidden, xs, dh,
+    )
+    mine = lax.dynamic_slice_in_dim(sums[:4], me % 2 * wrows, wrows, 1)
+    grad_bias = lax.dynamic_slice_in_dim(sums[4:7].reshape(2 * nb), me % 2 * nb, nb)
     return (
-        back_tokens(result.astype(b16)),
+        back_tokens(result),
         back_tokens(input_grad),
-        grad_qkv,
-        summed[:nb],
+        grad_qkv.astype(f32),
+        grad_bias,
         grad_out,
-        ff_back(grad_gu[..., :ffc]),
-        ff_back(grad_gu[..., ffc:]),
+        grad_gate.astype(f32),
+        grad_up.astype(f32),
         grad_down,
-        summed[nb : nb + wrows],
-        summed[nb + wrows : nb + 2 * wrows],
-        summed[nb + 2 * wrows : nb + 3 * wrows],
-        summed[nb + 3 * wrows :],
+        mine[0],
+        mine[1],
+        mine[2],
+        mine[3],
     )
 
 

time: 659 us -> 554 us (0.84); the launches traced: 648 us -> 551 us
  Pallas kernels: 426 us -> 520 us
  waiting for transfers between devices: 71.9 us -> 0 us
  blocking collectives: 38.8 us -> 0 us
  local copies, waits for them, and re-layouts: 55.7 us -> 23.7 us
  matrix products: 21.6 us -> 0 us
  between operations: 14.6 us -> 1.19 us
  starting transfers between devices: 9.42 us -> 0 us
    pallas_call x0 -> x1, Pallas kernels: none -> 103 us  [last(): pl.pallas_call(functools.partial(last_kernel, zs, n), out_shape=[jax.Shap...]
    reduce_scatter x3 -> x0, waiting for transfers between devices: 58 us -> none  [the longest x2 50.5 us: scatter_ctx(): lax.psum_scatter(v.astype(b16), 'ctx', scatter_dimension=0, tiled=True)]
    unnamed x1 -> x0, blocking collectives: 38.8 us -> none
    convert_element_type x9 -> x0, local copies, waits for them, and re-layouts: 29.1 us -> none  [the longest x6 17.8 us: ff_back(): return jnp.transpose(part.reshape(n, wrows, zs, ff_block), (1, 2, 0, 3))....]
    dot_general x3 -> x0, matrix products: 21.6 us -> none  [dot(): return lax.dot_general(a, b, (dims, ((), ())), preferred_element_type=f32)]
    all_to_all x2 -> x0, waiting for transfers between devices: 13.9 us -> none  [exchange(): return lax.all_to_all(v, 'ctx', 0, 0, tiled=True)]
    all_to_all x2 -> x0, starting transfers between devices: 9.3 us -> none  [exchange(): return lax.all_to_all(v, 'ctx', 0, 0, tiled=True)]
    pallas_call x1, Pallas kernels: 131 us -> 122 us  [backward(): pl.pallas_call(functools.partial(backward_kernel, zs, n), out_shape=[jax....]
  transfers between devices with their start and end apart: 5 -> 0, of which waited for: 3 -> 0; matrix products, arithmetic and copies ran while one was open for 7% -> 0% of each run, Pallas kernels for 20% -> 0%
where the time goes in v4:
time: 554 us; the launch traced here: 551 us
  Pallas kernels  520 us (94%)
  local copies, waits for them, and re-layouts  23.7 us (4%)
  other arithmetic  5.79 us (1%)
    pallas_call x1, Pallas kernels, backward(): pl.pallas_call(functools.partial(backward_kernel, zs, n), out_shape=[jax....  122 us
    pallas_call x1, Pallas kernels, forward(): pl.pallas_call(functools.partial(forward_kernel, zs, n), out_shape=[jax.S...  111 us
    pallas_call x1, Pallas kernels, last(): pl.pallas_call(functools.partial(last_kernel, zs, n), out_shape=[jax.Shap...  103 us
    pallas_call x1, Pallas kernels, middle(): pl.pallas_call(functools.partial(middle_kernel, zs, n), out_shape=[jax.Sh...  97.8 us
    pallas_call x1, Pallas kernels, spread(): pl.pallas_call(functools.partial(spread_kernel, zs, n), out_shape=[jax.Sh...  87.1 us
    unnamed x41, local copies, waits for them, and re-layouts  11.2 us

profile of v4, /device:TPU:1, one launch (start us, length us, event | category | flops | bytes accessed | tf_op | source)
XLA Modules:
  0.0 551.0 jit_solution(12396658513503048312)
XLA Ops:
  0.7 0.1 pad.17.clone
  0.8 0.1 pad.14.clone
  0.8 3.4 concatenate.16
  4.3 0.1 fusion.1
  4.4 0.1 maximum_maximum_fusion.1
  4.5 0.1 tile.26
  4.6 0.2 tile.27
  4.8 0.4 copy.33
  5.2 0.1 tile.28
  5.2 0.2 tile.29
  5.5 0.4 copy.34
  5.8 0.1 tile.24
  5.9 0.2 tile.25
  6.1 0.4 copy.32
  6.5 0.0 copy-start.15
  6.5 0.0 copy-start.16
  6.5 0.0 copy-start.8
  6.5 1.2 pad_maximum_fusion.tables
  7.8 0.0 copy-done.15
  7.8 0.2 copy.30
  7.9 0.0 copy-start.2
  8.0 0.1 copy-done.16
  8.1 0.2 copy.31
  8.3 0.2 copy-done.8
  8.5 0.6 copy-done.6
  9.1 0.3 copy-done.7
  9.4 0.1 copy-done.9
  9.5 87.1 %spread.1 = (bf16[4,8,64,768]{3,2,1,0:T(8,128)(2,1)S(1)}, bf16[4,64,2048]{2,1,0:T(8,128)(2,1)S(1)}, bf16[8,64,1408]{2,1,0:T(8,128)(2,1)S(1)}, bf16[8,128,2048]{2...) custom-call(bf16[64,6144]{1,0:T(8,128)(2,1)S(1)} %copy-done.6, ...), custom_call_target="tpu_custom_call" | custom-call | tf_op jit(solution)/shard_map/spread/pallas_call | solution.py:549
  96.6 0.0 copy-done.2
  96.6 0.0 copy-start
  96.6 1.9 copy-done
  98.6 1.6 copy-done.1
  100.2 1.0 copy-done.3
  101.1 2.0 copy-done.4
  103.1 1.1 copy-done.5
  104.3 0.1 fusion.3
  104.3 0.1 reshape.107
  104.4 0.1 reshape.110
  104.5 0.1 reshape.109
  104.6 0.1 reshape.108
  104.7 0.7 pad_maximum_fusion.1.norms
  105.3 0.1 reshape.111
  105.4 0.7 reshape.112.bias
  106.1 110.8 %forward.1 = (bf16[8,128,2048]{2,1,0:T(8,128)(2,1)}, bf16[3,2,8,64,256]{4,3,2,1,0:T(8,128)(2,1)}, bf16[2,4,512,512]{3,2,1,0:T(8,128)(2,1)}, bf16[8,2,64,256]{3,2...) custom-call(s32[1,2]{1,0:T(1,128)} %lengths.1, ...), custom_call_target="tpu_custom_call" | custom-call | tf_op jit(solution)/shard_map/forward/pallas_call | solution.py:824
  216.9 97.8 %middle.1 = (bf16[4,256,1408]{2,1,0:T(8,128)(2,1)}, bf16[4,176,2048]{2,1,0:T(8,128)(2,1)}, f32[176,2048]{1,0:T(8,128)}) custom-call(bf16[4,256,704]{2,1,0:T(8,128)(2,1)} %get-tuple-element.48.zz, f32[4,256,1408]{2,1,0:T(8,128)} %get-tuple-element.49.gu, bf16[8,128,2048]{2,1,0:T(8,128)(2,1)} %copy-done, bf16[176,2048]{1,0:T(8,128)(2,1)} %w_down.1), custom_call_target="tpu_custom_call" | custom-call | tf_op jit(solution)/shard_map/middle/pallas_call | solution.py:1023
  314.7 121.8 %backward.1 = (bf16[512,1408]{1,0:T(8,128)(2,1)}, f32[64,2048]{1,0:T(8,128)}, f32[128,2048]{1,0:T(8,128)}, bf16[8,2,64,768]{3,2,1,0:T(8,128)(2,1)}, f32[2,2048]{1,0:T(2,128)}, /*index=5*/f32[1,768]{1,0:T(1,128)}) custom-call(f32[4,2048]{1,0:T(4,128)} %pad_maximum_fusion.1.norms, f32[3,8,64,256]{3,2,1,0:T(8,128)} %pad_maximum_fusion.tables, ...), custom_call_target="tpu_custom_call" | custom-call | tf_op jit(solution)/shard_map/backward/pallas_call | solution.py:1269
  436.5 102.7 %last.1 = (bf16[128,2048]{1,0:T(8,128)(2,1)}, f32[128,2048]{1,0:T(8,128)}, bf16[64,6144]{1,0:T(8,128)(2,1)}, bf16[64,5632]{1,0:T(8,128)(2,1)}, bf16[64,5632]{1,0:T(8,128)(2,1)}, /*index=5*/f32[8,128]{1,0:T(8,128)}) custom-call(f32[4,2048]{1,0:T(4,128)} %pad_maximum_fusion.1.norms, f32[2,2048]{1,0:T(2,128)} %get-tuple-element.57.gains_two, ...), custom_call_target="tpu_custom_call" | custom-call | tf_op jit(solution)/shard_map/last/pallas_call | solution.py:1555
  539.3 0.0 copy-start.11
  539.3 0.0 copy-start.18
  539.3 0.0 copy-start.14
  539.3 2.5 copy.44
  541.8 0.0 copy-done.11
  541.8 1.8 copy.43
  543.6 0.6 dynamic_slice.11
  544.2 0.1 constant_dynamic-slice_fusion
  544.3 0.5 slice_bitcast_fusion.1
  544.9 0.0 copy-done.14
  544.9 1.2 convert_element_type.13
  546.1 1.2 convert_element_type.14
  547.2 0.2 copy-done.12
  547.5 1.2 convert_element_type.12
  548.7 0.8 copy.48
  549.5 0.1 copy-done.10
  549.6 1.1 copy.49
  (24 shorter events, 0.1 us)
Async XLA Ops:
  6.5 1.3 copy-start.15
  6.5 1.6 copy-start.16
  6.5 2.0 copy-start.8
  7.8 1.3 copy-start.6
  7.8 1.6 copy-start.7
  7.8 1.7 copy-start.9
  7.9 88.7 %copy-start.2 = (bf16[2,64,2048]{2,1,0:T(8,128)(2,1)}, bf16[2,64,2048]{2,1,0:T(8,128)(2,1)S(1)}, u32[]{:S(2)}) copy-start(bf16[2,64,2048]{2,1,0:T(8,128)(2,1)S(1)} %copy.30) | copy-start | bytes 1572868
  96.6 2.0 copy-start
  98.6 1.6 copy-start.1
  100.2 1.0 copy-start.3
  101.1 2.0 copy-start.4
  103.1 1.1 copy-start.5
  539.3 2.5 copy-start.11
  539.3 4.3 copy-start.18
  539.3 5.6 %copy-start.14 = (bf16[64,5632]{1,0:T(8,128)(2,1)S(1)}, bf16[64,5632]{1,0:T(8,128)(2,1)}, u32[]{:S(2)}) copy-start(bf16[64,5632]{1,0:T(8,128)(2,1)} %get-tuple-element.69) | copy-start | bytes 2162692
  543.6 2.5 copy-start.13
  546.0 1.4 copy-start.12
  547.5 1.3 copy-start.17
  547.5 2.1 copy-start.10

commit v5 on v3

--- a/solution.py
+++ b/solution.py
@@ -4,6 +4,7 @@
 
 import jax
 import jax.numpy as jnp
+import numpy as np
 from jax import lax
 from jax.experimental import pallas as pl
 from jax.experimental.pallas import tpu as pltpu
@@ -324,6 +325,7 @@
 MESH = pl.DeviceIdType.MESH
 HBM = pl.BlockSpec(memory_space=pltpu.HBM)
 VMEM = pl.BlockSpec(memory_space=pltpu.VMEM)
+VMEM_LIMIT = 60 << 20
 
 
 def flip(index, mask):
@@ -342,13 +344,16 @@
         self.number = itertools.count()
 
     def put(self, src, dst, z_mask, c_mask):
+        return self.put_to(src, dst, flip(self.z, z_mask), flip(self.c, c_mask))
+
+    def put_to(self, src, dst, z, c):
         i = next(self.number)
         return pltpu.make_async_remote_copy(
             src_ref=src,
             dst_ref=dst,
             send_sem=self.send.at[i],
             recv_sem=self.recv.at[i],
-            device_id=(flip(self.z, z_mask), flip(self.c, c_mask)),
+            device_id=(z, c),
             device_id_type=MESH,
         )
 
@@ -375,10 +380,14 @@
         far = flip(z, 2)
         self.on = wires.put(part(far), part(far), 1, 0)
 
-    def start(self):
-        self.skip.start()
-        pl.when(self.wires.inner)(self.mid.start)
-        self.near.start()
+    @staticmethod
+    def start(parts):
+        for part in parts:
+            part.skip.start()
+        for part in parts:
+            pl.when(part.wires.inner)(part.mid.start)
+        for part in parts:
+            part.near.start()
 
     def forward(self):
         @pl.when(self.wires.inner)
@@ -444,13 +453,11 @@
     w_up,
     w_out,
     xs,
-    dy,
     small,
     qkv_all,
     out_all,
     gu_own,
     xs_all,
-    dy_all,
     small_all,
     qkv_send,
     gu_send,
@@ -469,21 +476,20 @@
         pltpu.make_async_copy(qkv_send.at[c], qkv_all.at[z, c], local.at[1]),
         pltpu.make_async_copy(gu_send.at[c], gu_own.at[c], local.at[2]),
         pltpu.make_async_copy(xs, xs_all.at[c], local.at[3]),
-        pltpu.make_async_copy(dy, dy_all.at[c], local.at[4]),
-        pltpu.make_async_copy(small, small_all.at[z, c], local.at[5]),
+        pltpu.make_async_copy(small, small_all.at[z, c], local.at[4]),
     ]
-    for i in (0, 3, 4, 5):
+    for i in (0, 3, 4):
         own[i].start()
     pack_columns(
         qkv_send, [(w_qkv.at[:, i * width : (i + 1) * width], HEAD_DIM) for i in range(3)], n, zs
     )
     own[1].start()
     wires.greet(zs, n)
-    for i in (0, 5):
+    for i in (0, 4):
         own[i].wait()
 
     out_z = DepthGather(wires, lambda i: out_all.at[i])
-    out_z.start()
+    DepthGather.start([out_z])
     qkv_x = [
         wires.put(qkv_send.at[flip(c, m)], qkv_all.at[z, c], 0, m) for m in range(1, n)
     ]
@@ -506,32 +512,25 @@
     own[1].wait()
     for copy in qkv_x:
         copy.wait_recv()
-    half = n // 2
     qkv_z = [
-        DepthGather(wires, lambda i, p=p: qkv_all.at[i, p * half : (p + 1) * half])
-        for p in range(2)
+        DepthGather(wires, lambda i, a=a, s=s: qkv_all.at[i, a : a + s])
+        for a, s in pieces_of(n, 4, 1)
     ]
-    for part in qkv_z:
-        part.start()
+    DepthGather.start(qkv_z)
     out_z.forward()
     gu_x = [wires.put(gu_send.at[flip(c, m)], gu_own.at[c], 0, m) for m in range(1, n)]
     for copy in gu_x:
         copy.start()
     for m in (2, 4, 6):
         xs_g.forward(m)
-    dy_g = LayerGather(wires, dy_all, dy)
-    dy_g.start()
-    qkv_z[0].forward()
-    for m in (2, 4, 6):
-        dy_g.forward(m)
-    qkv_z[1].forward()
-
-    for i in (2, 3, 4):
+    for part in qkv_z:
+        part.forward()
+
+    for i in (2, 3):
         own[i].wait()
-    for group in (xs_g, dy_g):
-        for m in (1, 3, 5, 7):
-            group.arrived(m)
-        group.sent()
+    for m in (1, 3, 5, 7):
+        xs_g.arrived(m)
+    xs_g.sent()
     for copy in small_z:
         copy.wait_send()
     for copy in qkv_x:
@@ -542,7 +541,7 @@
         part.finish()
 
 
-def spread(zs, n, w_qkv, w_gate, w_up, w_out, xs, dy, small):
+def spread(zs, n, w_qkv, w_gate, w_up, w_out, xs, small):
     wrows, width = w_out.shape
     qc, gc = w_qkv.shape[1] // n, 2 * w_gate.shape[1] // n
     b16 = jnp.bfloat16
@@ -553,23 +552,22 @@
             jax.ShapeDtypeStruct((zs, wrows, width), b16),
             jax.ShapeDtypeStruct((n, wrows, gc), b16),
             jax.ShapeDtypeStruct((n, *xs.shape), b16),
-            jax.ShapeDtypeStruct((n, *dy.shape), b16),
             jax.ShapeDtypeStruct((zs, n, *small.shape), small.dtype),
         ],
-        in_specs=[VMEM, VMEM, VMEM, HBM, HBM, HBM, HBM],
-        out_specs=[HBM] * 6,
+        in_specs=[VMEM, VMEM, VMEM, HBM, HBM, HBM],
+        out_specs=[HBM] * 5,
         scratch_shapes=[
             pltpu.VMEM((n, wrows, qc), b16),
             pltpu.VMEM((n, wrows, gc), b16),
             pltpu.SemaphoreType.DMA((64,)),
             pltpu.SemaphoreType.DMA((64,)),
-            pltpu.SemaphoreType.DMA((6,)),
+            pltpu.SemaphoreType.DMA((5,)),
         ],
         compiler_params=pltpu.CompilerParams(
             collective_id=1, has_side_effects=True, vmem_limit_bytes=32 << 20
         ),
         name="spread",
-    )(w_qkv, w_gate, w_up, w_out, xs, dy, small)
+    )(w_qkv, w_gate, w_up, w_out, xs, small)
 
 
 class LayerScatter:
@@ -615,6 +613,7 @@
 def turn_pair(values, table, sign):
     half = ROTARY // 2
     columns = values.shape[-1]
+    table = [jnp.concatenate([t] * (columns // t.shape[-1]), -1) for t in table]
     return (
         values * table[0]
         + sign * (pltpu.roll(values, columns - half, 1) * table[1])
@@ -637,6 +636,7 @@
     w_qkv,
     w_out,
     gu_own,
+    dy,
     a1_out,
     qkv_out,
     probs_out,
@@ -646,6 +646,7 @@
     w_gu_out,
     gu_out,
     zz_out,
+    dy_all,
     xs_v,
     a1_v,
     w_qkv_v,
@@ -691,8 +692,9 @@
         DepthGather(wires, lambda i, p=p: w_gu_v.at[i, p * chunk : (p + 1) * chunk])
         for p in range(chunks)
     ]
-    for part_z in gu_z:
-        part_z.start()
+    DepthGather.start(gu_z)
+    dy_g = LayerGather(wires, dy_all, dy)
+    dy_g.start()
     stores = []
 
     def store(src, dst):
@@ -700,6 +702,7 @@
         copy.start()
         stores.append(copy)
 
+    store(dy, dy_all.at[c])
     for copy in loads[1:]:
         copy.wait()
 
@@ -709,7 +712,7 @@
         a1_v[pl.ds(2 * i, 2)] = a1.reshape(2, slots * rows, width)
         joined = dot(a1, w_qkv_v[...].reshape(width, 3 * hc)) + bias[...]
         for j in range(2):
-            table = tables[:, 2 * i + j]
+            table = [tables[k, 2 * i + j] for k in range(3)]
             for s in range(slots):
                 at = (j * slots + s) * rows
                 piece = joined[at : at + rows]
@@ -751,6 +754,8 @@
         return carry
 
     lax.fori_loop(0, slots, attend, 0)
+    for m in (2, 4, 6):
+        dy_g.forward(m)
     store(probs_v, probs_out)
     store(ob_v, ob_out)
 
@@ -797,11 +802,14 @@
     store(zz_v, zz_out)
     sums.sent()
     a2_g.sent()
+    for m in (1, 3, 5, 7):
+        dy_g.arrived(m)
+    dy_g.sent()
     for copy in stores:
         copy.wait()
 
 
-def forward(zs, n, slots, lengths, norms, bias, tables, xs_all, w_qkv, w_out, gu_own):
+def forward(zs, n, slots, lengths, norms, bias, tables, xs_all, w_qkv, w_out, gu_own, dy):
     _, local, width = xs_all.shape
     rows = local // slots
     seq = rows * n
@@ -823,9 +831,9 @@
     a1, qkv, probs, ob, hidden, a2, w_gu, gu, zz = [pltpu.VMEM(*k) for k in kept]
     return pl.pallas_call(
         functools.partial(forward_kernel, zs, n),
-        out_shape=[jax.ShapeDtypeStruct(*k) for k in kept],
-        in_specs=[pl.BlockSpec(memory_space=pltpu.SMEM)] + [VMEM] * 3 + [HBM] * 4,
-        out_specs=[HBM] * len(kept),
+        out_shape=[jax.ShapeDtypeStruct(*k) for k in (*kept, ((n, local, width), b16))],
+        in_specs=[pl.BlockSpec(memory_space=pltpu.SMEM)] + [VMEM] * 3 + [HBM] * 5,
+        out_specs=[HBM] * (len(kept) + 1),
         scratch_shapes=[
             pltpu.VMEM(xs_all.shape, b16),
             a1,
@@ -845,13 +853,13 @@
             pltpu.SemaphoreType.DMA((40,)),
             pltpu.SemaphoreType.DMA((40,)),
             pltpu.SemaphoreType.DMA((4,)),
-            pltpu.SemaphoreType.DMA((len(kept),)),
+            pltpu.SemaphoreType.DMA((len(kept) + 1,)),
         ],
         compiler_params=pltpu.CompilerParams(
             collective_id=2, has_side_effects=True, vmem_limit_bytes=60 << 20
         ),
         name="forward",
-    )(lengths, norms, bias, tables, xs_all, w_qkv, w_out, gu_own)
+    )(lengths, norms, bias, tables, xs_all, w_qkv, w_out, gu_own, dy)
 
 
 class DepthScatter:
@@ -863,15 +871,20 @@
         self.near = wires.put(part(flip(z, 1)), boxes[0], 1, 0)
         self.mid = wires.put(part(flip(z, 3)), boxes[2], 3, 0)
 
-    def start(self):
-        @pl.when(self.wires.outer)
-        def _():
-            self.far.start()
-            self.skip.start()
-            self.boxes[2][...] = jnp.zeros_like(self.boxes[2])
-
-        pl.when(self.wires.inner)(self.mid.start)
-        self.near.start()
+    def start(self, mask):
+        outer, inner = pl.when(self.wires.outer), pl.when(self.wires.inner)
+        if mask == 3:
+            outer(self.far.start)
+            inner(self.mid.start)
+        elif mask == 2:
+            outer(self.skip.start)
+        elif mask == 1:
+            self.near.start()
+        else:
+
+            @outer
+            def _():
+                self.boxes[2][...] = jnp.zeros_like(self.boxes[2])
 
     def relay(self):
         @pl.when(self.wires.inner)
@@ -922,6 +935,92 @@
     return [(a, b - a) for a, b in zip(cuts[:-1], cuts[1:])]
 
 
+class ChainGather:
+    def __init__(self, wires, part):
+        self.z = z = wires.z
+        self.right = [
+            wires.put_to(part((z - s + 4) % 4), part((z - s + 4) % 4), (z + 1) % 4, wires.c)
+            for s in range(3)
+        ]
+        self.left = [
+            wires.put_to(part((z + s) % 4), part((z + s) % 4), (z + 3) % 4, wires.c)
+            for s in range(3)
+        ]
+
+    def start(self):
+        pl.when(self.z <= 2)(self.right[0].start)
+        pl.when(self.z >= 1)(self.left[0].start)
+
+    def hop(self, s):
+        pl.when(self.z >= s)(self.right[s - 1].wait_recv)
+        pl.when((self.z >= s) & (self.z <= 2))(self.right[s].start)
+        pl.when(self.z <= 3 - s)(self.left[s - 1].wait_recv)
+        pl.when((self.z <= 3 - s) & (self.z >= 1))(self.left[s].start)
+
+    def finish(self):
+        pl.when(self.z >= 3)(self.right[2].wait_recv)
+        pl.when(self.z <= 0)(self.left[2].wait_recv)
+        for s in range(3):
+            pl.when((self.z >= s) & (self.z <= 2))(self.right[s].wait_send)
+            pl.when((self.z <= 3 - s) & (self.z >= 1))(self.left[s].wait_send)
+
+
+class ChainScatter:
+    def __init__(self, wires, part, right, left):
+        self.z = z = wires.z
+        self.part, self.right_box, self.left_box = part, right, left
+        self.right = {
+            j: wires.put_to(part(j), right(j), (z + 1) % 4, wires.c) for j in (3, 2, 1)
+        }
+        self.left = {j: wires.put_to(part(j), left(j), (z + 3) % 4, wires.c) for j in (0, 1, 2)}
+
+    def clear(self):
+        @pl.when(self.z == 0)
+        def _():
+            self.right_box(0)[...] = jnp.zeros_like(self.right_box(0))
+
+        @pl.when(self.z == 3)
+        def _():
+            self.left_box(3)[...] = jnp.zeros_like(self.left_box(3))
+
+    def start(self, distance):
+        pl.when(self.z == 0)(self.right[distance].start)
+        pl.when(self.z == 3)(self.left[3 - distance].start)
+
+    def pass_on(self, copy, j, box):
+        copy.wait_recv()
+        to = self.part(j)
+        to[...] = (to[...].astype(jnp.float32) + box(j)[...].astype(jnp.float32)).astype(to.dtype)
+        copy.start()
+
+    def hop(self, s, distance):
+        @pl.when(self.z == s)
+        def _():
+            self.pass_on(self.right[distance], distance, self.right_box)
+
+        @pl.when(self.z == 3 - s)
+        def _():
+            self.pass_on(self.left[3 - distance], 3 - distance, self.left_box)
+
+    def total(self):
+        for j in (1, 2, 3):
+            pl.when(self.z == j)(self.right[j].wait_recv)
+        for j in (0, 1, 2):
+            pl.when(self.z == j)(self.left[j].wait_recv)
+        z = self.z
+        return (
+            self.part(z)[...].astype(jnp.float32)
+            + self.right_box(z)[...].astype(jnp.float32)
+            + self.left_box(z)[...].astype(jnp.float32)
+        )
+
+    def sent(self):
+        for j in (1, 2, 3):
+            pl.when(self.z < j)(self.right[j].wait_send)
+        for j in (0, 1, 2):
+            pl.when(self.z > j)(self.left[j].wait_send)
+
+
 def middle_kernel(
     zs,
     n,
@@ -929,18 +1028,24 @@
     gu,
     dy_all,
     w_down,
+    hidden,
     dgu_out,
-    w_down_out,
     grad_down_out,
+    result_out,
     zz_v,
     gu_v,
     dy_v,
     w_down_v,
+    hidden_v,
     dgu_v,
     gd_v,
-    relay_v,
-    box_v,
+    right_v,
+    left_v,
     total_v,
+    dz_v,
+    part,
+    near,
+    far,
     send,
     recv,
     local,
@@ -955,50 +1060,79 @@
     wait_down = moves.load(w_down, w_down_v.at[z])
     wait_zz = moves.load(zz, zz_v)
     wait_dy = moves.load(dy_all, dy_v)
-    wait_gu = moves.load(gu, gu_v)
+    waits = [moves.load(gu, gu_v), moves.load(hidden, hidden_v)]
     wires.greet(zs, n)
     wait_down.wait()
-    down_z = [
-        DepthGather(wires, lambda i, a=a, s=s: w_down_v.at[i, a : a + s])
-        for a, s in pieces_of(block, 4, 16)
-    ]
-    for part in down_z:
-        part.start()
+    number = 4
+    tile = width // number
+    columns = [slice(p * tile, (p + 1) * tile) for p in range(number)]
+    down_z = [ChainGather(wires, lambda i, k=k: w_down_v.at[i, :, k]) for k in columns]
+    for chain in down_z:
+        chain.start()
     wait_zz.wait()
     wait_dy.wait()
-    number = 4
-    tile = width // number
     sums = [
-        DepthScatter(
+        ChainScatter(
             wires,
-            lambda i, a=p * tile: gd_v.at[i, :, a : a + tile],
-            relay_v.at[:, p * tile : (p + 1) * tile],
-            [box_v.at[j, :, p * tile : (p + 1) * tile] for j in range(3)],
+            lambda i, k=k: gd_v.at[i, :, k],
+            lambda i, k=k: right_v.at[i, :, k],
+            lambda i, k=k: left_v.at[i, :, k],
         )
-        for p in range(number)
+        for k in columns
     ]
-    for p in range(number):
+    y_sums = [
+        LayerScatter(wires, part.at[:, :, k], near.at[:, :, k], far.at[:, :, k]) for k in columns
+    ]
+    for k, chain in zip(columns, sums):
         gd = dot(
-            zz_v[...].reshape(tokens, ffc),
-            dy_v[:, :, p * tile : (p + 1) * tile].reshape(tokens, tile),
-            ((0,), (0,)),
+            zz_v[...].reshape(tokens, ffc), dy_v[:, :, k].reshape(tokens, tile), ((0,), (0,))
         )
-        gd_v[:, :, p * tile : (p + 1) * tile] = gd.astype(b16).reshape(zs, block, tile)
-        sums[p].start()
-    for p in range(number):
-        down_z[p].forward()
-        sums[p].relay()
-    for part in down_z:
-        part.finish()
-    moves.store(w_down_v, w_down_out)
-    wait_gu.wait()
+        gd_v[:, :, k] = gd.astype(b16).reshape(zs, block, tile)
+        chain.start(3)
+    for distance in (2, 1):
+        for chain in sums:
+            chain.start(distance)
+    for chain in sums:
+        chain.clear()
+    for copy in waits:
+        copy.wait()
+
+    def products(p):
+        k = columns[p]
+
+        def rows(i, carry):
+            weight = w_down_v[:, :, k].reshape(ffc, tile)
+            dy_rows = dy_v[pl.ds(2 * i, 2), :, k].reshape(2 * tokens // n, tile)
+            dz = dot(dy_rows, weight, ((1,), (1,)))
+            dz_v[i] = dz if p == 0 else dz_v[i] + dz
+            part[pl.ds(2 * i, 2), :, k] = (
+                dot(zz_v[i], weight).astype(b16).reshape(2, tokens // n, tile)
+            )
+            return carry
+
+        lax.fori_loop(0, n // 2, rows, 0)
+
+    for t in range(number + 1):
+        if t < number:
+            down_z[t].hop(1)
+        if t >= 1:
+            down_z[t - 1].hop(2)
+    for t in range(number):
+        sums[t].hop(1, 3)
+        down_z[t].finish()
+        products(t)
+        y_sums[t].start()
+        if t >= 1:
+            for m in (6, 4, 2):
+                y_sums[t - 1].step(m)
+    for m in (6, 4, 2):
+        y_sums[number - 1].step(m)
+    for chain in sums:
+        chain.hop(1, 2)
+        chain.hop(2, 3)
 
     def back(i, carry):
-        dz = dot(
-            dy_v[pl.ds(2 * i, 2)].reshape(tokens // (n // 2), width),
-            w_down_v[...].reshape(ffc, width),
-            ((1,), (1,)),
-        )
+        dz = dz_v[i]
         gu_block = gu_v[i]
         gate, up = gu_block[:, :ffc], gu_block[:, ffc:]
         sig = jax.nn.sigmoid(gate)
@@ -1009,45 +1143,64 @@
 
     lax.fori_loop(0, n // 2, back, 0)
     moves.store(dgu_v, dgu_out)
-    for p in range(number):
-        total_v[:, p * tile : (p + 1) * tile] = sums[p].total()
+    for k, chain in zip(columns, sums):
+        total_v[:, k] = chain.total()
     moves.store(total_v, grad_down_out)
-    for part in sums:
-        part.sent()
+    for k, y_sum in zip(columns, y_sums):
+        result_out[:, k] = (hidden_v[:, k] + y_sum.total()).astype(b16)
+    for group in (*sums, *y_sums):
+        group.sent()
     moves.finish()
 
 
-def middle(zs, n, zz, gu, dy_all, w_down):
+def middle(zs, n, zz, gu, dy_all, w_down, hidden):
     f32, b16 = jnp.float32, jnp.bfloat16
     block, width = w_down.shape
+    local = hidden.shape[0]
     return pl.pallas_call(
         functools.partial(middle_kernel, zs, n),
         out_shape=[
             jax.ShapeDtypeStruct(gu.shape, b16),
-            jax.ShapeDtypeStruct((zs, block, width), b16),
             jax.ShapeDtypeStruct((block, width), f32),
+            jax.ShapeDtypeStruct((local, width), b16),
         ],
-        in_specs=[HBM] * 4,
-        out_specs=[HBM] * 3,
+        in_specs=[HBM] * 5,
+        out_specs=[HBM, HBM, VMEM],
         scratch_shapes=[
             pltpu.VMEM(zz.shape, b16),
             pltpu.VMEM(gu.shape, f32),
             pltpu.VMEM(dy_all.shape, b16),
             pltpu.VMEM((zs, block, width), b16),
+            pltpu.VMEM((local, width), f32),
             pltpu.VMEM(gu.shape, b16),
             pltpu.VMEM((zs, block, width), b16),
-            pltpu.VMEM((block, width), b16),
-            pltpu.VMEM((3, block, width), b16),
+            pltpu.VMEM((zs, block, width), b16),
+            pltpu.VMEM((zs, block, width), b16),
             pltpu.VMEM((block, width), f32),
-            pltpu.SemaphoreType.DMA((40,)),
-            pltpu.SemaphoreType.DMA((40,)),
+            pltpu.VMEM(zz.shape, f32),
+            pltpu.VMEM((n, local, width), b16),
+            pltpu.VMEM((n // 2, local, width), b16),
+            pltpu.VMEM((n // 2 - 1, local, width), b16),
+            pltpu.SemaphoreType.DMA((80,)),
+            pltpu.SemaphoreType.DMA((80,)),
             pltpu.SemaphoreType.DMA((8,)),
         ],
         compiler_params=pltpu.CompilerParams(
             collective_id=3, has_side_effects=True, vmem_limit_bytes=60 << 20
         ),
         name="middle",
-    )(zz, gu, dy_all, w_down)
+    )(zz, gu, dy_all, w_down, hidden)
+
+
+def unpack_columns(dst, src, at, block, n, zs):
+    dst[...] = jnp.concatenate(
+        [
+            src[i, :, at + block * j : at + block * (j + 1)]
+            for j in range(zs)
+            for i in range(n)
+        ],
+        -1,
+    )
 
 
 def backward_kernel(
@@ -1055,45 +1208,53 @@
     n,
     norms,
     tables,
+    a1_all,
     a2_all,
     dgu,
     w_gu,
+    w_qkv,
     w_out,
     qkv,
     probs,
     ob,
     hidden,
     dy_all,
-    ggu_out,
+    xs,
     grad_out_out,
-    dh_out,
-    dj_out,
-    gains_out,
-    bias_out,
-    a2_v,
+    input_grad_out,
+    gq_out,
+    gate_out,
+    up_out,
+    small_out,
+    wide_v,
     dgu_v,
-    w_gu_v,
+    weight_v,
     w_out_v,
     qkv_v,
     probs_v,
     ob_v,
     hidden_v,
-    dy_v,
+    own_v,
     ggu_v,
     relay_v,
     box_v,
-    part,
     near,
     far,
-    dh_v,
     dh_all,
     go_v,
     go_relay,
     go_box,
-    go_total,
-    do_v,
     dqkv_v,
     dj_v,
+    bias_v,
+    gq_relay,
+    gq_box,
+    gu_rows,
+    gq_rows,
+    small_v,
+    small_x,
+    small_r,
+    small_z,
     send,
     recv,
     local,
@@ -1103,20 +1264,25 @@
     moves = Moves(local)
     z, c = wires.z, wires.c
     _, slots, rows, hc = ob_v.shape
-    width = dh_v.shape[-1]
+    width = dh_all.shape[-1]
     tokens, seq, local_rows = n * slots * rows, n * rows, slots * rows
     heads = hc // HEAD_DIM
     depth, gc = ggu_v.shape[1:]
-
-    wait_a2 = moves.load(a2_all, a2_v)
+    ffc, qc = gc // 2, 3 * hc
+    wrows = depth // n
+    part = wide_v
+    gu_weight = weight_v.at[:, :, 0:gc]
+    qkv_weight, gq_v = weight_v.at[:, :, 0:qc], weight_v.at[:, :, qc : 2 * qc]
+
+    wait_a2 = moves.load(a2_all, wide_v)
     wait_dgu = moves.load(dgu, dgu_v)
-    wait_w = moves.load(w_gu, w_gu_v)
+    wait_w = moves.load(w_gu, gu_weight)
     waits = [
         moves.load(hidden, hidden_v),
-        moves.load(dy_all.at[c], dy_v),
+        moves.load(dy_all.at[c], own_v),
         moves.load(w_out, w_out_v),
         moves.load(qkv, qkv_v),
-        moves.load(probs, probs_v),
+        moves.load(probs.at[0], probs_v),
         moves.load(ob, ob_v),
     ]
     wires.greet(zs, n)
@@ -1125,67 +1291,92 @@
 
     number = 4
     size = depth // number
-    sums = [
-        DepthScatter(
-            wires,
-            lambda i, a=p * size: ggu_v.at[i, a : a + size],
-            relay_v.at[p * size : (p + 1) * size],
-            [box_v.at[j, p * size : (p + 1) * size] for j in range(3)],
-        )
-        for p in range(number)
-    ]
     step = 2 * size
-    for p in range(number // 2):
-
-        def weigh(i, carry, p=p):
-            at = pl.multiple_of(i * depth + p * step, step)
-            left = a2_v[:, :, pl.ds(at, step)].reshape(tokens, step)
-            ggu_v[i, p * step : (p + 1) * step] = dot(
-                left, dgu_v[...].reshape(tokens, gc), ((0,), (0,))
-            ).astype(b16)
-            return carry
-
-        lax.fori_loop(0, zs, weigh, 0)
-        sums[2 * p].start()
-        sums[2 * p + 1].start()
+
+    def scatters(whole, relay, box):
+        return [
+            DepthScatter(
+                wires,
+                lambda i, a=p * size: whole.at[i, a : a + size],
+                relay.at[p * size : (p + 1) * size],
+                [box.at[j, p * size : (p + 1) * size] for j in range(3)],
+            )
+            for p in range(number)
+        ]
+
+    def weigh(sums, whole, left_v, grads):
+        for mask in (3, 2, 1, 0):
+            to = flip(z, mask)
+
+            def piece(p, carry, to=to):
+                at = pl.multiple_of(to * depth + p * step, step)
+                left = left_v[:, :, pl.ds(at, step)].reshape(tokens, step)
+                whole[to, pl.ds(pl.multiple_of(p * step, step), step)] = dot(
+                    left, grads(), ((0,), (0,))
+                ).astype(b16)
+                return carry
+
+            lax.fori_loop(0, number // 2, piece, 0)
+            for part_sum in sums:
+                part_sum.start(mask)
+
+    gu_sums = scatters(ggu_v, relay_v, box_v)
+    weigh(gu_sums, ggu_v, wide_v, lambda: dgu_v[...].reshape(tokens, gc))
 
     wait_w.wait()
 
-    def normed(i, carry):
+    def normed_two(i, carry):
         part[pl.ds(2 * i, 2)] = (
-            dot(dgu_v[i], w_gu_v[...].reshape(width, gc), ((1,), (1,)))
+            dot(dgu_v[i], gu_weight[...].reshape(width, gc), ((1,), (1,)))
             .astype(b16)
             .reshape(2, local_rows, width)
         )
         return carry
 
-    lax.fori_loop(0, n // 2, normed, 0)
-    sums[0].relay()
+    lax.fori_loop(0, n // 2, normed_two, 0)
+    wait_qkv = moves.load(w_qkv, qkv_weight)
     da2_sums = LayerScatter(wires, part, near, far)
     da2_sums.start()
+    gu_sums[0].relay()
     for m in (6, 4, 2):
         da2_sums.step(m)
     for copy in waits:
         copy.wait()
     n2, r2 = layer_stats(hidden_v[...])
-    sums[1].relay()
+    for part_sum in gu_sums[1:]:
+        part_sum.relay()
     da2 = da2_sums.total()
-    gains_out[0:1] = jnp.sum(da2 * n2, 0, keepdims=True)
-    gains_out[1:2] = jnp.sum(da2, 0, keepdims=True)
-    dh = dy_v[...].astype(f32) + norm_back(da2, n2, r2, norms[2:3])
-    dh_v[...] = dh
-    moves.store(dh_v, dh_out)
+    gains = [jnp.sum(da2 * n2, 0, keepdims=True), jnp.sum(da2, 0, keepdims=True)]
+    dh = own_v[...].astype(f32) + norm_back(da2, n2, r2, norms[2:3])
+    input_grad_out[...] = dh
     dh_all[c] = dh.astype(b16)
+    wait_xs = moves.load(xs, own_v)
     dh_g = LayerGather(wires, dh_all)
     dh_g.start()
     for m in (2, 4, 6):
         dh_g.forward(m)
-    sums[2].relay()
     for m in (1, 3, 5, 7):
         dh_g.arrived(m)
 
+    go_sums = DepthScatter(
+        wires, lambda i: go_v.at[i], go_relay, [go_box.at[j] for j in range(3)]
+    )
+    tile = width // 4
+
+    def heads_grad(p, carry):
+        at = pl.ds(pl.multiple_of(p * tile, tile), tile)
+        go = dot(
+            ob_v[...].reshape(tokens, hc), dh_all[:, :, at].reshape(tokens, tile), ((0,), (0,))
+        )
+        go_v[:, :, at] = go.astype(b16).reshape(zs, hc // zs, tile)
+        return carry
+
+    lax.fori_loop(0, 4, heads_grad, 0)
+    for mask in (3, 2, 1, 0):
+        go_sums.start(mask)
+
     def heads_back(i, carry):
-        do_v[i] = (
+        ob_v[i] = (
             dot(dh_all[i], w_out_v[...].reshape(hc, width), ((1,), (1,)))
             .astype(b16)
             .reshape(slots, rows, hc)
@@ -1193,12 +1384,13 @@
         return carry
 
     lax.fori_loop(0, n, heads_back, 0)
-
+    dh_g.sent()
+    wait_a1 = moves.load(a1_all, dh_all)
     half = seq // 2
 
     def attend(s, carry):
         q, k, v = [qkv_v[i, s].reshape(seq, hc) for i in range(3)]
-        do_s = do_v[:, s].reshape(seq, hc)
+        do_s = ob_v[:, s].reshape(seq, hc)
         dqkv_v[...] = jnp.zeros_like(dqkv_v)
         for part_q in range(2):
             keys = (part_q + 1) * half
@@ -1208,7 +1400,7 @@
             for h in range(heads):
                 mask, mask_k = head_mask(half, hc, h), head_mask(keys, hc, h)
                 do_h = jnp.where(mask, do_q, 0).astype(b16)
-                low = probs_v[s, h, at : at + half, 0:keys]
+                low = probs_v[h, at : at + half, 0:keys]
                 p32 = low.astype(f32)
                 t = p32 * dot(do_h, v[:keys], ((1,), (1,)))
                 ds = (t - p32 * jnp.sum(t, -1, keepdims=True)).astype(b16)
@@ -1218,48 +1410,155 @@
                 dqkv_v[1, 0:keys] += jnp.where(mask_k, dk, 0.0)
                 dqkv_v[2, 0:keys] += dv
             dqkv_v[0, at : at + half] = dq
+
+        @pl.when(s + 1 < slots)
+        def _():
+            copy = pltpu.make_async_copy(probs.at[s + 1], probs_v, probs_sem)
+            copy.start()
+            copy.wait()
+
         dq, dk = dqkv_v[0] * 0.125, dqkv_v[1] * 0.125
-        table = [tables[i].reshape(seq, hc) for i in range(3)]
+        table = [tables[i].reshape(seq, 2 * HEAD_DIM) for i in range(3)]
         dj = [turn_pair(dq, table, -1.0), turn_pair(dk, table, -1.0), dqkv_v[2]]
         for i in range(3):
-            dj_v[:, s, :, i * hc : (i + 1) * hc] = dj[i].astype(b16).reshape(n, rows, hc)
+            low = dj[i].astype(b16)
+            dj_v[:, s, :, i * hc : (i + 1) * hc] = low.reshape(n, rows, hc)
+            bias_v[:, i * hc : (i + 1) * hc] += jnp.sum(low.astype(f32), 0, keepdims=True)
         return carry
 
+    bias_v[...] = jnp.zeros_like(bias_v)
+
+    probs_sem = moves.sems.at[next(moves.number)]
     lax.fori_loop(0, slots, attend, 0)
-    moves.store(dj_v, dj_out)
-    sums[3].relay()
-    dj_all = dj_v[...].reshape(tokens, 3 * hc).astype(f32)
-    bias_out[...] = jnp.sum(dj_all, 0, keepdims=True)
-
-    go_sums = DepthScatter(
-        wires, lambda i: go_v.at[i], go_relay, [go_box.at[j] for j in range(3)]
-    )
-    tile = width // 4
-    for p in range(4):
-        go = dot(
-            ob_v[...].reshape(tokens, hc),
-            dh_all[:, :, p * tile : (p + 1) * tile].reshape(tokens, tile),
-            ((0,), (0,)),
+    go_sums.relay()
+
+    wait_a1.wait()
+    wait_qkv.wait()
+    qkv_sums = scatters(gq_v, gq_relay, gq_box)
+    weigh(qkv_sums, gq_v, dh_all, lambda: dj_v[...].reshape(tokens, qc))
+
+    def normed_one(i, carry):
+        part[pl.ds(2 * i, 2)] = (
+            dot(
+                dj_v[pl.ds(2 * i, 2)].reshape(2 * local_rows, qc),
+                qkv_weight[...].reshape(width, qc),
+                ((1,), (1,)),
+            )
+            .astype(b16)
+            .reshape(2, local_rows, width)
         )
-        go_v[:, :, p * tile : (p + 1) * tile] = go.astype(b16).reshape(zs, hc // zs, tile)
-    go_sums.start()
-    for p in range(number):
-        a = p * size
-        ggu_v[z, a : a + size] = sums[p].total().astype(b16)
-        moves.store(ggu_v.at[z, a : a + size], ggu_out.at[a : a + size])
-    go_sums.relay()
-    go_total[...] = go_sums.total()
-    moves.store(go_total, grad_out_out)
-    for group in (*sums, go_sums, da2_sums, dh_g):
+        return carry
+
+    da2_sums.sent()
+    lax.fori_loop(0, n // 2, normed_one, 0)
+    da1_sums = LayerScatter(wires, part, near, far)
+    da1_sums.start()
+    for m in (6, 4, 2):
+        da1_sums.step(m)
+
+    for p, part_sum in enumerate(gu_sums):
+        ggu_v[z, p * size : (p + 1) * size] = part_sum.total().astype(b16)
+    gu_x = [
+        wires.put(
+            ggu_v.at[z, pl.ds(pl.multiple_of(flip(c, m) * wrows, wrows), wrows)],
+            gu_rows.at[c],
+            0,
+            m,
+        )
+        for m in range(1, n)
+    ]
+    for copy in gu_x:
+        copy.start()
+    gu_rows[c] = ggu_v[z, pl.ds(pl.multiple_of(c * wrows, wrows), wrows)]
+
+    wait_xs.wait()
+    n1, r1 = layer_stats(own_v[...].astype(f32))
+    da1 = da1_sums.total()
+    input_grad_out[...] += norm_back(da1, n1, r1, norms[0:1])
+    gains = [jnp.sum(da1 * n1, 0, keepdims=True), jnp.sum(da1, 0, keepdims=True), *gains]
+    for part_sum in qkv_sums:
+        part_sum.relay()
+    chips = n // 2
+    lanes = 2 * HEAD_DIM
+    lane_half = lax.broadcasted_iota(jnp.int32, (1, lanes), 1) // HEAD_DIM
+    bias_part = bias_v[...]
+    for j in range(zs):
+        for chip in range(chips):
+            k = j * chips + chip
+            for r in range(4):
+                small_v[j, chip, r : r + 1] = gains[r][:, k * lanes : (k + 1) * lanes]
+            small_v[j, chip, 7:8] = jnp.zeros((1, lanes), f32)
+    for i in range(3):
+        for j in range(zs):
+            at = i * hc + j * HEAD_DIM
+            piece = bias_part[:, at : at + HEAD_DIM]
+            both = jnp.concatenate([piece, piece], -1)
+            for chip in range(chips):
+                tile = (i * zs + j) * chips + chip
+                pair, row = tile // 3, tile % 3
+                small_v[pair // chips, pair % chips, 4 + row : 5 + row] = jnp.where(
+                    (lane_half == c % 2) & (c // 2 == chip), both, 0.0
+                )
+    small_v_x = [
+        wires.put(small_v.at[:, flip(c, m) // 2], small_x.at[m], 0, m) for m in range(1, n)
+    ]
+    for copy in small_v_x:
+        copy.start()
+    hidden_v[0:wrows] = go_sums.total()
+    moves.store(hidden_v.at[0:wrows], grad_out_out)
+    for copy in gu_x:
+        copy.wait_recv()
+    unpack_columns(gate_out, gu_rows, 0, ffc // zs, n, zs)
+    unpack_columns(up_out, gu_rows, ffc, ffc // zs, n, zs)
+    small_sum = small_v[:, c // 2]
+    for m in range(1, n):
+        small_v_x[m - 1].wait_recv()
+        small_sum = small_sum + small_x[m]
+    small_r[...] = small_sum
+    small_z_x = [wires.put(small_r.at[flip(z, m)], small_z.at[m], m, 0) for m in range(1, zs)]
+    for copy in small_z_x:
+        copy.start()
+    small_sum = small_r[z]
+    for m in range(1, zs):
+        small_z_x[m - 1].wait_recv()
+        small_sum = small_sum + small_z[m]
+    small_out[...] = small_sum
+
+    for p, part_sum in enumerate(qkv_sums):
+        gq_v[z, p * size : (p + 1) * size] = part_sum.total().astype(b16)
+    gq_x = [
+        wires.put(
+            gq_v.at[z, pl.ds(pl.multiple_of(flip(c, m) * wrows, wrows), wrows)],
+            gq_rows.at[c],
+            0,
+            m,
+        )
+        for m in range(1, n)
+    ]
+    for copy in gq_x:
+        copy.start()
+    gq_rows[c] = gq_v[z, pl.ds(pl.multiple_of(c * wrows, wrows), wrows)]
+    for group in (*gu_sums, go_sums, *qkv_sums, da1_sums):
         group.sent()
+    for copy in (*gu_x, *small_v_x, *small_z_x):
+        copy.wait_send()
     moves.finish()
-
-
-def backward(zs, n, norms, tables, a2_all, dgu, w_gu, w_out, qkv, probs, ob, hidden, dy_all):
+    for copy in gq_x:
+        copy.wait()
+    for i in range(3):
+        unpack_columns(
+            gq_out.at[:, i * width : (i + 1) * width], gq_rows, i * hc, HEAD_DIM, n, zs
+        )
+
+
+def backward(zs, n, norms, tables, *arrays):
     f32, b16 = jnp.float32, jnp.bfloat16
+    a1_all, a2_all, dgu, w_gu, w_qkv, w_out, qkv, probs, ob, hidden, dy_all, xs = arrays
     _, slots, rows, hc = ob.shape
     local, width = hidden.shape
     _, depth, gc = w_gu.shape
+    qc = 3 * hc
+    wrows = depth // n
     seq = n * rows
     wide = (n, local, width)
 
@@ -1269,42 +1568,54 @@
     return pl.pallas_call(
         functools.partial(backward_kernel, zs, n),
         out_shape=[
-            jax.ShapeDtypeStruct((depth, gc), b16),
             jax.ShapeDtypeStruct((hc // zs, width), f32),
             jax.ShapeDtypeStruct((local, width), f32),
-            jax.ShapeDtypeStruct((n, slots, rows, 3 * hc), b16),
-            jax.ShapeDtypeStruct((2, width), f32),
-            jax.ShapeDtypeStruct((1, 3 * hc), f32),
+            jax.ShapeDtypeStruct((wrows, n * qc), b16),
+            jax.ShapeDtypeStruct((wrows, n * gc // 2), b16),
+            jax.ShapeDtypeStruct((wrows, n * gc // 2), b16),
+            jax.ShapeDtypeStruct((8, 2 * HEAD_DIM), f32),
         ],
-        in_specs=[VMEM] * 2 + [HBM] * 9,
-        out_specs=[HBM] * 4 + [VMEM] * 2,
+        in_specs=[VMEM] * 2 + [HBM] * 12,
+        out_specs=[HBM] + [VMEM] * 5,
         scratch_shapes=[
-            *[buf(v) for v in (a2_all, dgu, w_gu, w_out, qkv, probs, ob, hidden)],
+            pltpu.VMEM(wide, b16),
+            buf(dgu),
+            pltpu.VMEM((zs, depth, max(gc, 2 * qc)), b16),
+            buf(w_out),
+            buf(qkv),
+            pltpu.VMEM(probs.shape[1:], b16),
+            buf(ob),
+            buf(hidden),
             pltpu.VMEM((local, width), b16),
             pltpu.VMEM((zs, depth, gc), b16),
             pltpu.VMEM((depth, gc), b16),
             pltpu.VMEM((3, depth, gc), b16),
-            pltpu.VMEM(wide, b16),
             pltpu.VMEM((n // 2, local, width), b16),
             pltpu.VMEM((n // 2 - 1, local, width), b16),
-            pltpu.VMEM((local, width), f32),
             pltpu.VMEM(wide, b16),
             pltpu.VMEM((zs, hc // zs, width), b16),
             pltpu.VMEM((hc // zs, width), b16),
             pltpu.VMEM((3, hc // zs, width), b16),
-            pltpu.VMEM((hc // zs, width), f32),
-            pltpu.VMEM(ob.shape, b16),
             pltpu.VMEM((3, seq, hc), f32),
-            pltpu.VMEM((n, slots, rows, 3 * hc), b16),
-            pltpu.SemaphoreType.DMA((48,)),
-            pltpu.SemaphoreType.DMA((48,)),
+            pltpu.VMEM((n, slots, rows, qc), b16),
+            pltpu.VMEM((1, qc), f32),
+            pltpu.VMEM((depth, qc), b16),
+            pltpu.VMEM((3, depth, qc), b16),
+            pltpu.VMEM((n, wrows, gc), b16),
+            pltpu.VMEM((n, wrows, qc), b16),
+            pltpu.VMEM((zs, n // 2, 8, 2 * HEAD_DIM), f32),
+            pltpu.VMEM((n, zs, 8, 2 * HEAD_DIM), f32),
+            pltpu.VMEM((zs, 8, 2 * HEAD_DIM), f32),
+            pltpu.VMEM((zs, 8, 2 * HEAD_DIM), f32),
+            pltpu.SemaphoreType.DMA((96,)),
+            pltpu.SemaphoreType.DMA((96,)),
             pltpu.SemaphoreType.DMA((24,)),
         ],
         compiler_params=pltpu.CompilerParams(
-            collective_id=4, has_side_effects=True, vmem_limit_bytes=62 << 20
+            collective_id=4, has_side_effects=True, vmem_limit_bytes=VMEM_LIMIT
         ),
         name="backward",
-    )(norms, tables, a2_all, dgu, w_gu, w_out, qkv, probs, ob, hidden, dy_all)
+    )(norms, tables, *arrays)
 
 
 def tensor_shards(
@@ -1331,12 +1642,8 @@
     seq = rows * n
     wrows = w_qkv.shape[0]
     ff_block = w_down.shape[0]
-    heads = HEADS // n
-    hc = heads * HEAD_DIM
+    hc = HEADS // n * HEAD_DIM
     ffc = ff_block * zs
-
-    def dot(a, b, dims):
-        return lax.dot_general(a, b, (dims, ((), ())), preferred_element_type=f32)
 
     def local_tokens(v):
         return jnp.transpose(v, (1, 0, 2)).reshape(local, width)
@@ -1344,30 +1651,18 @@
     def back_tokens(v):
         return jnp.transpose(v.reshape(slots, rows, width), (1, 0, 2))
 
-    def exchange(v):
-        return lax.all_to_all(v, "ctx", 0, 0, tiled=True)
-
-    def gather_ctx(v):
-        return lax.all_gather(v, "ctx", axis=0, tiled=True)
-
-    def scatter_ctx(v):
-        return lax.psum_scatter(v.astype(b16), "ctx", scatter_dimension=0, tiled=True).astype(f32)
-
-    def gather_dp(v):
-        return lax.all_gather(v, "dp", axis=0, tiled=True)
-
-    def scatter_dp(v):
-        return lax.psum_scatter(v.astype(b16), "dp", scatter_dimension=0, tiled=True)
-
     xs = local_tokens(inputs)
     dy = local_tokens(cotangent)
-    small = jnp.concatenate([b_qkv, gain_one, shift_one, gain_two, shift_two]).astype(f32)
-    small = jnp.pad(small, (0, 1024 - small.shape[0])).reshape(8, 128)
-    w_qkv_c, w_out_c, gu_own, a_all, dy_all, small = spread(
-        zs, n, w_qkv, w_gate, w_up, w_out, xs, dy, small
+    small, at = jnp.zeros(1024, f32), 0
+    for vector in (b_qkv, gain_one, shift_one, gain_two, shift_two):
+        size = vector.shape[0]
+        small = small + jnp.pad(vector.astype(f32), (at, 1024 - at - size))
+        at += size
+    small = small.reshape(8, 128)
+    w_qkv_c, w_out_c, gu_own, a_all, small = spread(
+        zs, n, w_qkv, w_gate, w_up, w_out, xs, small
     )
     small = small.reshape(zs * n, 1024)
-    dy_all = dy_all.reshape(tokens, width)
     nb = b_qkv.shape[0]
     bias_full = small[:, :nb].reshape(3, zs, n, HEAD_DIM)
     bias_own = lax.dynamic_index_in_dim(bias_full, me, 2, keepdims=False).reshape(1, 3 * hc)
@@ -1376,95 +1671,46 @@
     ]
 
 
-    counter = jnp.arange(ROTARY // 2, dtype=f32)
-    angles = jnp.arange(seq, dtype=f32)[:, None] * (10000.0 ** (-2.0 * counter / ROTARY))[None, :]
-    cos_t, sin_t = jnp.cos(angles), jnp.sin(angles)
-    zero = jnp.zeros_like(sin_t)
-    rest = jnp.ones((seq, HEAD_DIM - ROTARY), f32)
-    table_c = jnp.tile(jnp.concatenate([cos_t, cos_t, rest], -1), (1, heads))
-    table_l = jnp.tile(jnp.concatenate([-sin_t, zero, 0 * rest], -1), (1, heads))
-    table_r = jnp.tile(jnp.concatenate([zero, sin_t, 0 * rest], -1), (1, heads))
-
-    def by_slot(v):
-        return v.reshape(n, slots, rows, v.shape[-1]).transpose(1, 0, 2, 3).reshape(
-            slots, seq, v.shape[-1]
-        )
-
-    def by_device(v):
-        return v.reshape(slots, n, rows, v.shape[-1]).transpose(1, 0, 2, 3).reshape(
-            tokens, v.shape[-1]
-        )
-
-    def turn(v, sign):
-        half = ROTARY // 2
-        return (
-            v * table_c
-            + sign * jnp.roll(v, -half, -1) * table_l
-            + sign * jnp.roll(v, half, -1) * table_r
-        )
-
-    tables = jnp.stack([table_c, table_l, table_r]).reshape(3, n, rows, hc)
+    angles = np.arange(seq)[:, None] * 10000.0 ** (-2.0 * np.arange(ROTARY // 2) / ROTARY)[None, :]
+    cos_t, sin_t = np.cos(angles), np.sin(angles)
+    zero, rest = np.zeros_like(sin_t), np.zeros((seq, HEAD_DIM - ROTARY))
+    tables = np.stack(
+        [
+            np.concatenate(two, -1)
+            for two in (
+                2 * [cos_t, cos_t, rest + 1.0],
+                2 * [-sin_t, zero, rest],
+                2 * [zero, sin_t, rest],
+            )
+        ]
+    ).astype(np.float32)
+
+    tables = jnp.asarray(tables.reshape(3, n, rows, 2 * HEAD_DIM))
     norms = jnp.concatenate([g1, s1, g2, s2])
-    a1_all, qkv, probs, ob, hidden, a2_all, w_gu_c, gu, z = forward(
+    a1_all, qkv, probs, ob, hidden, a2_all, w_gu_c, gu, z, dy_all = forward(
         zs, n, slots, lengths, norms, bias_own, tables, a_all, w_qkv_c, w_out_c,
-        gu_own.reshape(n * wrows, 2 * ffc),
-    )
-    dgu, w_down_c, grad_down = middle(zs, n, z, gu, dy_all.reshape(n, local, width), w_down)
-    ggu, grad_out, dh, dj, gains_two, bias_part = backward(
-        zs, n, norms, tables, a2_all, dgu, w_gu_c, w_out_c, qkv, probs, ob, hidden,
-        dy_all.reshape(n, local, width),
-    )
-    grad_gu = exchange(ggu.reshape(n, wrows, 2 * ffc))
-    gain_two_part, shift_two_part = gains_two[0], gains_two[1]
-    bias_part = bias_part.reshape(3, zs, 1, HEAD_DIM)
-    w_qkv_c = w_qkv_c.reshape(width, 3 * hc)
-    a1_all = a1_all.reshape(tokens, width)
-    dj = dj.reshape(tokens, 3 * hc)
-    n1, r1 = layer_stats(xs.astype(f32))
-    z = z.reshape(tokens, ffc)
-    w_down_c = w_down_c.reshape(ffc, width)
-    result = hidden + scatter_ctx(dot(z, w_down_c, ((1,), (0,))))
-    grad_qkv = exchange(scatter_dp(dot(a1_all, dj, ((0,), (0,)))).reshape(n, wrows, 3 * hc))
-    da1 = scatter_ctx(dot(dj, w_qkv_c, ((1,), (1,))))
-    gain_one_part = jnp.sum(da1 * n1, 0)
-    shift_one_part = jnp.sum(da1, 0)
-    input_grad = dh + norm_back(da1, n1, r1, g1)
-
-    own = (jnp.arange(n) == me)[None, None, :, None]
-    devices = zs * n
-    pieces = jnp.concatenate(
-        [
-            jnp.where(own, bias_part, 0.0).reshape(devices, nb),
-            gain_one_part.reshape(devices, wrows),
-            shift_one_part.reshape(devices, wrows),
-            gain_two_part.reshape(devices, wrows),
-            shift_two_part.reshape(devices, wrows),
-        ],
-        -1,
-    )
-    summed = lax.psum_scatter(pieces, ("dp", "ctx"), scatter_dimension=0, tiled=True)[0]
-
-    def ff_back(part):
-        return jnp.transpose(part.reshape(n, wrows, zs, ff_block), (1, 2, 0, 3)).reshape(
-            wrows, zs * n * ff_block
-        ).astype(f32)
-
-    grad_qkv = jnp.transpose(grad_qkv.reshape(n, wrows, 3, zs, HEAD_DIM), (1, 2, 3, 0, 4)).reshape(
-        wrows, 3 * width
-    ).astype(f32)
+        gu_own.reshape(n * wrows, 2 * ffc), dy,
+    )
+    dgu, grad_down, result = middle(zs, n, z, gu, dy_all, w_down, hidden)
+    grad_out, input_grad, grad_qkv, grad_gate, grad_up, sums = backward(
+        zs, n, norms, tables, a1_all, a2_all, dgu, w_gu_c, w_qkv_c.reshape(zs, n * wrows, 3 * hc),
+        w_out_c, qkv, probs, ob, hidden, dy_all, xs,
+    )
+    mine = lax.dynamic_slice_in_dim(sums[:4], me % 2 * wrows, wrows, 1)
+    grad_bias = lax.dynamic_slice_in_dim(sums[4:7].reshape(2 * nb), me % 2 * nb, nb)
     return (
-        back_tokens(result.astype(b16)),
+        back_tokens(result),
         back_tokens(input_grad),
-        grad_qkv,
-        summed[:nb],
+        grad_qkv.astype(f32),
+        grad_bias,
         grad_out,
-        ff_back(grad_gu[..., :ffc]),
-        ff_back(grad_gu[..., ffc:]),
+        grad_gate.astype(f32),
+        grad_up.astype(f32),
         grad_down,
-        summed[nb : nb + wrows],
-        summed[nb + wrows : nb + 2 * wrows],
-        summed[nb + 2 * wrows : nb + 3 * wrows],
-        summed[nb + 3 * wrows :],
+        mine[0],
+        mine[1],
+        mine[2],
+        mine[3],
     )
 
 

time: 659 us -> 487 us (0.74)
  waiting for transfers between devices: 71.9 us -> 0 us
  blocking collectives: 38.8 us -> 0 us
  local copies, waits for them, and re-layouts: 55.7 us -> 22.1 us
  Pallas kernels: 426 us -> 449 us
  matrix products: 21.6 us -> 0 us
  between operations: 14.6 us -> 1.24 us
  starting transfers between devices: 9.42 us -> 0 us
    reduce_scatter x3 -> x0, waiting for transfers between devices: 58 us -> none  [the longest x2 50.5 us: scatter_ctx(): lax.psum_scatter(v.astype(b16), 'ctx', scatter_dimension=0, tiled=True)]
    pallas_call x1, Pallas kernels: 131 us -> 184 us  [backward(): pl.pallas_call(functools.partial(backward_kernel, zs, n), out_shape=[jax....]
    unnamed x1 -> x0, blocking collectives: 38.8 us -> none
    convert_element_type x9 -> x0, local copies, waits for them, and re-layouts: 29.1 us -> none  [the longest x6 17.8 us: ff_back(): return jnp.transpose(part.reshape(n, wrows, zs, ff_block), (1, 2, 0, 3))....]
    pallas_call x1, Pallas kernels: 97.8 us -> 73.7 us  [middle(): pl.pallas_call(functools.partial(middle_kernel, zs, n), out_shape=[jax.Sh...]
    dot_general x3 -> x0, matrix products: 21.6 us -> none  [dot(): return lax.dot_general(a, b, (dims, ((), ())), preferred_element_type=f32)]
    all_to_all x2 -> x0, waiting for transfers between devices: 13.9 us -> none  [exchange(): return lax.all_to_all(v, 'ctx', 0, 0, tiled=True)]
    all_to_all x2 -> x0, starting transfers between devices: 9.3 us -> none  [exchange(): return lax.all_to_all(v, 'ctx', 0, 0, tiled=True)]
  transfers between devices with their start and end apart: 5 -> 0, of which waited for: 3 -> 0; matrix products, arithmetic and copies ran while one was open for 7% -> 0% of each run, Pallas kernels for 20% -> 0%
where the time goes in v5:
time: 487 us; the launch traced here: 478 us
  Pallas kernels  449 us (92%)
  local copies, waits for them, and re-layouts  22.1 us (5%)
  other arithmetic  5.09 us (1%)
    pallas_call x1, Pallas kernels, backward(): pl.pallas_call(functools.partial(backward_kernel, zs, n), out_shape=[jax....  184 us
    pallas_call x1, Pallas kernels, forward(): pl.pallas_call(functools.partial(forward_kernel, zs, n), out_shape=[jax.S...  108 us
    pallas_call x1, Pallas kernels, spread(): pl.pallas_call(functools.partial(spread_kernel, zs, n), out_shape=[jax.Sh...  82.8 us
    pallas_call x1, Pallas kernels, middle(): pl.pallas_call(functools.partial(middle_kernel, zs, n), out_shape=[jax.Sh...  73.7 us
    unnamed x35, local copies, waits for them, and re-layouts  11.9 us

profile of v5, /device:TPU:1, one launch (start us, length us, event | category | flops | bytes accessed | tf_op | source)
XLA Modules:
  0.0 477.9 jit_solution(17111284400078539416)
XLA Ops:
  0.7 0.8 add_bitcast_fusion.small
  1.5 1.2 copy.26
  2.7 0.0 copy-start.1
  2.7 2.2 copy.28
  4.9 0.0 copy-start.5
  4.9 1.1 copy-done.5
  6.0 0.0 copy-start.6
  6.0 1.1 copy-done.6
  7.1 0.0 copy-start.7
  7.1 1.1 copy-done.7
  8.2 0.0 copy-start.8
  8.2 0.9 copy-done.8
  9.2 82.8 %spread.1 = (bf16[4,8,64,768]{3,2,1,0:T(8,128)(2,1)S(1)}, bf16[4,64,2048]{2,1,0:T(8,128)(2,1)S(1)}, bf16[8,64,1408]{2,1,0:T(8,128)(2,1)S(1)}, bf16[8,128,2048]{2,1,0:T(8,128)(2,1)S(1)}, f32[4,8,8,128]{3,2,1,0:T(8,128)S(1)}) custom-call(bf16[64,6144]{1,0:T(8,128)(2,1)S(1)} %copy-done.5, bf16[64,5632]{1,0:T(8,128)(2,1)S(1)} %copy-done.6, ...), custom_call_target="tpu_custom_call" | custom-call | tf_op jit(solution)/shard_map/spread/pallas_call | solution.py:548
  92.0 0.0 copy-start
  92.0 1.6 copy-done
  93.6 0.0 copy-start.2
  93.6 1.0 copy-done.2
  94.6 0.0 copy-start.3
  94.6 2.0 copy-done.3
  96.6 0.0 copy-start.4
  96.6 1.1 copy-done.4
  97.7 0.1 fusion
  97.8 0.1 reshape.73
  97.9 0.1 reshape.76
  98.0 0.1 reshape.75
  98.1 0.1 reshape.74
  98.1 0.7 pad_maximum_fusion.norms
  98.8 0.1 reshape.77
  98.9 0.7 reshape.78.bias
  99.5 108.5 %forward.1 = (bf16[8,128,2048]{2,1,0:T(8,128)(2,1)}, bf16[3,2,8,64,256]{4,3,2,1,0:T(8,128)(2,1)}, bf16[2,4,512,512]{3,2,1,0:T(8,128)(2,1)}, bf16[8,2,64,256]{3,2...) custom-call(s32[1,2]{1,0:T(1,128)} %lengths.1, ...), custom_call_target="tpu_custom_call" | custom-call | tf_op jit(solution)/shard_map/forward/pallas_call | solution.py:832
  208.0 0.0 copy-done.1
  208.0 73.7 %middle.1 = (bf16[4,256,1408]{2,1,0:T(8,128)(2,1)}, f32[176,2048]{1,0:T(8,128)}, bf16[128,2048]{1,0:T(8,128)(2,1)}) custom-call(bf16[4,256,704]{2,1,0:T(8,128)(2,1)} %get-tuple-element.41.zz, f32[4,256,1408]{2,1,0:T(8,128)} %get-tuple-element.42.gu, bf16[8,128,2048]{2,1,0:T(8,128)(2,1)} %get-tuple-element.43.dy_all, bf16[176,2048]{1,0:T(8,128)(2,1)} %w_down.1, ...), custom_call_target="tpu_custom_call" | custom-call | tf_op jit(solution)/shard_map/middle/pallas_call | solution.py:1160
  281.7 0.0 copy-start.14
  281.7 184.4 %backward.1 = (f32[64,2048]{1,0:T(8,128)}, f32[128,2048]{1,0:T(8,128)}, bf16[64,6144]{1,0:T(8,128)(2,1)}, bf16[64,5632]{1,0:T(8,128)(2,1)}, bf16[64,5632]{1,0:T(8,128)(2,1)}, /*index=5*/f32[8,128]{1,0:T(8,128)}) custom-call(f32[4,2048]{1,0:T(4,128)} %pad_maximum_fusion.norms, f32[3,8,64,128]{3,2,1,0:T(8,128)} %constant.38.clone.tables, ...), custom_call_target="tpu_custom_call" | custom-call | tf_op jit(solution)/shard_map/backward/pallas_call | solution.py:1568
  466.2 0.0 copy-start.15
  466.2 0.0 copy-start.12
  466.2 0.0 copy-start.11
  466.2 0.0 copy-done.14
  466.2 1.3 copy.37
  467.6 0.0 copy-start.10
  467.6 3.1 copy.36
  470.6 0.0 copy-done.15
  470.7 0.6 dynamic_slice.11
  471.3 0.1 constant_dynamic-slice_fusion
  471.4 0.5 slice_bitcast_fusion.1
  471.9 0.0 copy-done.12
  471.9 0.0 copy-start.13
  471.9 1.2 convert_element_type.17
  473.1 0.0 copy-done.11
  473.1 0.0 copy-start.9
  473.1 1.2 convert_element_type.26
  474.3 0.0 copy-done.10
  474.3 1.2 convert_element_type.16
  475.5 0.0 copy-done.13
  475.5 0.8 copy.41
  476.3 0.0 copy-done.9
  476.3 1.1 copy.42
  (5 shorter events, 0.0 us)
Async XLA Ops:
  2.7 205.4 %copy-start.1 = (bf16[2,64,2048]{2,1,0:T(8,128)(2,1)}, bf16[2,64,2048]{2,1,0:T(8,128)(2,1)S(1)}, u32[]{:S(2)}) copy-start(bf16[2,64,2048]{2,1,0:T(8,128)(2,1)S(1)} %copy.26) | copy-start | bytes 1572868
  4.9 1.1 copy-start.5
  6.0 1.1 copy-start.6
  7.1 1.1 copy-start.7
  8.2 0.9 copy-start.8
  92.0 1.6 copy-start
  93.6 1.0 copy-start.2
  94.6 2.0 copy-start.3
  96.6 1.1 copy-start.4
  281.7 184.5 %copy-start.14 = (bf16[128,2048]{1,0:T(8,128)(2,1)S(1)}, bf16[128,2048]{1,0:T(8,128)(2,1)}, u32[]{:S(2)}) copy-start(bf16[128,2048]{1,0:T(8,128)(2,1)} %get-tuple-element.45) | copy-start | bytes 1572868
  466.2 4.5 copy-start.15
  466.2 5.7 %copy-start.12 = (bf16[64,5632]{1,0:T(8,128)(2,1)S(1)}, bf16[64,5632]{1,0:T(8,128)(2,1)}, u32[]{:S(2)}) copy-start(bf16[64,5632]{1,0:T(8,128)(2,1)} %get-tuple-element.57) | copy-start | bytes 2162692
  466.2 6.9 %copy-start.11 = (bf16[64,5632]{1,0:T(8,128)(2,1)S(1)}, bf16[64,5632]{1,0:T(8,128)(2,1)}, u32[]{:S(2)}) copy-start(bf16[64,5632]{1,0:T(8,128)(2,1)} %get-tuple-element.58) | copy-start | bytes 2162692
  467.6 6.7 %copy-start.10 = (bf16[64,6144]{1,0:T(8,128)(2,1)S(1)}, bf16[64,6144]{1,0:T(8,128)(2,1)}, u32[]{:S(2)}) copy-start(bf16[64,6144]{1,0:T(8,128)(2,1)} %get-tuple-element.54) | copy-start | bytes 2359300
  471.9 3.6 copy-start.13
  473.1 3.2 copy-start.9

commit v6 on v5

--- a/solution.py
+++ b/solution.py
@@ -413,13 +413,11 @@
 
 
 class LayerGather:
-    def __init__(self, wires, buf, source=None):
+    def __init__(self, wires, block, source=None):
         c = wires.c
-        mine = buf.at[c] if source is None else source
-        self.direct = {m: wires.put(mine, buf.at[c], 0, m) for m in (2, 4, 6, 1)}
-        self.on = {
-            m: wires.put(buf.at[flip(c, m)], buf.at[flip(c, m)], 0, 1) for m in (2, 4, 6)
-        }
+        mine = block(c) if source is None else source
+        self.direct = {m: wires.put(mine, block(c), 0, m) for m in (2, 4, 6, 1)}
+        self.on = {m: wires.put(block(flip(c, m)), block(flip(c, m)), 0, 1) for m in (2, 4, 6)}
 
     def start(self):
         for m in (2, 4, 6, 1):
@@ -445,141 +443,14 @@
         dst[i] = jnp.concatenate(pieces, -1)
 
 
-def spread_kernel(
-    zs,
-    n,
-    w_qkv,
-    w_gate,
-    w_up,
-    w_out,
-    xs,
-    small,
-    qkv_all,
-    out_all,
-    gu_own,
-    xs_all,
-    small_all,
-    qkv_send,
-    gu_send,
-    send,
-    recv,
-    local,
-):
-    wires = Wires(send, recv)
-    z, c = wires.z, wires.c
-    hc = HEAD_DIM * HEADS // n
-    width = HEADS * HEAD_DIM
-    ff_block = w_gate.shape[1] // (zs * n)
-
-    own = [
-        pltpu.make_async_copy(w_out, out_all.at[z], local.at[0]),
-        pltpu.make_async_copy(qkv_send.at[c], qkv_all.at[z, c], local.at[1]),
-        pltpu.make_async_copy(gu_send.at[c], gu_own.at[c], local.at[2]),
-        pltpu.make_async_copy(xs, xs_all.at[c], local.at[3]),
-        pltpu.make_async_copy(small, small_all.at[z, c], local.at[4]),
-    ]
-    for i in (0, 3, 4):
-        own[i].start()
-    pack_columns(
-        qkv_send, [(w_qkv.at[:, i * width : (i + 1) * width], HEAD_DIM) for i in range(3)], n, zs
-    )
-    own[1].start()
-    wires.greet(zs, n)
-    for i in (0, 4):
-        own[i].wait()
-
-    out_z = DepthGather(wires, lambda i: out_all.at[i])
-    DepthGather.start([out_z])
-    qkv_x = [
-        wires.put(qkv_send.at[flip(c, m)], qkv_all.at[z, c], 0, m) for m in range(1, n)
-    ]
-    for copy in qkv_x:
-        copy.start()
-    small_z = [wires.put(small_all.at[z, c], small_all.at[z, c], m, 0) for m in range(1, zs)]
-    for copy in small_z:
-        copy.start()
-    xs_g = LayerGather(wires, xs_all, xs)
-    xs_g.start()
-    pack_columns(gu_send, [(w_gate, ff_block), (w_up, ff_block)], n, zs)
-    own[2].start()
-    for copy in small_z:
-        copy.wait_recv()
-    small_x = [
-        wires.put(small_all.at[:, c], small_all.at[:, c], 0, m) for m in range(1, n)
-    ]
-    for copy in small_x:
-        copy.start()
-    own[1].wait()
-    for copy in qkv_x:
-        copy.wait_recv()
-    qkv_z = [
-        DepthGather(wires, lambda i, a=a, s=s: qkv_all.at[i, a : a + s])
-        for a, s in pieces_of(n, 4, 1)
-    ]
-    DepthGather.start(qkv_z)
-    out_z.forward()
-    gu_x = [wires.put(gu_send.at[flip(c, m)], gu_own.at[c], 0, m) for m in range(1, n)]
-    for copy in gu_x:
-        copy.start()
-    for m in (2, 4, 6):
-        xs_g.forward(m)
-    for part in qkv_z:
-        part.forward()
-
-    for i in (2, 3):
-        own[i].wait()
-    for m in (1, 3, 5, 7):
-        xs_g.arrived(m)
-    xs_g.sent()
-    for copy in small_z:
-        copy.wait_send()
-    for copy in qkv_x:
-        copy.wait_send()
-    for copy in (*small_x, *gu_x):
-        copy.wait()
-    for part in (out_z, *qkv_z):
-        part.finish()
-
-
-def spread(zs, n, w_qkv, w_gate, w_up, w_out, xs, small):
-    wrows, width = w_out.shape
-    qc, gc = w_qkv.shape[1] // n, 2 * w_gate.shape[1] // n
-    b16 = jnp.bfloat16
-    return pl.pallas_call(
-        functools.partial(spread_kernel, zs, n),
-        out_shape=[
-            jax.ShapeDtypeStruct((zs, n, wrows, qc), b16),
-            jax.ShapeDtypeStruct((zs, wrows, width), b16),
-            jax.ShapeDtypeStruct((n, wrows, gc), b16),
-            jax.ShapeDtypeStruct((n, *xs.shape), b16),
-            jax.ShapeDtypeStruct((zs, n, *small.shape), small.dtype),
-        ],
-        in_specs=[VMEM, VMEM, VMEM, HBM, HBM, HBM],
-        out_specs=[HBM] * 5,
-        scratch_shapes=[
-            pltpu.VMEM((n, wrows, qc), b16),
-            pltpu.VMEM((n, wrows, gc), b16),
-            pltpu.SemaphoreType.DMA((64,)),
-            pltpu.SemaphoreType.DMA((64,)),
-            pltpu.SemaphoreType.DMA((5,)),
-        ],
-        compiler_params=pltpu.CompilerParams(
-            collective_id=1, has_side_effects=True, vmem_limit_bytes=32 << 20
-        ),
-        name="spread",
-    )(w_qkv, w_gate, w_up, w_out, xs, small)
-
-
 class LayerScatter:
     def __init__(self, wires, part, near, far):
         c = wires.c
         self.c, self.part, self.near, self.far = c, part, near, far
         self.pair = {
-            m: wires.put(part.at[flip(c, m + 1)], near.at[m // 2], 0, 1) for m in (6, 4, 2, 0)
+            m: wires.put(part(flip(c, m + 1)), near(m // 2), 0, 1) for m in (6, 4, 2, 0)
         }
-        self.chips = {
-            m: wires.put(part.at[flip(c, m)], far.at[m // 2 - 1], 0, m) for m in (6, 4, 2)
-        }
+        self.chips = {m: wires.put(part(flip(c, m)), far(m // 2 - 1), 0, m) for m in (6, 4, 2)}
 
     def start(self):
         for copy in self.pair.values():
@@ -587,18 +458,19 @@
 
     def step(self, m):
         self.pair[m].wait_recv()
-        to = flip(self.c, m)
-        self.part[to] = (
-            self.part[to].astype(jnp.float32) + self.near[m // 2].astype(jnp.float32)
-        ).astype(self.part.dtype)
+        to = self.part(flip(self.c, m))
+        to[...] = (
+            to[...].astype(jnp.float32) + self.near(m // 2)[...].astype(jnp.float32)
+        ).astype(to.dtype)
         self.chips[m].start()
 
     def total(self):
         self.pair[0].wait_recv()
-        result = self.part[self.c].astype(jnp.float32) + self.near[0].astype(jnp.float32)
+        result = self.part(self.c)[...].astype(jnp.float32)
+        result = result + self.near(0)[...].astype(jnp.float32)
         for m in (2, 4, 6):
             self.chips[m].wait_recv()
-            result = result + self.far[m // 2 - 1].astype(jnp.float32)
+            result = result + self.far(m // 2 - 1)[...].astype(jnp.float32)
         return result
 
     def sent(self):
@@ -625,92 +497,345 @@
     return lax.broadcasted_iota(jnp.int32, (rows, columns), 1) // HEAD_DIM == head
 
 
-def forward_kernel(
+class DepthScatter:
+    def __init__(self, wires, part, relay, boxes):
+        z = wires.z
+        self.wires, self.part, self.relay_box, self.boxes = wires, part, relay, boxes
+        self.far = wires.put(part(flip(z, 3)), relay, 1, 0)
+        self.skip = wires.put(part(flip(z, 2)), boxes[1], 2, 0)
+        self.near = wires.put(part(flip(z, 1)), boxes[0], 1, 0)
+        self.mid = wires.put(part(flip(z, 3)), boxes[2], 3, 0)
+
+    def start(self, mask):
+        outer, inner = pl.when(self.wires.outer), pl.when(self.wires.inner)
+        if mask == 3:
+            outer(self.far.start)
+            inner(self.mid.start)
+        elif mask == 2:
+            outer(self.skip.start)
+        elif mask == 1:
+            self.near.start()
+        else:
+
+            @outer
+            def _():
+                self.boxes[2][...] = jnp.zeros_like(self.boxes[2])
+
+    def relay(self):
+        @pl.when(self.wires.inner)
+        def _():
+            self.far.wait_recv()
+            to = self.part(flip(self.wires.z, 2))
+            to[...] = (
+                to[...].astype(jnp.float32) + self.relay_box[...].astype(jnp.float32)
+            ).astype(to.dtype)
+            self.skip.start()
+
+    def total(self):
+        self.near.wait_recv()
+        self.skip.wait_recv()
+        pl.when(self.wires.inner)(self.mid.wait_recv)
+        result = self.part(self.wires.z)[...].astype(jnp.float32)
+        for box in self.boxes:
+            result = result + box[...].astype(jnp.float32)
+        return result
+
+    def sent(self):
+        self.near.wait_send()
+        self.skip.wait_send()
+        pl.when(self.wires.outer)(self.far.wait_send)
+        pl.when(self.wires.inner)(self.mid.wait_send)
+
+
+class Moves:
+    def __init__(self, sems):
+        self.sems, self.number, self.stores = sems, itertools.count(), []
+
+    def load(self, src, dst):
+        copy = pltpu.make_async_copy(src, dst, self.sems.at[next(self.number)])
+        copy.start()
+        return copy
+
+    def store(self, src, dst):
+        self.stores.append(self.load(src, dst))
+
+    def finish(self):
+        for copy in self.stores:
+            copy.wait()
+
+
+def pieces_of(total, number, unit):
+    units = total // unit
+    cuts = [units * i // number * unit for i in range(number + 1)]
+    return [(a, b - a) for a, b in zip(cuts[:-1], cuts[1:])]
+
+
+class ChainGather:
+    def __init__(self, wires, part):
+        self.z = z = wires.z
+        self.right = [
+            wires.put_to(part((z - s + 4) % 4), part((z - s + 4) % 4), (z + 1) % 4, wires.c)
+            for s in range(3)
+        ]
+        self.left = [
+            wires.put_to(part((z + s) % 4), part((z + s) % 4), (z + 3) % 4, wires.c)
+            for s in range(3)
+        ]
+
+    def start(self):
+        pl.when(self.z <= 2)(self.right[0].start)
+        pl.when(self.z >= 1)(self.left[0].start)
+
+    def hop(self, s):
+        pl.when(self.z >= s)(self.right[s - 1].wait_recv)
+        pl.when((self.z >= s) & (self.z <= 2))(self.right[s].start)
+        pl.when(self.z <= 3 - s)(self.left[s - 1].wait_recv)
+        pl.when((self.z <= 3 - s) & (self.z >= 1))(self.left[s].start)
+
+    def finish(self):
+        pl.when(self.z >= 3)(self.right[2].wait_recv)
+        pl.when(self.z <= 0)(self.left[2].wait_recv)
+        for s in range(3):
+            pl.when((self.z >= s) & (self.z <= 2))(self.right[s].wait_send)
+            pl.when((self.z <= 3 - s) & (self.z >= 1))(self.left[s].wait_send)
+
+
+class ChainScatter:
+    def __init__(self, wires, part, right, left):
+        self.z = z = wires.z
+        self.part, self.right_box, self.left_box = part, right, left
+        self.right = {
+            j: wires.put_to(part(j), right(j), (z + 1) % 4, wires.c) for j in (3, 2, 1)
+        }
+        self.left = {j: wires.put_to(part(j), left(j), (z + 3) % 4, wires.c) for j in (0, 1, 2)}
+
+    def clear(self):
+        @pl.when(self.z == 0)
+        def _():
+            self.right_box(0)[...] = jnp.zeros_like(self.right_box(0))
+
+        @pl.when(self.z == 3)
+        def _():
+            self.left_box(3)[...] = jnp.zeros_like(self.left_box(3))
+
+    def start(self, distance):
+        pl.when(self.z == 0)(self.right[distance].start)
+        pl.when(self.z == 3)(self.left[3 - distance].start)
+
+    def pass_on(self, copy, j, box):
+        copy.wait_recv()
+        to = self.part(j)
+        to[...] = (to[...].astype(jnp.float32) + box(j)[...].astype(jnp.float32)).astype(to.dtype)
+        copy.start()
+
+    def hop(self, s, distance):
+        @pl.when(self.z == s)
+        def _():
+            self.pass_on(self.right[distance], distance, self.right_box)
+
+        @pl.when(self.z == 3 - s)
+        def _():
+            self.pass_on(self.left[3 - distance], 3 - distance, self.left_box)
+
+    def total(self):
+        for j in (1, 2, 3):
+            pl.when(self.z == j)(self.right[j].wait_recv)
+        for j in (0, 1, 2):
+            pl.when(self.z == j)(self.left[j].wait_recv)
+        z = self.z
+        return (
+            self.part(z)[...].astype(jnp.float32)
+            + self.right_box(z)[...].astype(jnp.float32)
+            + self.left_box(z)[...].astype(jnp.float32)
+        )
+
+    def sent(self):
+        for j in (1, 2, 3):
+            pl.when(self.z < j)(self.right[j].wait_send)
+        for j in (0, 1, 2):
+            pl.when(self.z > j)(self.left[j].wait_send)
+
+
+def front_kernel(
     zs,
     n,
+    slots,
     lengths,
-    norms,
-    bias,
     tables,
-    xs_all,
+    small,
     w_qkv,
+    w_gate,
+    w_up,
     w_out,
-    gu_own,
+    w_down,
+    xs,
     dy,
+    w_qkv_out,
+    w_out_out,
+    w_gu_out,
     a1_out,
     qkv_out,
     probs_out,
     ob_out,
     hidden_out,
     a2_out,
-    w_gu_out,
-    gu_out,
-    zz_out,
-    dy_all,
-    xs_v,
-    a1_v,
+    dgu_out,
+    grad_down_out,
+    result_out,
+    norms,
+    qkv_send,
+    gu_send,
+    small_v,
+    bias_v,
     w_qkv_v,
     w_out_v,
+    w_gu_v,
+    w_down_v,
+    wide_x,
+    wide_a,
+    dy_v,
     qkv_v,
     probs_v,
     ob_v,
-    part,
     near,
     far,
     hidden_v,
-    a2_v,
-    w_gu_v,
     gu_v,
     zz_v,
+    dz_v,
+    right_v,
+    left_v,
+    total_v,
     send,
     recv,
     local,
-    drain,
 ):
     f32, b16 = jnp.float32, jnp.bfloat16
     wires = Wires(send, recv)
+    moves = Moves(local)
     z, c = wires.z, wires.c
-    _, slots, rows, hc = ob_v.shape
-    tokens, width = n * slots * rows, a1_v.shape[-1]
-    seq = n * rows
+    local_rows, width = xs.shape
+    rows = local_rows // slots
+    tokens, seq = n * local_rows, n * rows
+    pair = 2 * local_rows
+    hc = qkv_v.shape[-1]
     heads = hc // HEAD_DIM
-    ffc = zz_v.shape[-1]
-    chunks = 4
-    chunk = w_gu_v.shape[1] // chunks
-
-    loads = [
-        pltpu.make_async_copy(gu_own, w_gu_v.at[z], local.at[0]),
-        pltpu.make_async_copy(xs_all, xs_v, local.at[1]),
-        pltpu.make_async_copy(w_qkv, w_qkv_v, local.at[2]),
-        pltpu.make_async_copy(w_out, w_out_v, local.at[3]),
+    block = w_down_v.shape[1]
+    ffc = zs * block
+    lanes = 2 * HEAD_DIM
+    lane_half = lax.broadcasted_iota(jnp.int32, (1, lanes), 1) // HEAD_DIM
+
+    def block_of(ref, i):
+        return ref.at[pl.ds(pl.multiple_of(i * local_rows, local_rows), local_rows)]
+
+    def pair_at(i):
+        return pl.ds(pl.multiple_of(i * pair, pair), pair)
+
+    wait_out = moves.load(w_out, w_out_v.at[z])
+    wait_small = moves.load(small, small_v.at[z, c])
+    wait_xs = moves.load(xs, block_of(wide_x, c))
+    wait_dy = moves.load(dy, dy_v.at[c])
+    wait_down = moves.load(w_down, w_down_v.at[z])
+    pack_columns(
+        qkv_send, [(w_qkv.at[:, i * width : (i + 1) * width], HEAD_DIM) for i in range(3)], n, zs
+    )
+    wait_own_qkv = moves.load(qkv_send.at[c], w_qkv_v.at[z, c])
+    wires.greet(zs, n)
+    wait_out.wait()
+    wait_small.wait()
+    out_z = DepthGather(wires, lambda i: w_out_v.at[i])
+    DepthGather.start([out_z])
+    qkv_x = [wires.put(qkv_send.at[flip(c, m)], w_qkv_v.at[z, c], 0, m) for m in range(1, n)]
+    for copy in qkv_x:
+        copy.start()
+    small_z = [wires.put(small_v.at[z, c], small_v.at[z, c], m, 0) for m in range(1, zs)]
+    for copy in small_z:
+        copy.start()
+    xs_g = LayerGather(wires, lambda i: block_of(wide_x, i), xs)
+    xs_g.start()
+    pack_columns(gu_send, [(w_gate, block), (w_up, block)], n, zs)
+    wait_own_gu = moves.load(gu_send.at[c], w_gu_v.at[z, c])
+    for copy in small_z:
+        copy.wait_recv()
+    small_x = [wires.put(small_v.at[:, c], small_v.at[:, c], 0, m) for m in range(1, n)]
+    for copy in small_x:
+        copy.start()
+    wait_own_qkv.wait()
+    for copy in qkv_x:
+        copy.wait_recv()
+    number = 4
+    qkv_z = [
+        DepthGather(wires, lambda i, a=a, s=s: w_qkv_v.at[i, a : a + s])
+        for a, s in pieces_of(n, number, 1)
     ]
-    for copy in loads:
+    DepthGather.start(qkv_z)
+    gu_x = [wires.put(gu_send.at[flip(c, m)], w_gu_v.at[z, c], 0, m) for m in range(1, n)]
+    for copy in gu_x:
         copy.start()
-    wires.greet(zs, n)
-    loads[0].wait()
+    out_z.forward()
+    for m in (2, 4, 6):
+        xs_g.forward(m)
+
+    for copy in small_x:
+        copy.wait()
+    for r in range(4):
+        norms[r : r + 1] = jnp.concatenate(
+            [
+                jnp.where(
+                    lane_half == 0,
+                    small_v[d // n, d % n, r : r + 1],
+                    small_v[d // n, d % n + 1, r : r + 1],
+                )
+                for d in range(0, zs * n, 2)
+            ],
+            -1,
+        )
+    norms[4:8] = jnp.zeros_like(norms[4:8])
+    per_owner = 3 * zs * n // (zs * n)
+    for i in range(3):
+        for j in range(0, zs, 2):
+            both = []
+            for h in range(2):
+                group = i * zs * n + (j + h) * n + c
+                owner, k = group // per_owner, group % per_owner
+                tile = small_v[owner // n, owner % n]
+                row = jnp.where(k == 2, tile[5:6], tile[4:5])
+                both.append(jnp.where(k % 2 == h, row, pltpu.roll(row, HEAD_DIM, 1)))
+            at = (i * zs + j) * HEAD_DIM
+            bias_v[:, at : at + lanes] = jnp.where(lane_half == 0, both[0], both[1])
+
+    for m in (1, 3, 5, 7):
+        xs_g.arrived(m)
+    wait_xs.wait()
+    hidden_v[...] = block_of(wide_x, c)[...].astype(f32)
+
+    def norm_one(i, carry):
+        x = wide_x[pair_at(i)].astype(f32)
+        wide_a[pair_at(i)] = (layer_stats(x)[0] * norms[0:1] + norms[1:2]).astype(b16)
+        return carry
+
+    lax.fori_loop(0, n // 2, norm_one, 0)
+    wait_a1 = moves.load(wide_a, a1_out)
+    wait_own_gu.wait()
+    for copy in gu_x:
+        copy.wait_recv()
     gu_z = [
-        DepthGather(wires, lambda i, p=p: w_gu_v.at[i, p * chunk : (p + 1) * chunk])
-        for p in range(chunks)
+        DepthGather(wires, lambda i, a=a, s=s: w_gu_v.at[i, a : a + s])
+        for a, s in pieces_of(n, number, 1)
     ]
+    for part in qkv_z:
+        part.forward()
     DepthGather.start(gu_z)
-    dy_g = LayerGather(wires, dy_all, dy)
+    wait_dy.wait()
+    dy_g = LayerGather(wires, lambda i: dy_v.at[i])
     dy_g.start()
-    stores = []
-
-    def store(src, dst):
-        copy = pltpu.make_async_copy(src, dst, drain.at[len(stores)])
-        copy.start()
-        stores.append(copy)
-
-    store(dy, dy_all.at[c])
-    for copy in loads[1:]:
-        copy.wait()
+    for part in (out_z, *qkv_z):
+        part.finish()
+    moves.store(w_qkv_v, w_qkv_out)
+    moves.store(w_out_v, w_out_out)
 
     def project(i, carry):
-        x = xs_v[pl.ds(2 * i, 2)].reshape(2 * slots * rows, width).astype(f32)
-        a1 = (layer_stats(x)[0] * norms[0:1] + norms[1:2]).astype(b16)
-        a1_v[pl.ds(2 * i, 2)] = a1.reshape(2, slots * rows, width)
-        joined = dot(a1, w_qkv_v[...].reshape(width, 3 * hc)) + bias[...]
+        joined = dot(wide_a[pair_at(i)], w_qkv_v[...].reshape(width, 3 * hc)) + bias_v[...]
         for j in range(2):
             table = [tables[k, 2 * i + j] for k in range(3)]
             for s in range(slots):
@@ -722,14 +847,17 @@
         return carry
 
     lax.fori_loop(0, n // 2, project, 0)
-    store(a1_v, a1_out)
-    store(qkv_v, qkv_out)
+    moves.store(qkv_v, qkv_out)
+    for m in (2, 4, 6):
+        dy_g.forward(m)
 
     half = seq // 2
+    probs_sem = moves.sems.at[next(moves.number)]
 
     def attend(s, carry):
         q, k, v = [qkv_v[i, s].reshape(seq, hc) for i in range(3)]
         length = lengths[0, s]
+        kept = pltpu.make_async_copy(probs_v, probs_out.at[s], probs_sem)
         for part_q in range(2):
             keys = (part_q + 1) * half
             at = part_q * half
@@ -746,371 +874,117 @@
                 weights = jnp.where(allowed, jnp.exp(scores - peak), 0.0)
                 total = jnp.maximum(jnp.sum(weights, -1, keepdims=True), 1.0)
                 probs = (weights * (1.0 / total)).astype(b16)
-                probs_v[s, h, at : at + half, 0:keys] = probs
+                probs_v[h, at : at + half, 0:keys] = probs
+                if keys < seq:
+                    probs_v[h, at : at + half, keys:seq] = jnp.zeros((half, seq - keys), b16)
                 out = jnp.where(mask, dot(probs, v[:keys]), out)
             ob_v[part_q * n // 2 : (part_q + 1) * n // 2, s] = out.astype(b16).reshape(
                 n // 2, rows, hc
             )
+        kept.start()
+        kept.wait()
         return carry
 
     lax.fori_loop(0, slots, attend, 0)
-    for m in (2, 4, 6):
-        dy_g.forward(m)
-    store(probs_v, probs_out)
-    store(ob_v, ob_out)
+    moves.store(ob_v, ob_out)
+    gu_z[0].forward()
+
+    xs_g.sent()
 
     def to_hidden(i, carry):
-        part[i] = dot(
-            ob_v[i].reshape(slots * rows, hc), w_out_v[...].reshape(hc, width)
+        block_of(wide_x, i)[...] = dot(
+            ob_v[i].reshape(local_rows, hc), w_out_v[...].reshape(hc, width)
         ).astype(b16)
         return carry
 
     lax.fori_loop(0, n, to_hidden, 0)
-    sums = LayerScatter(wires, part, near, far)
+    wait_a1.wait()
+    sums = LayerScatter(
+        wires, lambda i: block_of(wide_x, i), lambda j: near.at[j], lambda j: far.at[j]
+    )
     sums.start()
     for m in (6, 4, 2):
         sums.step(m)
-    gu_z[0].forward()
-    hidden = xs_v[c].astype(f32) + sums.total()
+    gu_z[1].forward()
+    hidden = hidden_v[...] + sums.total()
     hidden_v[...] = hidden
-    store(hidden_v, hidden_out)
-    a2_v[c] = (layer_stats(hidden)[0] * norms[2:3] + norms[3:4]).astype(b16)
-    a2_g = LayerGather(wires, a2_v)
+    moves.store(hidden_v, hidden_out)
+    block_of(wide_a, c)[...] = (layer_stats(hidden)[0] * norms[2:3] + norms[3:4]).astype(b16)
+    a2_g = LayerGather(wires, lambda i: block_of(wide_a, i))
     a2_g.start()
-    gu_z[1].forward()
+    gu_z[2].forward()
     for m in (2, 4, 6):
         a2_g.forward(m)
-    gu_z[2].forward()
-    for m in (1, 3, 5, 7):
-        a2_g.arrived(m)
     gu_z[3].forward()
-    store(a2_v, a2_out)
-    for part_z in gu_z:
-        part_z.finish()
-    store(w_gu_v, w_gu_out)
-
-    def feed(i, carry):
-        a2 = a2_v[pl.ds(2 * i, 2)].reshape(2 * slots * rows, width)
-        gu = dot(a2, w_gu_v[...].reshape(width, 2 * ffc))
-        gu_v[i] = gu
-        gate = gu[:, :ffc]
-        zz_v[i] = (gate * jax.nn.sigmoid(gate) * gu[:, ffc:]).astype(b16)
-        return carry
-
-    lax.fori_loop(0, n // 2, feed, 0)
-    store(gu_v, gu_out)
-    store(zz_v, zz_out)
-    sums.sent()
-    a2_g.sent()
-    for m in (1, 3, 5, 7):
-        dy_g.arrived(m)
-    dy_g.sent()
-    for copy in stores:
-        copy.wait()
-
-
-def forward(zs, n, slots, lengths, norms, bias, tables, xs_all, w_qkv, w_out, gu_own, dy):
-    _, local, width = xs_all.shape
-    rows = local // slots
-    seq = rows * n
-    heads = HEADS // n
-    hc = heads * HEAD_DIM
-    gc = gu_own.shape[-1]
-    f32, b16 = jnp.float32, jnp.bfloat16
-    kept = [
-        ((n, local, width), b16),
-        ((3, slots, n, rows, hc), b16),
-        ((slots, heads, seq, seq), b16),
-        ((n, slots, rows, hc), b16),
-        ((local, width), f32),
-        ((n, local, width), b16),
-        ((zs, *gu_own.shape), b16),
-        ((n // 2, 2 * local, gc), f32),
-        ((n // 2, 2 * local, gc // 2), b16),
-    ]
-    a1, qkv, probs, ob, hidden, a2, w_gu, gu, zz = [pltpu.VMEM(*k) for k in kept]
-    return pl.pallas_call(
-        functools.partial(forward_kernel, zs, n),
-        out_shape=[jax.ShapeDtypeStruct(*k) for k in (*kept, ((n, local, width), b16))],
-        in_specs=[pl.BlockSpec(memory_space=pltpu.SMEM)] + [VMEM] * 3 + [HBM] * 5,
-        out_specs=[HBM] * (len(kept) + 1),
-        scratch_shapes=[
-            pltpu.VMEM(xs_all.shape, b16),
-            a1,
-            pltpu.VMEM(w_qkv.shape, b16),
-            pltpu.VMEM(w_out.shape, b16),
-            qkv,
-            probs,
-            ob,
-            pltpu.VMEM((n, local, width), b16),
-            pltpu.VMEM((n // 2, local, width), b16),
-            pltpu.VMEM((n // 2 - 1, local, width), b16),
-            hidden,
-            a2,
-            w_gu,
-            gu,
-            zz,
-            pltpu.SemaphoreType.DMA((40,)),
-            pltpu.SemaphoreType.DMA((40,)),
-            pltpu.SemaphoreType.DMA((4,)),
-            pltpu.SemaphoreType.DMA((len(kept) + 1,)),
-        ],
-        compiler_params=pltpu.CompilerParams(
-            collective_id=2, has_side_effects=True, vmem_limit_bytes=60 << 20
-        ),
-        name="forward",
-    )(lengths, norms, bias, tables, xs_all, w_qkv, w_out, gu_own, dy)
-
-
-class DepthScatter:
-    def __init__(self, wires, part, relay, boxes):
-        z = wires.z
-        self.wires, self.part, self.relay_box, self.boxes = wires, part, relay, boxes
-        self.far = wires.put(part(flip(z, 3)), relay, 1, 0)
-        self.skip = wires.put(part(flip(z, 2)), boxes[1], 2, 0)
-        self.near = wires.put(part(flip(z, 1)), boxes[0], 1, 0)
-        self.mid = wires.put(part(flip(z, 3)), boxes[2], 3, 0)
-
-    def start(self, mask):
-        outer, inner = pl.when(self.wires.outer), pl.when(self.wires.inner)
-        if mask == 3:
-            outer(self.far.start)
-            inner(self.mid.start)
-        elif mask == 2:
-            outer(self.skip.start)
-        elif mask == 1:
-            self.near.start()
-        else:
-
-            @outer
-            def _():
-                self.boxes[2][...] = jnp.zeros_like(self.boxes[2])
-
-    def relay(self):
-        @pl.when(self.wires.inner)
-        def _():
-            self.far.wait_recv()
-            to = self.part(flip(self.wires.z, 2))
-            to[...] = (
-                to[...].astype(jnp.float32) + self.relay_box[...].astype(jnp.float32)
-            ).astype(to.dtype)
-            self.skip.start()
-
-    def total(self):
-        self.near.wait_recv()
-        self.skip.wait_recv()
-        pl.when(self.wires.inner)(self.mid.wait_recv)
-        result = self.part(self.wires.z)[...].astype(jnp.float32)
-        for box in self.boxes:
-            result = result + box[...].astype(jnp.float32)
-        return result
-
-    def sent(self):
-        self.near.wait_send()
-        self.skip.wait_send()
-        pl.when(self.wires.outer)(self.far.wait_send)
-        pl.when(self.wires.inner)(self.mid.wait_send)
-
-
-class Moves:
-    def __init__(self, sems):
-        self.sems, self.number, self.stores = sems, itertools.count(), []
-
-    def load(self, src, dst):
-        copy = pltpu.make_async_copy(src, dst, self.sems.at[next(self.number)])
-        copy.start()
-        return copy
-
-    def store(self, src, dst):
-        self.stores.append(self.load(src, dst))
-
-    def finish(self):
-        for copy in self.stores:
-            copy.wait()
-
-
-def pieces_of(total, number, unit):
-    units = total // unit
-    cuts = [units * i // number * unit for i in range(number + 1)]
-    return [(a, b - a) for a, b in zip(cuts[:-1], cuts[1:])]
-
-
-class ChainGather:
-    def __init__(self, wires, part):
-        self.z = z = wires.z
-        self.right = [
-            wires.put_to(part((z - s + 4) % 4), part((z - s + 4) % 4), (z + 1) % 4, wires.c)
-            for s in range(3)
-        ]
-        self.left = [
-            wires.put_to(part((z + s) % 4), part((z + s) % 4), (z + 3) % 4, wires.c)
-            for s in range(3)
-        ]
-
-    def start(self):
-        pl.when(self.z <= 2)(self.right[0].start)
-        pl.when(self.z >= 1)(self.left[0].start)
-
-    def hop(self, s):
-        pl.when(self.z >= s)(self.right[s - 1].wait_recv)
-        pl.when((self.z >= s) & (self.z <= 2))(self.right[s].start)
-        pl.when(self.z <= 3 - s)(self.left[s - 1].wait_recv)
-        pl.when((self.z <= 3 - s) & (self.z >= 1))(self.left[s].start)
-
-    def finish(self):
-        pl.when(self.z >= 3)(self.right[2].wait_recv)
-        pl.when(self.z <= 0)(self.left[2].wait_recv)
-        for s in range(3):
-            pl.when((self.z >= s) & (self.z <= 2))(self.right[s].wait_send)
-            pl.when((self.z <= 3 - s) & (self.z >= 1))(self.left[s].wait_send)
-
-
-class ChainScatter:
-    def __init__(self, wires, part, right, left):
-        self.z = z = wires.z
-        self.part, self.right_box, self.left_box = part, right, left
-        self.right = {
-            j: wires.put_to(part(j), right(j), (z + 1) % 4, wires.c) for j in (3, 2, 1)
-        }
-        self.left = {j: wires.put_to(part(j), left(j), (z + 3) % 4, wires.c) for j in (0, 1, 2)}
-
-    def clear(self):
-        @pl.when(self.z == 0)
-        def _():
-            self.right_box(0)[...] = jnp.zeros_like(self.right_box(0))
-
-        @pl.when(self.z == 3)
-        def _():
-            self.left_box(3)[...] = jnp.zeros_like(self.left_box(3))
-
-    def start(self, distance):
-        pl.when(self.z == 0)(self.right[distance].start)
-        pl.when(self.z == 3)(self.left[3 - distance].start)
-
-    def pass_on(self, copy, j, box):
-        copy.wait_recv()
-        to = self.part(j)
-        to[...] = (to[...].astype(jnp.float32) + box(j)[...].astype(jnp.float32)).astype(to.dtype)
-        copy.start()
-
-    def hop(self, s, distance):
-        @pl.when(self.z == s)
-        def _():
-            self.pass_on(self.right[distance], distance, self.right_box)
-
-        @pl.when(self.z == 3 - s)
-        def _():
-            self.pass_on(self.left[3 - distance], 3 - distance, self.left_box)
-
-    def total(self):
-        for j in (1, 2, 3):
-            pl.when(self.z == j)(self.right[j].wait_recv)
-        for j in (0, 1, 2):
-            pl.when(self.z == j)(self.left[j].wait_recv)
-        z = self.z
-        return (
-            self.part(z)[...].astype(jnp.float32)
-            + self.right_box(z)[...].astype(jnp.float32)
-            + self.left_box(z)[...].astype(jnp.float32)
-        )
-
-    def sent(self):
-        for j in (1, 2, 3):
-            pl.when(self.z < j)(self.right[j].wait_send)
-        for j in (0, 1, 2):
-            pl.when(self.z > j)(self.left[j].wait_send)
-
-
-def middle_kernel(
-    zs,
-    n,
-    zz,
-    gu,
-    dy_all,
-    w_down,
-    hidden,
-    dgu_out,
-    grad_down_out,
-    result_out,
-    zz_v,
-    gu_v,
-    dy_v,
-    w_down_v,
-    hidden_v,
-    dgu_v,
-    gd_v,
-    right_v,
-    left_v,
-    total_v,
-    dz_v,
-    part,
-    near,
-    far,
-    send,
-    recv,
-    local,
-):
-    f32, b16 = jnp.float32, jnp.bfloat16
-    wires = Wires(send, recv)
-    moves = Moves(local)
-    z = wires.z
-    _, block, width = w_down_v.shape
-    ffc = zs * block
-    tokens = n * dy_v.shape[1]
-    wait_down = moves.load(w_down, w_down_v.at[z])
-    wait_zz = moves.load(zz, zz_v)
-    wait_dy = moves.load(dy_all, dy_v)
-    waits = [moves.load(gu, gu_v), moves.load(hidden, hidden_v)]
-    wires.greet(zs, n)
     wait_down.wait()
-    number = 4
     tile = width // number
     columns = [slice(p * tile, (p + 1) * tile) for p in range(number)]
     down_z = [ChainGather(wires, lambda i, k=k: w_down_v.at[i, :, k]) for k in columns]
     for chain in down_z:
         chain.start()
-    wait_zz.wait()
-    wait_dy.wait()
-    sums = [
+    for m in (1, 3, 5, 7):
+        dy_g.arrived(m)
+    for m in (1, 3, 5, 7):
+        a2_g.arrived(m)
+    wait_a2 = moves.load(wide_a, a2_out)
+    for part in gu_z:
+        part.finish()
+    moves.store(w_gu_v, w_gu_out)
+
+    def feed(i, carry):
+        gu = dot(wide_a[pair_at(i)], w_gu_v[...].reshape(width, 2 * ffc))
+        gu_v[i] = gu.astype(b16)
+        gate = gu[:, :ffc]
+        zz_v[i] = (gate * jax.nn.sigmoid(gate) * gu[:, ffc:]).astype(b16)
+        return carry
+
+    lax.fori_loop(0, n // 2, feed, 0)
+    a2_g.sent()
+    wait_a2.wait()
+
+    down_sums = [
         ChainScatter(
             wires,
-            lambda i, k=k: gd_v.at[i, :, k],
+            lambda i, k=k: wide_a.at[pl.ds(pl.multiple_of(i * block, 16), block), k],
             lambda i, k=k: right_v.at[i, :, k],
             lambda i, k=k: left_v.at[i, :, k],
         )
         for k in columns
     ]
-    y_sums = [
-        LayerScatter(wires, part.at[:, :, k], near.at[:, :, k], far.at[:, :, k]) for k in columns
-    ]
-    for k, chain in zip(columns, sums):
-        gd = dot(
+    for k, chain in zip(columns, down_sums):
+        wide_a[0:ffc, k] = dot(
             zz_v[...].reshape(tokens, ffc), dy_v[:, :, k].reshape(tokens, tile), ((0,), (0,))
-        )
-        gd_v[:, :, k] = gd.astype(b16).reshape(zs, block, tile)
+        ).astype(b16)
         chain.start(3)
     for distance in (2, 1):
-        for chain in sums:
+        for chain in down_sums:
             chain.start(distance)
-    for chain in sums:
+    for chain in down_sums:
         chain.clear()
-    for copy in waits:
-        copy.wait()
+    sums.sent()
+
+    y_sums = [
+        LayerScatter(
+            wires,
+            lambda i, k=k: block_of(wide_x, i).at[:, k],
+            lambda j, k=k: near.at[j, :, k],
+            lambda j, k=k: far.at[j, :, k],
+        )
+        for k in columns
+    ]
 
     def products(p):
         k = columns[p]
 
-        def rows(i, carry):
+        def rows_of(i, carry):
             weight = w_down_v[:, :, k].reshape(ffc, tile)
-            dy_rows = dy_v[pl.ds(2 * i, 2), :, k].reshape(2 * tokens // n, tile)
+            dy_rows = dy_v[pl.ds(2 * i, 2), :, k].reshape(pair, tile)
             dz = dot(dy_rows, weight, ((1,), (1,)))
             dz_v[i] = dz if p == 0 else dz_v[i] + dz
-            part[pl.ds(2 * i, 2), :, k] = (
-                dot(zz_v[i], weight).astype(b16).reshape(2, tokens // n, tile)
-            )
+            wide_x[pair_at(i), k] = dot(zz_v[i], weight).astype(b16)
             return carry
 
-        lax.fori_loop(0, n // 2, rows, 0)
+        lax.fori_loop(0, n // 2, rows_of, 0)
 
     for t in range(number + 1):
         if t < number:
@@ -1118,78 +992,124 @@
         if t >= 1:
             down_z[t - 1].hop(2)
     for t in range(number):
-        sums[t].hop(1, 3)
+        down_sums[t].hop(1, 3)
         down_z[t].finish()
         products(t)
         y_sums[t].start()
         if t >= 1:
             for m in (6, 4, 2):
                 y_sums[t - 1].step(m)
-    for m in (6, 4, 2):
-        y_sums[number - 1].step(m)
-    for chain in sums:
-        chain.hop(1, 2)
-        chain.hop(2, 3)
 
     def back(i, carry):
         dz = dz_v[i]
-        gu_block = gu_v[i]
-        gate, up = gu_block[:, :ffc], gu_block[:, ffc:]
+        gu = gu_v[i].astype(f32)
+        gate, up = gu[:, :ffc], gu[:, ffc:]
         sig = jax.nn.sigmoid(gate)
         dg = dz * up * sig * (1.0 + gate * (1.0 - sig))
         du = dz * gate * sig
-        dgu_v[i] = jnp.concatenate([dg, du], -1).astype(b16)
+        gu_v[i] = jnp.concatenate([dg, du], -1).astype(b16)
         return carry
 
     lax.fori_loop(0, n // 2, back, 0)
-    moves.store(dgu_v, dgu_out)
-    for k, chain in zip(columns, sums):
-        total_v[:, k] = chain.total()
-    moves.store(total_v, grad_down_out)
+    moves.store(gu_v, dgu_out)
+    for m in (6, 4, 2):
+        y_sums[number - 1].step(m)
+    for chain in down_sums:
+        chain.hop(1, 2)
+        chain.hop(2, 3)
     for k, y_sum in zip(columns, y_sums):
         result_out[:, k] = (hidden_v[:, k] + y_sum.total()).astype(b16)
-    for group in (*sums, *y_sums):
+    stored = [None, None]
+    for p, (k, chain) in enumerate(zip(columns, down_sums)):
+        if stored[p % 2] is not None:
+            stored[p % 2].wait()
+        total_v[p % 2] = chain.total()
+        stored[p % 2] = moves.load(total_v.at[p % 2], grad_down_out.at[:, k])
+    for copy in stored:
+        copy.wait()
+    for group in (*down_sums, *y_sums, dy_g):
         group.sent()
+    for copy in (*small_z, *qkv_x, *gu_x):
+        copy.wait_send()
     moves.finish()
 
 
-def middle(zs, n, zz, gu, dy_all, w_down, hidden):
+def front(zs, n, slots, lengths, tables, small, w_qkv, w_gate, w_up, w_out, w_down, xs, dy):
     f32, b16 = jnp.float32, jnp.bfloat16
-    block, width = w_down.shape
-    local = hidden.shape[0]
+    local, width = xs.shape
+    rows = local // slots
+    seq, tokens = rows * n, local * n
+    heads = HEADS // n
+    hc = heads * HEAD_DIM
+    wrows = w_out.shape[0]
+    block = w_down.shape[0]
+    gc = 2 * zs * block
+    qkv_all = ((zs, n, wrows, 3 * hc), b16)
+    out_all = ((zs, wrows, width), b16)
+    gu_all = ((zs, n, wrows, gc), b16)
+    down_all = ((zs, block, width), b16)
+    wide = ((tokens, width), b16)
+    qkv = ((3, slots, n, rows, hc), b16)
+    probs = ((slots, heads, seq, seq), b16)
+    ob = ((n, slots, rows, hc), b16)
+    hidden = ((local, width), f32)
+    gu = ((n // 2, 2 * local, gc), b16)
+    outs = [
+        qkv_all,
+        out_all,
+        gu_all,
+        wide,
+        qkv,
+        probs,
+        ob,
+        hidden,
+        wide,
+        gu,
+        ((block, width), f32),
+        ((local, width), b16),
+        ((8, width), f32),
+    ]
+    scratch = [
+        ((n, wrows, 3 * hc), b16),
+        ((n, wrows, gc), b16),
+        ((zs, n, *small.shape), f32),
+        ((1, 3 * hc), f32),
+        qkv_all,
+        out_all,
+        gu_all,
+        down_all,
+        wide,
+        wide,
+        ((n, local, width), b16),
+        qkv,
+        (probs[0][1:], b16),
+        ob,
+        ((n // 2, local, width), b16),
+        ((n // 2 - 1, local, width), b16),
+        hidden,
+        gu,
+        ((n // 2, 2 * local, gc // 2), b16),
+        ((n // 2, 2 * local, gc // 2), f32),
+        down_all,
+        down_all,
+        ((2, block, width // 4), f32),
+    ]
     return pl.pallas_call(
-        functools.partial(middle_kernel, zs, n),
-        out_shape=[
-            jax.ShapeDtypeStruct(gu.shape, b16),
-            jax.ShapeDtypeStruct((block, width), f32),
-            jax.ShapeDtypeStruct((local, width), b16),
-        ],
-        in_specs=[HBM] * 5,
-        out_specs=[HBM, HBM, VMEM],
+        functools.partial(front_kernel, zs, n, slots),
+        out_shape=[jax.ShapeDtypeStruct(*k) for k in outs],
+        in_specs=[pl.BlockSpec(memory_space=pltpu.SMEM), VMEM, HBM, *[VMEM] * 3, *[HBM] * 4],
+        out_specs=[HBM] * (len(outs) - 2) + [VMEM] * 2,
         scratch_shapes=[
-            pltpu.VMEM(zz.shape, b16),
-            pltpu.VMEM(gu.shape, f32),
-            pltpu.VMEM(dy_all.shape, b16),
-            pltpu.VMEM((zs, block, width), b16),
-            pltpu.VMEM((local, width), f32),
-            pltpu.VMEM(gu.shape, b16),
-            pltpu.VMEM((zs, block, width), b16),
-            pltpu.VMEM((zs, block, width), b16),
-            pltpu.VMEM((zs, block, width), b16),
-            pltpu.VMEM((block, width), f32),
-            pltpu.VMEM(zz.shape, f32),
-            pltpu.VMEM((n, local, width), b16),
-            pltpu.VMEM((n // 2, local, width), b16),
-            pltpu.VMEM((n // 2 - 1, local, width), b16),
-            pltpu.SemaphoreType.DMA((80,)),
-            pltpu.SemaphoreType.DMA((80,)),
-            pltpu.SemaphoreType.DMA((8,)),
+            *[pltpu.VMEM(*k) for k in scratch],
+            pltpu.SemaphoreType.DMA((192,)),
+            pltpu.SemaphoreType.DMA((192,)),
+            pltpu.SemaphoreType.DMA((32,)),
         ],
         compiler_params=pltpu.CompilerParams(
-            collective_id=3, has_side_effects=True, vmem_limit_bytes=60 << 20
+            collective_id=1, has_side_effects=True, vmem_limit_bytes=VMEM_LIMIT
         ),
-        name="middle",
-    )(zz, gu, dy_all, w_down, hidden)
+        name="front",
+    )(lengths, tables, small, w_qkv, w_gate, w_up, w_out, w_down, xs, dy)
 
 
 def unpack_columns(dst, src, at, block, n, zs):
@@ -1218,7 +1138,7 @@
     probs,
     ob,
     hidden,
-    dy_all,
+    dy,
     xs,
     grad_out_out,
     input_grad_out,
@@ -1279,7 +1199,7 @@
     wait_w = moves.load(w_gu, gu_weight)
     waits = [
         moves.load(hidden, hidden_v),
-        moves.load(dy_all.at[c], own_v),
+        moves.load(dy, own_v),
         moves.load(w_out, w_out_v),
         moves.load(qkv, qkv_v),
         moves.load(probs.at[0], probs_v),
@@ -1335,7 +1255,9 @@
 
     lax.fori_loop(0, n // 2, normed_two, 0)
     wait_qkv = moves.load(w_qkv, qkv_weight)
-    da2_sums = LayerScatter(wires, part, near, far)
+    da2_sums = LayerScatter(
+        wires, lambda i: part.at[i], lambda j: near.at[j], lambda j: far.at[j]
+    )
     da2_sums.start()
     gu_sums[0].relay()
     for m in (6, 4, 2):
@@ -1351,7 +1273,7 @@
     input_grad_out[...] = dh
     dh_all[c] = dh.astype(b16)
     wait_xs = moves.load(xs, own_v)
-    dh_g = LayerGather(wires, dh_all)
+    dh_g = LayerGather(wires, lambda i: dh_all.at[i])
     dh_g.start()
     for m in (2, 4, 6):
         dh_g.forward(m)
@@ -1451,7 +1373,9 @@
 
     da2_sums.sent()
     lax.fori_loop(0, n // 2, normed_one, 0)
-    da1_sums = LayerScatter(wires, part, near, far)
+    da1_sums = LayerScatter(
+        wires, lambda i: part.at[i], lambda j: near.at[j], lambda j: far.at[j]
+    )
     da1_sums.start()
     for m in (6, 4, 2):
         da1_sums.step(m)
@@ -1553,7 +1477,7 @@
 
 def backward(zs, n, norms, tables, *arrays):
     f32, b16 = jnp.float32, jnp.bfloat16
-    a1_all, a2_all, dgu, w_gu, w_qkv, w_out, qkv, probs, ob, hidden, dy_all, xs = arrays
+    a1_all, a2_all, dgu, w_gu, w_qkv, w_out, qkv, probs, ob, hidden, dy, xs = arrays
     _, slots, rows, hc = ob.shape
     local, width = hidden.shape
     _, depth, gc = w_gu.shape
@@ -1638,7 +1562,6 @@
     zs, n = lax.axis_size("dp"), lax.axis_size("ctx")
     me = lax.axis_index("ctx")
     local = rows * slots
-    tokens = local * n
     seq = rows * n
     wrows = w_qkv.shape[0]
     ff_block = w_down.shape[0]
@@ -1653,23 +1576,14 @@
 
     xs = local_tokens(inputs)
     dy = local_tokens(cotangent)
+    nb = b_qkv.shape[0]
+    vectors = [v for gain in (gain_one, shift_one, gain_two, shift_two) for v in (gain, gain)]
     small, at = jnp.zeros(1024, f32), 0
-    for vector in (b_qkv, gain_one, shift_one, gain_two, shift_two):
+    for vector in (*vectors, b_qkv):
         size = vector.shape[0]
         small = small + jnp.pad(vector.astype(f32), (at, 1024 - at - size))
         at += size
     small = small.reshape(8, 128)
-    w_qkv_c, w_out_c, gu_own, a_all, small = spread(
-        zs, n, w_qkv, w_gate, w_up, w_out, xs, small
-    )
-    small = small.reshape(zs * n, 1024)
-    nb = b_qkv.shape[0]
-    bias_full = small[:, :nb].reshape(3, zs, n, HEAD_DIM)
-    bias_own = lax.dynamic_index_in_dim(bias_full, me, 2, keepdims=False).reshape(1, 3 * hc)
-    g1, s1, g2, s2 = [
-        small[:, nb + i * wrows : nb + (i + 1) * wrows].reshape(1, width) for i in range(4)
-    ]
-
 
     angles = np.arange(seq)[:, None] * 10000.0 ** (-2.0 * np.arange(ROTARY // 2) / ROTARY)[None, :]
     cos_t, sin_t = np.cos(angles), np.sin(angles)
@@ -1686,15 +1600,14 @@
     ).astype(np.float32)
 
     tables = jnp.asarray(tables.reshape(3, n, rows, 2 * HEAD_DIM))
-    norms = jnp.concatenate([g1, s1, g2, s2])
-    a1_all, qkv, probs, ob, hidden, a2_all, w_gu_c, gu, z, dy_all = forward(
-        zs, n, slots, lengths, norms, bias_own, tables, a_all, w_qkv_c, w_out_c,
-        gu_own.reshape(n * wrows, 2 * ffc), dy,
-    )
-    dgu, grad_down, result = middle(zs, n, z, gu, dy_all, w_down, hidden)
+    w_qkv_c, w_out_c, w_gu_c, a1, qkv, probs, ob, hidden, a2, dgu, grad_down, result, norms = front(
+        zs, n, slots, lengths, tables, small, w_qkv, w_gate, w_up, w_out, w_down, xs, dy
+    )
+    wide = (n, local, width)
     grad_out, input_grad, grad_qkv, grad_gate, grad_up, sums = backward(
-        zs, n, norms, tables, a1_all, a2_all, dgu, w_gu_c, w_qkv_c.reshape(zs, n * wrows, 3 * hc),
-        w_out_c, qkv, probs, ob, hidden, dy_all, xs,
+        zs, n, norms, tables, a1.reshape(wide), a2.reshape(wide), dgu,
+        w_gu_c.reshape(zs, n * wrows, 2 * ffc), w_qkv_c.reshape(zs, n * wrows, 3 * hc),
+        w_out_c, qkv, probs, ob, hidden, dy, xs,
     )
     mine = lax.dynamic_slice_in_dim(sums[:4], me % 2 * wrows, wrows, 1)
     grad_bias = lax.dynamic_slice_in_dim(sums[4:7].reshape(2 * nb), me % 2 * nb, nb)

time: 487 us -> 473 us (0.971)
  local copies, waits for them, and re-layouts: 22.1 us -> 10.3 us
  Pallas kernels: 449 us -> 443 us
  other arithmetic: 5.09 us -> 10 us
    unnamed x35 -> x14, local copies, waits for them, and re-layouts: 11.9 us -> 1.92 us
    pallas_call x3 -> x1, Pallas kernels: 265 us -> 259 us  [front(): pl.pallas_call(functools.partial(front_kernel, zs, n, slots), out_shape=[...]
where the time goes in v6:
time: 473 us; the launch traced here: 464 us
  Pallas kernels  443 us (94%)
  local copies, waits for them, and re-layouts  10.3 us (2%)
  other arithmetic  10 us (2%)
    pallas_call x1, Pallas kernels, front(): pl.pallas_call(functools.partial(front_kernel, zs, n, slots), out_shape=[...  259 us
    pallas_call x1, Pallas kernels, backward(): pl.pallas_call(functools.partial(backward_kernel, zs, n), out_shape=[jax....  184 us

profile of v6, /device:TPU:1, one launch (start us, length us, event | category | flops | bytes accessed | tf_op | source)
XLA Modules:
  0.0 464.3 jit_solution(16430983885961886231)
XLA Ops:
  0.6 2.0 copy.26
  2.6 2.0 copy.27
  4.6 0.7 convert_element_type.44
  5.3 0.7 convert_element_type.45
  5.9 0.7 convert_element_type.46
  6.6 0.7 convert_element_type.47
  7.3 1.3 add_bitcast_fusion.small
  8.6 258.6 %front.1 = (bf16[4,8,64,768]{3,2,1,0:T(8,128)(2,1)}, bf16[4,64,2048]{2,1,0:T(8,128)(2,1)}, bf16[4,8,64,1408]{3,2,1,0:T(8,128)(2,1)}, bf16[1024,2048]{1,0:T(8,128...) custom-call(s32[1,2]{1,0:T(1,128)} %lengths.1, ...), custom_call_target="tpu_custom_call" | custom-call | tf_op jit(solution)/shard_map/front/pallas_call | solution.py:1097
  267.2 184.3 %backward.1 = (f32[64,2048]{1,0:T(8,128)}, f32[128,2048]{1,0:T(8,128)}, bf16[64,6144]{1,0:T(8,128)(2,1)}, bf16[64,5632]{1,0:T(8,128)(2,1)}, bf16[64,5632]{1,0:T(8,128)(2,1)}, /*index=5*/f32[8,128]{1,0:T(8,128)}) custom-call(f32[8,2048]{1,0:T(8,128)} %get-tuple-element.32.norms, f32[3,8,64,128]{3,2,1,0:T(8,128)} %constant.34.clone.tables, ...), custom_call_target="tpu_custom_call" | custom-call | tf_op jit(solution)/shard_map/backward/pallas_call | solution.py:1492
  451.5 0.0 copy-start.2
  451.5 0.0 copy-start.1
  451.6 2.5 convert_element_type.48
  454.1 0.0 copy-start.5
  454.1 0.0 copy-start.3
  454.1 2.4 convert_element_type.49
  456.4 0.0 copy-start.4
  456.4 0.0 copy-done.2
  456.4 0.0 copy-start
  456.4 1.2 convert_element_type.50
  457.6 0.0 copy-done.1
  457.6 1.8 copy.32
  459.4 0.0 copy-done.5
  459.4 0.1 constant_dynamic-slice_fusion
  459.5 0.5 slice_bitcast_fusion.1
  460.0 0.6 dynamic_slice.6
  460.7 0.0 copy-done.3
  460.7 1.3 copy.33
  462.0 0.0 copy-done.4
  462.0 0.8 copy.36
  462.8 0.0 copy-done
  462.8 1.1 copy.37
  (2 shorter events, 0.0 us)
Async XLA Ops:
  451.5 4.9 %copy-start.2 = (bf16[64,5632]{1,0:T(8,128)(2,1)S(1)}, bf16[64,5632]{1,0:T(8,128)(2,1)}, u32[]{:S(2)}) copy-start(bf16[64,5632]{1,0:T(8,128)(2,1)} %get-tuple-element.48) | copy-start | bytes 2162692
  451.5 6.1 %copy-start.1 = (f32[128,2048]{1,0:T(8,128)S(1)}, f32[128,2048]{1,0:T(8,128)}, u32[]{:S(2)}) copy-start(f32[128,2048]{1,0:T(8,128)} %get-tuple-element.43) | copy-start | bytes 3145732
  454.1 5.4 %copy-start.5 = (f32[8,128]{1,0:T(8,128)S(1)}, f32[8,128]{1,0:T(8,128)}, u32[]{:S(2)}) copy-start(f32[8,128]{1,0:T(8,128)} %get-tuple-element.45) | copy-start | bytes 12292
  454.1 6.6 %copy-start.3 = (bf16[128,2048]{1,0:T(8,128)(2,1)S(1)}, bf16[128,2048]{1,0:T(8,128)(2,1)}, u32[]{:S(2)}) copy-start(bf16[128,2048]{1,0:T(8,128)(2,1)} %get-tuple-element.31) | copy-start | bytes 1572868
  456.4 5.6 %copy-start.4 = (f32[64,2048]{1,0:T(8,128)S(1)}, f32[64,2048]{1,0:T(8,128)}, u32[]{:S(2)}) copy-start(f32[64,2048]{1,0:T(8,128)} %get-tuple-element.70) | copy-start | bytes 1572868
  456.4 6.4 %copy-start = (f32[176,2048]{1,0:T(8,128)S(1)}, f32[176,2048]{1,0:T(8,128)}, u32[]{:S(2)}) copy-start(f32[176,2048]{1,0:T(8,128)} %get-tuple-element.73) | copy-start | bytes 4325380

commit v7 on v6

--- a/solution.py
+++ b/solution.py
@@ -438,8 +438,9 @@
 def pack_columns(dst, refs, n, zs):
     for i in range(n):
         pieces = []
-        for ref, block in refs:
-            pieces += [ref[:, block * (j * n + i) : block * (j * n + i + 1)] for j in range(zs)]
+        for ref, block, at, size in refs:
+            starts = [block * (j * n + i) + at for j in range(zs)]
+            pieces += [ref[:, start : start + size] for start in starts]
         dst[i] = jnp.concatenate(pieces, -1)
 
 
@@ -612,11 +613,11 @@
     def clear(self):
         @pl.when(self.z == 0)
         def _():
-            self.right_box(0)[...] = jnp.zeros_like(self.right_box(0))
+            self.right_box(1)[...] = jnp.zeros_like(self.right_box(1))
 
         @pl.when(self.z == 3)
         def _():
-            self.left_box(3)[...] = jnp.zeros_like(self.left_box(3))
+            self.left_box(2)[...] = jnp.zeros_like(self.left_box(2))
 
     def start(self, distance):
         pl.when(self.z == 0)(self.right[distance].start)
@@ -645,8 +646,8 @@
         z = self.z
         return (
             self.part(z)[...].astype(jnp.float32)
-            + self.right_box(z)[...].astype(jnp.float32)
-            + self.left_box(z)[...].astype(jnp.float32)
+            + self.right_box(jnp.maximum(z, 1))[...].astype(jnp.float32)
+            + self.left_box(jnp.minimum(z, 2))[...].astype(jnp.float32)
         )
 
     def sent(self):
@@ -654,6 +655,11 @@
             pl.when(self.z < j)(self.right[j].wait_send)
         for j in (0, 1, 2):
             pl.when(self.z > j)(self.left[j].wait_send)
+
+
+def halves_of(block):
+    first = (block // 16 + 1) // 2 * 16
+    return [(0, first), (first, block - first)]
 
 
 def front_kernel(
@@ -680,8 +686,8 @@
     hidden_out,
     a2_out,
     dgu_out,
+    y_out,
     grad_down_out,
-    result_out,
     norms,
     qkv_send,
     gu_send,
@@ -703,9 +709,9 @@
     gu_v,
     zz_v,
     dz_v,
+    gd_v,
     right_v,
     left_v,
-    total_v,
     send,
     recv,
     local,
@@ -722,6 +728,8 @@
     heads = hc // HEAD_DIM
     block = w_down_v.shape[1]
     ffc = zs * block
+    halves = halves_of(block)
+    spans = [(2 * zs * at, zs * size) for at, size in halves]
     lanes = 2 * HEAD_DIM
     lane_half = lax.broadcasted_iota(jnp.int32, (1, lanes), 1) // HEAD_DIM
 
@@ -737,7 +745,10 @@
     wait_dy = moves.load(dy, dy_v.at[c])
     wait_down = moves.load(w_down, w_down_v.at[z])
     pack_columns(
-        qkv_send, [(w_qkv.at[:, i * width : (i + 1) * width], HEAD_DIM) for i in range(3)], n, zs
+        qkv_send,
+        [(w_qkv.at[:, i * width : (i + 1) * width], HEAD_DIM, 0, HEAD_DIM) for i in range(3)],
+        n,
+        zs,
     )
     wait_own_qkv = moves.load(qkv_send.at[c], w_qkv_v.at[z, c])
     wires.greet(zs, n)
@@ -753,7 +764,9 @@
         copy.start()
     xs_g = LayerGather(wires, lambda i: block_of(wide_x, i), xs)
     xs_g.start()
-    pack_columns(gu_send, [(w_gate, block), (w_up, block)], n, zs)
+    pack_columns(
+        gu_send, [(w, block, at, size) for at, size in halves for w in (w_gate, w_up)], n, zs
+    )
     wait_own_gu = moves.load(gu_send.at[c], w_gu_v.at[z, c])
     for copy in small_z:
         copy.wait_recv()
@@ -820,12 +833,18 @@
     for copy in gu_x:
         copy.wait_recv()
     gu_z = [
-        DepthGather(wires, lambda i, a=a, s=s: w_gu_v.at[i, a : a + s])
-        for a, s in pieces_of(n, number, 1)
+        [
+            DepthGather(
+                wires, lambda i, a=a, s=s, k=slice(at, at + 2 * size): w_gu_v.at[i, a : a + s, :, k]
+            )
+            for a, s in pieces_of(n, number, 1)
+        ]
+        for at, size in spans
     ]
     for part in qkv_z:
         part.forward()
-    DepthGather.start(gu_z)
+    for part in gu_z:
+        DepthGather.start(part)
     wait_dy.wait()
     dy_g = LayerGather(wires, lambda i: dy_v.at[i])
     dy_g.start()
@@ -887,7 +906,8 @@
 
     lax.fori_loop(0, slots, attend, 0)
     moves.store(ob_v, ob_out)
-    gu_z[0].forward()
+    for part in gu_z[0][:2]:
+        part.forward()
 
     xs_g.sent()
 
@@ -905,17 +925,19 @@
     sums.start()
     for m in (6, 4, 2):
         sums.step(m)
-    gu_z[1].forward()
+    for part in gu_z[0][2:]:
+        part.forward()
     hidden = hidden_v[...] + sums.total()
     hidden_v[...] = hidden
     moves.store(hidden_v, hidden_out)
     block_of(wide_a, c)[...] = (layer_stats(hidden)[0] * norms[2:3] + norms[3:4]).astype(b16)
     a2_g = LayerGather(wires, lambda i: block_of(wide_a, i))
     a2_g.start()
-    gu_z[2].forward()
+    gu_z[1][0].forward()
     for m in (2, 4, 6):
         a2_g.forward(m)
-    gu_z[3].forward()
+    for part in gu_z[1][1:]:
+        part.forward()
     wait_down.wait()
     tile = width // number
     columns = [slice(p * tile, (p + 1) * tile) for p in range(number)]
@@ -927,107 +949,105 @@
     for m in (1, 3, 5, 7):
         a2_g.arrived(m)
     wait_a2 = moves.load(wide_a, a2_out)
-    for part in gu_z:
-        part.finish()
+
+    down_sums = []
+    for step, ((at, size), (start, count), parts) in enumerate(zip(halves, spans, gu_z)):
+        units, gates = slice(at, at + size), slice(start, start + 2 * count)
+        inner = slice(zs * at, zs * (at + size))
+        for part in parts:
+            part.finish()
+
+        def feed(i, carry, inner=inner, gates=gates, count=count):
+            gu = dot(wide_a[pair_at(i)], w_gu_v[:, :, :, gates].reshape(width, 2 * count))
+            gu_v[i, :, gates] = gu.astype(b16)
+            gate = gu[:, :count]
+            zz_v[i, :, inner] = (gate * jax.nn.sigmoid(gate) * gu[:, count:]).astype(b16)
+            return carry
+
+        lax.fori_loop(0, n // 2, feed, 0)
+        if step == 1:
+            down_z[0].hop(1)
+            down_z[1].hop(1)
+        chains = []
+        for p in range(2):
+            k = slice(p * width // 2, (p + 1) * width // 2)
+            for q in columns[2 * p : 2 * p + 2]:
+                gd = dot(
+                    zz_v[:, :, inner].reshape(tokens, count),
+                    dy_v[:, :, q].reshape(tokens, tile),
+                    ((0,), (0,)),
+                )
+                gd_v[:, units, q] = gd.astype(b16).reshape(zs, size, tile)
+            chains.append(
+                ChainScatter(
+                    wires,
+                    lambda i, u=units, k=k: gd_v.at[i, u, k],
+                    lambda i, u=units, k=k: right_v.at[i - 1, u, k],
+                    lambda i, u=units, k=k: left_v.at[i, u, k],
+                )
+            )
+            chains[-1].start(3)
+            down_sums.append((units, k, chains[-1]))
+            if step == 1:
+                down_z[2 + p].hop(1)
+                down_z[p].hop(2)
+        for distance in (2, 1):
+            for chain in chains:
+                chain.start(distance)
+        for chain in chains:
+            chain.clear()
     moves.store(w_gu_v, w_gu_out)
-
-    def feed(i, carry):
-        gu = dot(wide_a[pair_at(i)], w_gu_v[...].reshape(width, 2 * ffc))
-        gu_v[i] = gu.astype(b16)
-        gate = gu[:, :ffc]
-        zz_v[i] = (gate * jax.nn.sigmoid(gate) * gu[:, ffc:]).astype(b16)
-        return carry
-
-    lax.fori_loop(0, n // 2, feed, 0)
+    sums.sent()
     a2_g.sent()
     wait_a2.wait()
 
-    down_sums = [
-        ChainScatter(
-            wires,
-            lambda i, k=k: wide_a.at[pl.ds(pl.multiple_of(i * block, 16), block), k],
-            lambda i, k=k: right_v.at[i, :, k],
-            lambda i, k=k: left_v.at[i, :, k],
-        )
-        for k in columns
-    ]
-    for k, chain in zip(columns, down_sums):
-        wide_a[0:ffc, k] = dot(
-            zz_v[...].reshape(tokens, ffc), dy_v[:, :, k].reshape(tokens, tile), ((0,), (0,))
-        ).astype(b16)
-        chain.start(3)
-    for distance in (2, 1):
-        for chain in down_sums:
-            chain.start(distance)
-    for chain in down_sums:
-        chain.clear()
-    sums.sent()
-
-    y_sums = [
-        LayerScatter(
-            wires,
-            lambda i, k=k: block_of(wide_x, i).at[:, k],
-            lambda j, k=k: near.at[j, :, k],
-            lambda j, k=k: far.at[j, :, k],
-        )
-        for k in columns
-    ]
-
     def products(p):
         k = columns[p]
 
         def rows_of(i, carry):
-            weight = w_down_v[:, :, k].reshape(ffc, tile)
             dy_rows = dy_v[pl.ds(2 * i, 2), :, k].reshape(pair, tile)
-            dz = dot(dy_rows, weight, ((1,), (1,)))
-            dz_v[i] = dz if p == 0 else dz_v[i] + dz
-            wide_x[pair_at(i), k] = dot(zz_v[i], weight).astype(b16)
+            y = jnp.zeros((pair, tile), f32)
+            for at, size in halves:
+                weight = w_down_v[:, at : at + size, k].reshape(zs * size, tile)
+                inner = slice(zs * at, zs * (at + size))
+                dz = dot(dy_rows, weight, ((1,), (1,)))
+                dz_v[i, :, inner] = dz if p == 0 else dz_v[i, :, inner] + dz
+                y = y + dot(zz_v[i, :, inner], weight)
+            wide_x[pair_at(i), k] = y.astype(b16)
             return carry
 
         lax.fori_loop(0, n // 2, rows_of, 0)
 
-    for t in range(number + 1):
-        if t < number:
-            down_z[t].hop(1)
-        if t >= 1:
-            down_z[t - 1].hop(2)
+    down_z[2].hop(2)
+    down_z[3].hop(2)
+    chains = [chain for _, _, chain in down_sums]
     for t in range(number):
-        down_sums[t].hop(1, 3)
+        chains[t].hop(1, 3)
         down_z[t].finish()
         products(t)
-        y_sums[t].start()
-        if t >= 1:
-            for m in (6, 4, 2):
-                y_sums[t - 1].step(m)
+    moves.store(wide_x, y_out)
+    for pair_of in (chains[:2], chains[2:]):
+        for chain in pair_of:
+            chain.hop(1, 2)
+        for chain in pair_of:
+            chain.hop(2, 3)
 
     def back(i, carry):
-        dz = dz_v[i]
-        gu = gu_v[i].astype(f32)
-        gate, up = gu[:, :ffc], gu[:, ffc:]
-        sig = jax.nn.sigmoid(gate)
-        dg = dz * up * sig * (1.0 + gate * (1.0 - sig))
-        du = dz * gate * sig
-        gu_v[i] = jnp.concatenate([dg, du], -1).astype(b16)
+        for (at, size), (start, count) in zip(halves, spans):
+            dz = dz_v[i, :, zs * at : zs * (at + size)]
+            gate = gu_v[i, :, start : start + count].astype(f32)
+            up = gu_v[i, :, start + count : start + 2 * count].astype(f32)
+            sig = jax.nn.sigmoid(gate)
+            dg = dz * up * sig * (1.0 + gate * (1.0 - sig))
+            du = dz * gate * sig
+            gu_v[i, :, start : start + 2 * count] = jnp.concatenate([dg, du], -1).astype(b16)
         return carry
 
     lax.fori_loop(0, n // 2, back, 0)
     moves.store(gu_v, dgu_out)
-    for m in (6, 4, 2):
-        y_sums[number - 1].step(m)
-    for chain in down_sums:
-        chain.hop(1, 2)
-        chain.hop(2, 3)
-    for k, y_sum in zip(columns, y_sums):
-        result_out[:, k] = (hidden_v[:, k] + y_sum.total()).astype(b16)
-    stored = [None, None]
-    for p, (k, chain) in enumerate(zip(columns, down_sums)):
-        if stored[p % 2] is not None:
-            stored[p % 2].wait()
-        total_v[p % 2] = chain.total()
-        stored[p % 2] = moves.load(total_v.at[p % 2], grad_down_out.at[:, k])
-    for copy in stored:
-        copy.wait()
-    for group in (*down_sums, *y_sums, dy_g):
+    for units, k, chain in down_sums:
+        grad_down_out[units, k] = chain.total()
+    for group in (*chains, dy_g):
         group.sent()
     for copy in (*small_z, *qkv_x, *gu_x):
         copy.wait_send()
@@ -1065,8 +1085,8 @@
         hidden,
         wide,
         gu,
+        wide,
         ((block, width), f32),
-        ((local, width), b16),
         ((8, width), f32),
     ]
     scratch = [
@@ -1091,8 +1111,8 @@
         ((n // 2, 2 * local, gc // 2), b16),
         ((n // 2, 2 * local, gc // 2), f32),
         down_all,
-        down_all,
-        ((2, block, width // 4), f32),
+        ((zs - 1, block, width), b16),
+        ((zs - 1, block, width), b16),
     ]
     return pl.pallas_call(
         functools.partial(front_kernel, zs, n, slots),
@@ -1112,12 +1132,13 @@
     )(lengths, tables, small, w_qkv, w_gate, w_up, w_out, w_down, xs, dy)
 
 
-def unpack_columns(dst, src, at, block, n, zs):
+def unpack_columns(dst, src, parts, n, zs):
     dst[...] = jnp.concatenate(
         [
-            src[i, :, at + block * j : at + block * (j + 1)]
+            src[i, :, at + size * j : at + size * (j + 1)]
             for j in range(zs)
             for i in range(n)
+            for at, size in parts
         ],
         -1,
     )
@@ -1140,7 +1161,9 @@
     hidden,
     dy,
     xs,
+    y_part,
     grad_out_out,
+    result_out,
     input_grad_out,
     gq_out,
     gate_out,
@@ -1178,6 +1201,7 @@
     send,
     recv,
     local,
+    free,
 ):
     f32, b16 = jnp.float32, jnp.bfloat16
     wires = Wires(send, recv)
@@ -1224,7 +1248,7 @@
             for p in range(number)
         ]
 
-    def weigh(sums, whole, left_v, grads):
+    def weigh(sums, whole, left_v, grads, also=None):
         for mask in (3, 2, 1, 0):
             to = flip(z, mask)
 
@@ -1239,6 +1263,8 @@
             lax.fori_loop(0, number // 2, piece, 0)
             for part_sum in sums:
                 part_sum.start(mask)
+            if mask == 3 and also is not None:
+                also.start(3)
 
     gu_sums = scatters(ggu_v, relay_v, box_v)
     weigh(gu_sums, ggu_v, wide_v, lambda: dgu_v[...].reshape(tokens, gc))
@@ -1294,8 +1320,6 @@
         return carry
 
     lax.fori_loop(0, 4, heads_grad, 0)
-    for mask in (3, 2, 1, 0):
-        go_sums.start(mask)
 
     def heads_back(i, carry):
         ob_v[i] = (
@@ -1352,12 +1376,13 @@
 
     probs_sem = moves.sems.at[next(moves.number)]
     lax.fori_loop(0, slots, attend, 0)
-    go_sums.relay()
 
     wait_a1.wait()
     wait_qkv.wait()
     qkv_sums = scatters(gq_v, gq_relay, gq_box)
-    weigh(qkv_sums, gq_v, dh_all, lambda: dj_v[...].reshape(tokens, qc))
+    weigh(qkv_sums, gq_v, dh_all, lambda: dj_v[...].reshape(tokens, qc), go_sums)
+    for mask in (2, 1, 0):
+        go_sums.start(mask)
 
     def normed_one(i, carry):
         part[pl.ds(2 * i, 2)] = (
@@ -1395,13 +1420,19 @@
         copy.start()
     gu_rows[c] = ggu_v[z, pl.ds(pl.multiple_of(c * wrows, wrows), wrows)]
 
+    for part_sum in qkv_sums:
+        part_sum.relay()
+    go_sums.relay()
+
     wait_xs.wait()
     n1, r1 = layer_stats(own_v[...].astype(f32))
     da1 = da1_sums.total()
+    for m in (1, 2, 4, 6):
+        pl.semaphore_signal(free, inc=1, device_id=(z, flip(c, m)), device_id_type=MESH)
+    da1_sums.sent()
+    wait_y = moves.load(y_part, part)
     input_grad_out[...] += norm_back(da1, n1, r1, norms[0:1])
     gains = [jnp.sum(da1 * n1, 0, keepdims=True), jnp.sum(da1, 0, keepdims=True), *gains]
-    for part_sum in qkv_sums:
-        part_sum.relay()
     chips = n // 2
     lanes = 2 * HEAD_DIM
     lane_half = lax.broadcasted_iota(jnp.int32, (1, lanes), 1) // HEAD_DIM
@@ -1428,12 +1459,15 @@
     ]
     for copy in small_v_x:
         copy.start()
-    hidden_v[0:wrows] = go_sums.total()
-    moves.store(hidden_v.at[0:wrows], grad_out_out)
-    for copy in gu_x:
-        copy.wait_recv()
-    unpack_columns(gate_out, gu_rows, 0, ffc // zs, n, zs)
-    unpack_columns(up_out, gu_rows, ffc, ffc // zs, n, zs)
+
+    wait_y.wait()
+    pl.semaphore_wait(free, 4)
+    y_sums = LayerScatter(
+        wires, lambda i: part.at[i], lambda j: near.at[j], lambda j: far.at[j]
+    )
+    y_sums.start()
+    for m in (6, 4, 2):
+        y_sums.step(m)
     small_sum = small_v[:, c // 2]
     for m in range(1, n):
         small_v_x[m - 1].wait_recv()
@@ -1442,11 +1476,11 @@
     small_z_x = [wires.put(small_r.at[flip(z, m)], small_z.at[m], m, 0) for m in range(1, zs)]
     for copy in small_z_x:
         copy.start()
-    small_sum = small_r[z]
-    for m in range(1, zs):
-        small_z_x[m - 1].wait_recv()
-        small_sum = small_sum + small_z[m]
-    small_out[...] = small_sum
+    for copy in gu_x:
+        copy.wait_recv()
+    halves = halves_of(ffc // zs)
+    unpack_columns(gate_out, gu_rows, [(2 * zs * at, size) for at, size in halves], n, zs)
+    unpack_columns(up_out, gu_rows, [(zs * (2 * at + size), size) for at, size in halves], n, zs)
 
     for p, part_sum in enumerate(qkv_sums):
         gq_v[z, p * size : (p + 1) * size] = part_sum.total().astype(b16)
@@ -1462,7 +1496,15 @@
     for copy in gq_x:
         copy.start()
     gq_rows[c] = gq_v[z, pl.ds(pl.multiple_of(c * wrows, wrows), wrows)]
-    for group in (*gu_sums, go_sums, *qkv_sums, da1_sums):
+    result_out[...] = (hidden_v[...] + y_sums.total()).astype(b16)
+    small_sum = small_r[z]
+    for m in range(1, zs):
+        small_z_x[m - 1].wait_recv()
+        small_sum = small_sum + small_z[m]
+    small_out[...] = small_sum
+    hidden_v[0:wrows] = go_sums.total()
+    moves.store(hidden_v.at[0:wrows], grad_out_out)
+    for group in (*gu_sums, go_sums, *qkv_sums, y_sums):
         group.sent()
     for copy in (*gu_x, *small_v_x, *small_z_x):
         copy.wait_send()
@@ -1471,13 +1513,13 @@
         copy.wait()
     for i in range(3):
         unpack_columns(
-            gq_out.at[:, i * width : (i + 1) * width], gq_rows, i * hc, HEAD_DIM, n, zs
+            gq_out.at[:, i * width : (i + 1) * width], gq_rows, [(i * hc, HEAD_DIM)], n, zs
         )
 
 
 def backward(zs, n, norms, tables, *arrays):
     f32, b16 = jnp.float32, jnp.bfloat16
-    a1_all, a2_all, dgu, w_gu, w_qkv, w_out, qkv, probs, ob, hidden, dy, xs = arrays
+    a1_all, a2_all, dgu, w_gu, w_qkv, w_out, qkv, probs, ob, hidden, dy, xs, _ = arrays
     _, slots, rows, hc = ob.shape
     local, width = hidden.shape
     _, depth, gc = w_gu.shape
@@ -1493,14 +1535,15 @@
         functools.partial(backward_kernel, zs, n),
         out_shape=[
             jax.ShapeDtypeStruct((hc // zs, width), f32),
+            jax.ShapeDtypeStruct((local, width), b16),
             jax.ShapeDtypeStruct((local, width), f32),
             jax.ShapeDtypeStruct((wrows, n * qc), b16),
             jax.ShapeDtypeStruct((wrows, n * gc // 2), b16),
             jax.ShapeDtypeStruct((wrows, n * gc // 2), b16),
             jax.ShapeDtypeStruct((8, 2 * HEAD_DIM), f32),
         ],
-        in_specs=[VMEM] * 2 + [HBM] * 12,
-        out_specs=[HBM] + [VMEM] * 5,
+        in_specs=[VMEM] * 2 + [HBM] * 13,
+        out_specs=[HBM] + [VMEM] * 6,
         scratch_shapes=[
             pltpu.VMEM(wide, b16),
             buf(dgu),
@@ -1534,6 +1577,7 @@
             pltpu.SemaphoreType.DMA((96,)),
             pltpu.SemaphoreType.DMA((96,)),
             pltpu.SemaphoreType.DMA((24,)),
+            pltpu.SemaphoreType.REGULAR,
         ],
         compiler_params=pltpu.CompilerParams(
             collective_id=4, has_side_effects=True, vmem_limit_bytes=VMEM_LIMIT
@@ -1600,14 +1644,14 @@
     ).astype(np.float32)
 
     tables = jnp.asarray(tables.reshape(3, n, rows, 2 * HEAD_DIM))
-    w_qkv_c, w_out_c, w_gu_c, a1, qkv, probs, ob, hidden, a2, dgu, grad_down, result, norms = front(
+    w_qkv_c, w_out_c, w_gu_c, a1, qkv, probs, ob, hidden, a2, dgu, y, grad_down, norms = front(
         zs, n, slots, lengths, tables, small, w_qkv, w_gate, w_up, w_out, w_down, xs, dy
     )
     wide = (n, local, width)
-    grad_out, input_grad, grad_qkv, grad_gate, grad_up, sums = backward(
+    grad_out, result, input_grad, grad_qkv, grad_gate, grad_up, sums = backward(
         zs, n, norms, tables, a1.reshape(wide), a2.reshape(wide), dgu,
         w_gu_c.reshape(zs, n * wrows, 2 * ffc), w_qkv_c.reshape(zs, n * wrows, 3 * hc),
-        w_out_c, qkv, probs, ob, hidden, dy, xs,
+        w_out_c, qkv, probs, ob, hidden, dy, xs, y.reshape(wide),
     )
     mine = lax.dynamic_slice_in_dim(sums[:4], me % 2 * wrows, wrows, 1)
     grad_bias = lax.dynamic_slice_in_dim(sums[4:7].reshape(2 * nb), me % 2 * nb, nb)

time: 473 us -> 460 us (0.973)
  Pallas kernels: 443 us -> 431 us
    pallas_call x1, Pallas kernels: 184 us -> 178 us  [backward(): pl.pallas_call(functools.partial(backward_kernel, zs, n), out_shape=[jax....]
    pallas_call x1, Pallas kernels: 259 us -> 253 us  [front(): pl.pallas_call(functools.partial(front_kernel, zs, n, slots), out_shape=[...]
where the time goes in v7:
time: 460 us; the launch traced here: 453 us
  Pallas kernels  431 us (94%)
  local copies, waits for them, and re-layouts  10.3 us (2%)
  other arithmetic  10 us (2%)
    pallas_call x1, Pallas kernels, front(): pl.pallas_call(functools.partial(front_kernel, zs, n, slots), out_shape=[...  253 us
    pallas_call x1, Pallas kernels, backward(): pl.pallas_call(functools.partial(backward_kernel, zs, n), out_shape=[jax....  178 us

profile of v7, /device:TPU:1, one launch (start us, length us, event | category | flops | bytes accessed | tf_op | source)
XLA Modules:
  0.0 452.9 jit_solution(9483189759882320735)
XLA Ops:
  0.6 2.0 copy.26
  2.6 2.0 copy.27
  4.6 0.7 convert_element_type.44
  5.3 0.7 convert_element_type.45
  5.9 0.7 convert_element_type.46
  6.6 0.7 convert_element_type.47
  7.3 1.3 add_bitcast_fusion.small
  8.6 253.5 %front.1 = (bf16[4,8,64,768]{3,2,1,0:T(8,128)(2,1)}, bf16[4,64,2048]{2,1,0:T(8,128)(2,1)}, bf16[4,8,64,1408]{3,2,1,0:T(8,128)(2,1)}, bf16[1024,2048]{1,0:T(8,128...) custom-call(s32[1,2]{1,0:T(1,128)} %lengths.1, ...), custom_call_target="tpu_custom_call" | custom-call | tf_op jit(solution)/shard_map/front/pallas_call | solution.py:1117
  262.1 178.0 %backward.1 = (f32[64,2048]{1,0:T(8,128)}, bf16[128,2048]{1,0:T(8,128)(2,1)}, f32[128,2048]{1,0:T(8,128)}, bf16[64,6144]{1,0:T(8,128)(2,1)}, bf16[64,5632]{1,0:T...) custom-call(f32[8,2048]{1,0:T(8,128)} %get-tuple-element.32.norms, f32[3,8,64,128]{3,2,1,0:T(8,128)} %constant.34.clone.tables, ...), custom_call_target="tpu_custom_call" | custom-call | tf_op jit(solution)/shard_map/backward/pallas_call | solution.py:1534
  440.1 0.0 copy-start.2
  440.1 0.0 copy-start.1
  440.1 2.5 convert_element_type.48
  442.6 0.0 copy-start.4
  442.6 2.4 convert_element_type.49
  445.0 0.0 copy-start.5
  445.0 0.0 copy-start.3
  445.0 0.0 copy-done.2
  445.0 0.0 copy-start
  445.0 1.2 convert_element_type.50
  446.2 0.0 copy-done.1
  446.2 1.8 copy.32
  448.0 0.0 copy-done.4
  448.0 1.3 copy.33
  449.3 0.0 copy-done.5
  449.3 0.1 constant_dynamic-slice_fusion
  449.4 0.5 slice_bitcast_fusion.1
  449.9 0.6 dynamic_slice.6
  450.5 0.0 copy-done.3
  450.5 0.8 copy.36
  451.3 0.0 copy-done
  451.3 1.1 copy.37
  (2 shorter events, 0.0 us)
Async XLA Ops:
  440.1 4.9 %copy-start.2 = (bf16[64,5632]{1,0:T(8,128)(2,1)S(1)}, bf16[64,5632]{1,0:T(8,128)(2,1)}, u32[]{:S(2)}) copy-start(bf16[64,5632]{1,0:T(8,128)(2,1)} %get-tuple-element.50) | copy-start | bytes 2162692
  440.1 6.1 %copy-start.1 = (f32[128,2048]{1,0:T(8,128)S(1)}, f32[128,2048]{1,0:T(8,128)}, u32[]{:S(2)}) copy-start(f32[128,2048]{1,0:T(8,128)} %get-tuple-element.45) | copy-start | bytes 3145732
  442.6 5.4 %copy-start.4 = (bf16[128,2048]{1,0:T(8,128)(2,1)S(1)}, bf16[128,2048]{1,0:T(8,128)(2,1)}, u32[]{:S(2)}) copy-start(bf16[128,2048]{1,0:T(8,128)(2,1)} %get-tuple-element.44) | copy-start | bytes 1572868
  445.0 4.3 copy-start.5
  445.0 5.6 %copy-start.3 = (f32[64,2048]{1,0:T(8,128)S(1)}, f32[64,2048]{1,0:T(8,128)}, u32[]{:S(2)}) copy-start(f32[64,2048]{1,0:T(8,128)} %get-tuple-element.72) | copy-start | bytes 1572868
  445.0 6.4 %copy-start = (f32[176,2048]{1,0:T(8,128)S(1)}, f32[176,2048]{1,0:T(8,128)}, u32[]{:S(2)}) copy-start(f32[176,2048]{1,0:T(8,128)} %get-tuple-element.75) | copy-start | bytes 4325380

commit v8 on v7

--- a/solution.py
+++ b/solution.py
@@ -662,6 +662,18 @@
     return [(0, first), (first, block - first)]
 
 
+def by_slot(dst, src):
+    rows, slots, _ = src.shape
+    for s in range(slots):
+        dst[s * rows : (s + 1) * rows] = src[:, s, :]
+
+
+def by_position(dst, values):
+    rows, slots, _ = dst.shape
+    for s in range(slots):
+        dst[:, s, :] = values[s * rows : (s + 1) * rows].astype(dst.dtype)
+
+
 def front_kernel(
     zs,
     n,
@@ -674,8 +686,8 @@
     w_up,
     w_out,
     w_down,
-    xs,
-    dy,
+    inputs,
+    cotangent,
     w_qkv_out,
     w_out_out,
     w_gu_out,
@@ -712,6 +724,7 @@
     gd_v,
     right_v,
     left_v,
+    raw_v,
     send,
     recv,
     local,
@@ -720,8 +733,8 @@
     wires = Wires(send, recv)
     moves = Moves(local)
     z, c = wires.z, wires.c
-    local_rows, width = xs.shape
-    rows = local_rows // slots
+    rows, _, width = inputs.shape
+    local_rows = rows * slots
     tokens, seq = n * local_rows, n * rows
     pair = 2 * local_rows
     hc = qkv_v.shape[-1]
@@ -741,8 +754,7 @@
 
     wait_out = moves.load(w_out, w_out_v.at[z])
     wait_small = moves.load(small, small_v.at[z, c])
-    wait_xs = moves.load(xs, block_of(wide_x, c))
-    wait_dy = moves.load(dy, dy_v.at[c])
+    waits = [moves.load(inputs, raw_v.at[0]), moves.load(cotangent, raw_v.at[1])]
     wait_down = moves.load(w_down, w_down_v.at[z])
     pack_columns(
         qkv_send,
@@ -751,6 +763,8 @@
         zs,
     )
     wait_own_qkv = moves.load(qkv_send.at[c], w_qkv_v.at[z, c])
+    waits[0].wait()
+    by_slot(block_of(wide_x, c), raw_v.at[0])
     wires.greet(zs, n)
     wait_out.wait()
     wait_small.wait()
@@ -762,7 +776,7 @@
     small_z = [wires.put(small_v.at[z, c], small_v.at[z, c], m, 0) for m in range(1, zs)]
     for copy in small_z:
         copy.start()
-    xs_g = LayerGather(wires, lambda i: block_of(wide_x, i), xs)
+    xs_g = LayerGather(wires, lambda i: block_of(wide_x, i))
     xs_g.start()
     pack_columns(
         gu_send, [(w, block, at, size) for at, size in halves for w in (w_gate, w_up)], n, zs
@@ -819,7 +833,6 @@
 
     for m in (1, 3, 5, 7):
         xs_g.arrived(m)
-    wait_xs.wait()
     hidden_v[...] = block_of(wide_x, c)[...].astype(f32)
 
     def norm_one(i, carry):
@@ -845,7 +858,8 @@
         part.forward()
     for part in gu_z:
         DepthGather.start(part)
-    wait_dy.wait()
+    waits[1].wait()
+    by_slot(dy_v.at[c], raw_v.at[1])
     dy_g = LayerGather(wires, lambda i: dy_v.at[i])
     dy_g.start()
     for part in (out_z, *qkv_z):
@@ -1054,10 +1068,10 @@
     moves.finish()
 
 
-def front(zs, n, slots, lengths, tables, small, w_qkv, w_gate, w_up, w_out, w_down, xs, dy):
+def front(zs, n, lengths, tables, small, w_qkv, w_gate, w_up, w_out, w_down, inputs, cotangent):
     f32, b16 = jnp.float32, jnp.bfloat16
-    local, width = xs.shape
-    rows = local // slots
+    rows, slots, width = inputs.shape
+    local = rows * slots
     seq, tokens = rows * n, local * n
     heads = HEADS // n
     hc = heads * HEAD_DIM
@@ -1113,6 +1127,7 @@
         down_all,
         ((zs - 1, block, width), b16),
         ((zs - 1, block, width), b16),
+        ((2, *inputs.shape), b16),
     ]
     return pl.pallas_call(
         functools.partial(front_kernel, zs, n, slots),
@@ -1129,7 +1144,7 @@
             collective_id=1, has_side_effects=True, vmem_limit_bytes=VMEM_LIMIT
         ),
         name="front",
-    )(lengths, tables, small, w_qkv, w_gate, w_up, w_out, w_down, xs, dy)
+    )(lengths, tables, small, w_qkv, w_gate, w_up, w_out, w_down, inputs, cotangent)
 
 
 def unpack_columns(dst, src, parts, n, zs):
@@ -1141,7 +1156,7 @@
             for at, size in parts
         ],
         -1,
-    )
+    ).astype(dst.dtype)
 
 
 def backward_kernel(
@@ -1159,15 +1174,14 @@
     probs,
     ob,
     hidden,
-    dy,
-    xs,
+    cotangent,
+    inputs,
     y_part,
     grad_out_out,
     result_out,
     input_grad_out,
     gq_out,
-    gate_out,
-    up_out,
+    gu_out,
     small_out,
     wide_v,
     dgu_v,
@@ -1178,6 +1192,7 @@
     ob_v,
     hidden_v,
     own_v,
+    raw_v,
     ggu_v,
     relay_v,
     box_v,
@@ -1219,11 +1234,11 @@
     qkv_weight, gq_v = weight_v.at[:, :, 0:qc], weight_v.at[:, :, qc : 2 * qc]
 
     wait_a2 = moves.load(a2_all, wide_v)
+    wait_dy = moves.load(cotangent, raw_v)
     wait_dgu = moves.load(dgu, dgu_v)
     wait_w = moves.load(w_gu, gu_weight)
     waits = [
         moves.load(hidden, hidden_v),
-        moves.load(dy, own_v),
         moves.load(w_out, w_out_v),
         moves.load(qkv, qkv_v),
         moves.load(probs.at[0], probs_v),
@@ -1290,15 +1305,17 @@
         da2_sums.step(m)
     for copy in waits:
         copy.wait()
+    wait_dy.wait()
+    by_slot(own_v, raw_v)
+    wait_xs = moves.load(inputs, raw_v)
     n2, r2 = layer_stats(hidden_v[...])
     for part_sum in gu_sums[1:]:
         part_sum.relay()
     da2 = da2_sums.total()
     gains = [jnp.sum(da2 * n2, 0, keepdims=True), jnp.sum(da2, 0, keepdims=True)]
     dh = own_v[...].astype(f32) + norm_back(da2, n2, r2, norms[2:3])
-    input_grad_out[...] = dh
+    by_position(input_grad_out, dh)
     dh_all[c] = dh.astype(b16)
-    wait_xs = moves.load(xs, own_v)
     dh_g = LayerGather(wires, lambda i: dh_all.at[i])
     dh_g.start()
     for m in (2, 4, 6):
@@ -1425,13 +1442,16 @@
     go_sums.relay()
 
     wait_xs.wait()
+    by_slot(own_v, raw_v)
     n1, r1 = layer_stats(own_v[...].astype(f32))
     da1 = da1_sums.total()
     for m in (1, 2, 4, 6):
         pl.semaphore_signal(free, inc=1, device_id=(z, flip(c, m)), device_id_type=MESH)
     da1_sums.sent()
     wait_y = moves.load(y_part, part)
-    input_grad_out[...] += norm_back(da1, n1, r1, norms[0:1])
+    grad = norm_back(da1, n1, r1, norms[0:1])
+    for s in range(slots):
+        input_grad_out[:, s, :] += grad[s * rows : (s + 1) * rows]
     gains = [jnp.sum(da1 * n1, 0, keepdims=True), jnp.sum(da1, 0, keepdims=True), *gains]
     chips = n // 2
     lanes = 2 * HEAD_DIM
@@ -1478,10 +1498,7 @@
         copy.start()
     for copy in gu_x:
         copy.wait_recv()
-    halves = halves_of(ffc // zs)
-    unpack_columns(gate_out, gu_rows, [(2 * zs * at, size) for at, size in halves], n, zs)
-    unpack_columns(up_out, gu_rows, [(zs * (2 * at + size), size) for at, size in halves], n, zs)
-
+    moves.store(gu_rows, gu_out)
     for p, part_sum in enumerate(qkv_sums):
         gq_v[z, p * size : (p + 1) * size] = part_sum.total().astype(b16)
     gq_x = [
@@ -1496,7 +1513,7 @@
     for copy in gq_x:
         copy.start()
     gq_rows[c] = gq_v[z, pl.ds(pl.multiple_of(c * wrows, wrows), wrows)]
-    result_out[...] = (hidden_v[...] + y_sums.total()).astype(b16)
+    by_position(result_out, hidden_v[...] + y_sums.total())
     small_sum = small_r[z]
     for m in range(1, zs):
         small_z_x[m - 1].wait_recv()
@@ -1508,18 +1525,15 @@
         group.sent()
     for copy in (*gu_x, *small_v_x, *small_z_x):
         copy.wait_send()
-    moves.finish()
     for copy in gq_x:
         copy.wait()
-    for i in range(3):
-        unpack_columns(
-            gq_out.at[:, i * width : (i + 1) * width], gq_rows, [(i * hc, HEAD_DIM)], n, zs
-        )
+    moves.store(gq_rows, gq_out)
+    moves.finish()
 
 
 def backward(zs, n, norms, tables, *arrays):
     f32, b16 = jnp.float32, jnp.bfloat16
-    a1_all, a2_all, dgu, w_gu, w_qkv, w_out, qkv, probs, ob, hidden, dy, xs, _ = arrays
+    a1_all, a2_all, dgu, w_gu, w_qkv, w_out, qkv, probs, ob, hidden, _, inputs, _ = arrays
     _, slots, rows, hc = ob.shape
     local, width = hidden.shape
     _, depth, gc = w_gu.shape
@@ -1535,15 +1549,14 @@
         functools.partial(backward_kernel, zs, n),
         out_shape=[
             jax.ShapeDtypeStruct((hc // zs, width), f32),
-            jax.ShapeDtypeStruct((local, width), b16),
-            jax.ShapeDtypeStruct((local, width), f32),
-            jax.ShapeDtypeStruct((wrows, n * qc), b16),
-            jax.ShapeDtypeStruct((wrows, n * gc // 2), b16),
-            jax.ShapeDtypeStruct((wrows, n * gc // 2), b16),
+            jax.ShapeDtypeStruct(inputs.shape, b16),
+            jax.ShapeDtypeStruct(inputs.shape, f32),
+            jax.ShapeDtypeStruct((n, wrows, qc), b16),
+            jax.ShapeDtypeStruct((n, wrows, gc), b16),
             jax.ShapeDtypeStruct((8, 2 * HEAD_DIM), f32),
         ],
         in_specs=[VMEM] * 2 + [HBM] * 13,
-        out_specs=[HBM] + [VMEM] * 6,
+        out_specs=[HBM, VMEM, VMEM, HBM, HBM, VMEM],
         scratch_shapes=[
             pltpu.VMEM(wide, b16),
             buf(dgu),
@@ -1554,6 +1567,7 @@
             buf(ob),
             buf(hidden),
             pltpu.VMEM((local, width), b16),
+            pltpu.VMEM(inputs.shape, b16),
             pltpu.VMEM((zs, depth, gc), b16),
             pltpu.VMEM((depth, gc), b16),
             pltpu.VMEM((3, depth, gc), b16),
@@ -1586,6 +1600,102 @@
     )(norms, tables, *arrays)
 
 
+def finish_kernel(
+    zs,
+    n,
+    gq,
+    gu,
+    small,
+    grad_out,
+    grad_down,
+    result,
+    input_grad,
+    qkv_out,
+    gate_out,
+    up_out,
+    grad_out_out,
+    grad_down_out,
+    result_out,
+    input_grad_out,
+    bias_out,
+    gain_one_out,
+    shift_one_out,
+    gain_two_out,
+    shift_two_out,
+    gq_v,
+    gu_v,
+    qkv_v,
+    gate_v,
+    up_v,
+    grad_out_v,
+    grad_down_v,
+    result_v,
+    input_grad_v,
+    local,
+):
+    moves = Moves(local)
+    width = grad_out.shape[1]
+    wait_gu = moves.load(gu, gu_v)
+    wait_gq = moves.load(gq, gq_v)
+    passed = [
+        (moves.load(src, held), held, dst)
+        for src, held, dst in (
+            (input_grad, input_grad_v, input_grad_out),
+            (grad_down, grad_down_v, grad_down_out),
+            (result, result_v, result_out),
+            (grad_out, grad_out_v, grad_out_out),
+        )
+    ]
+    odd = lax.axis_index("ctx") % 2
+    for r, out in enumerate((gain_one_out, shift_one_out, gain_two_out, shift_two_out)):
+        row = small[r : r + 1]
+        out[...] = jnp.where(odd == 0, row[:, :HEAD_DIM], row[:, HEAD_DIM:])
+    bias = jnp.concatenate([small[4 + r : 5 + r] for r in range(3)], -1)
+    size = bias_out.shape[1]
+    bias_out[...] = jnp.where(odd == 0, bias[:, :size], bias[:, size:])
+    ffc = gu_v.shape[-1] // 2
+    halves = halves_of(ffc // zs)
+    for copy, held, dst in passed:
+        copy.wait()
+        moves.store(held, dst)
+    wait_gu.wait()
+    unpack_columns(gate_v, gu_v, [(2 * zs * at, size) for at, size in halves], n, zs)
+    moves.store(gate_v, gate_out)
+    unpack_columns(up_v, gu_v, [(zs * (2 * at + size), size) for at, size in halves], n, zs)
+    moves.store(up_v, up_out)
+    wait_gq.wait()
+    hc = gq_v.shape[-1] // 3
+    for i in range(3):
+        unpack_columns(
+            qkv_v.at[:, i * width : (i + 1) * width], gq_v, [(i * hc, HEAD_DIM)], n, zs
+        )
+    moves.store(qkv_v, qkv_out)
+    moves.finish()
+
+
+def finish(zs, n, gq, gu, small, grad_out, grad_down, result, input_grad):
+    f32 = jnp.float32
+    _, wrows, qc = gq.shape
+    gc = gu.shape[-1]
+    wide = [((wrows, n * qc), f32), ((wrows, n * gc // 2), f32), ((wrows, n * gc // 2), f32)]
+    whole = [(v.shape, v.dtype) for v in (grad_out, grad_down, result, input_grad)]
+    rows = [((1, 3 * HEAD_DIM), f32), *[((1, wrows), f32)] * 4]
+    return pl.pallas_call(
+        functools.partial(finish_kernel, zs, n),
+        out_shape=[jax.ShapeDtypeStruct(*k) for k in (*wide, *whole, *rows)],
+        in_specs=[HBM, HBM, VMEM, HBM, HBM, HBM, HBM],
+        out_specs=[HBM] * 7 + [VMEM] * 5,
+        scratch_shapes=[
+            pltpu.VMEM(gq.shape, gq.dtype),
+            pltpu.VMEM(gu.shape, gu.dtype),
+            *[pltpu.VMEM(*k) for k in (*wide, *whole)],
+            pltpu.SemaphoreType.DMA((16,)),
+        ],
+        compiler_params=pltpu.CompilerParams(vmem_limit_bytes=VMEM_LIMIT),
+        name="finish",
+    )(gq, gu, small, grad_out, grad_down, result, input_grad)
+
+
 def tensor_shards(
     inputs,
     lengths,
@@ -1612,14 +1722,6 @@
     hc = HEADS // n * HEAD_DIM
     ffc = ff_block * zs
 
-    def local_tokens(v):
-        return jnp.transpose(v, (1, 0, 2)).reshape(local, width)
-
-    def back_tokens(v):
-        return jnp.transpose(v.reshape(slots, rows, width), (1, 0, 2))
-
-    xs = local_tokens(inputs)
-    dy = local_tokens(cotangent)
     nb = b_qkv.shape[0]
     vectors = [v for gain in (gain_one, shift_one, gain_two, shift_two) for v in (gain, gain)]
     small, at = jnp.zeros(1024, f32), 0
@@ -1645,29 +1747,34 @@
 
     tables = jnp.asarray(tables.reshape(3, n, rows, 2 * HEAD_DIM))
     w_qkv_c, w_out_c, w_gu_c, a1, qkv, probs, ob, hidden, a2, dgu, y, grad_down, norms = front(
-        zs, n, slots, lengths, tables, small, w_qkv, w_gate, w_up, w_out, w_down, xs, dy
+        zs, n, lengths, tables, small, w_qkv, w_gate, w_up, w_out, w_down, inputs, cotangent
     )
     wide = (n, local, width)
-    grad_out, result, input_grad, grad_qkv, grad_gate, grad_up, sums = backward(
+    grad_out, result, input_grad, gq, gu, sums = backward(
         zs, n, norms, tables, a1.reshape(wide), a2.reshape(wide), dgu,
         w_gu_c.reshape(zs, n * wrows, 2 * ffc), w_qkv_c.reshape(zs, n * wrows, 3 * hc),
-        w_out_c, qkv, probs, ob, hidden, dy, xs, y.reshape(wide),
-    )
-    mine = lax.dynamic_slice_in_dim(sums[:4], me % 2 * wrows, wrows, 1)
-    grad_bias = lax.dynamic_slice_in_dim(sums[4:7].reshape(2 * nb), me % 2 * nb, nb)
+        w_out_c, qkv, probs, ob, hidden, cotangent, inputs,
+        y.reshape(wide),
+    )
+    grad_qkv, grad_gate, grad_up, grad_out, grad_down, result, input_grad, *rows = finish(
+        zs, n, gq, gu, sums, grad_out, grad_down, result, input_grad
+    )
+    grad_bias, grad_gain_one, grad_shift_one, grad_gain_two, grad_shift_two = [
+        row.reshape(row.shape[1]) for row in rows
+    ]
     return (
-        back_tokens(result),
-        back_tokens(input_grad),
-        grad_qkv.astype(f32),
+        result,
+        input_grad,
+        grad_qkv,
         grad_bias,
         grad_out,
-        grad_gate.astype(f32),
-        grad_up.astype(f32),
+        grad_gate,
+        grad_up,
         grad_down,
-        mine[0],
-        mine[1],
-        mine[2],
-        mine[3],
+        grad_gain_one,
+        grad_shift_one,
+        grad_gain_two,
+        grad_shift_two,
     )
 
 

time: 460 us -> 454 us (0.987)
  local copies, waits for them, and re-layouts: 10.3 us -> 0 us
  Pallas kernels: 431 us -> 440 us
  other arithmetic: 10 us -> 3.96 us
    pallas_call x0 -> x1, Pallas kernels: none -> 6.62 us  [finish(): pl.pallas_call(functools.partial(finish_kernel, zs, n), out_shape=[jax.Sh...]
    convert_element_type x3 -> x0, other arithmetic: 6.06 us -> none  [the longest x1 2.51 us: tensor_shards(): grad_qkv.astype(f32)]
where the time goes in v8:
time: 454 us; the launch traced here: 446 us
  Pallas kernels  440 us (97%)
    pallas_call x1, Pallas kernels, front(): pl.pallas_call(functools.partial(front_kernel, zs, n, slots), out_shape=[...  255 us
    pallas_call x1, Pallas kernels, backward(): pl.pallas_call(functools.partial(backward_kernel, zs, n), out_shape=[jax....  178 us

profile of v8, /device:TPU:1, one launch (start us, length us, event | category | flops | bytes accessed | tf_op | source)
XLA Modules:
  0.0 445.6 jit_solution(6707243059210930611)
XLA Ops:
  0.6 0.7 convert_element_type.25
  1.3 0.7 convert_element_type.36
  2.0 0.7 convert_element_type.37
  2.6 0.7 convert_element_type.38
  3.3 1.3 add_bitcast_fusion.small
  4.6 255.4 %front.1 = (bf16[4,8,64,768]{3,2,1,0:T(8,128)(2,1)}, bf16[4,64,2048]{2,1,0:T(8,128)(2,1)}, bf16[4,8,64,1408]{3,2,1,0:T(8,128)(2,1)}, bf16[1024,2048]{1,0:T(8,128...) custom-call(s32[1,2]{1,0:T(1,128)} %lengths.1, ...), custom_call_target="tpu_custom_call" | custom-call | tf_op jit(solution)/shard_map/front/pallas_call | solution.py:1132
  260.0 178.4 %backward.1 = (f32[64,2048]{1,0:T(8,128)}, bf16[64,2,2048]{2,1,0:T(2,128)(2,1)}, f32[64,2,2048]{2,1,0:T(2,128)}, bf16[8,64,768]{2,1,0:T(8,128)(2,1)}, bf16[8,64,1408]{2,1,0:T(8,128)(2,1)}, /*index=5*/f32[8,128]{1,0:T(8,128)}) custom-call(f32[8,2048]{1,0:T(8,128)} %get-tuple-element.43.norms, f32[3,8,64,128]{3,2,1,0:T(8,128)} %constant.7.clone.tables, ...), custom_call_target="tpu_custom_call" | custom-call | tf_op jit(solution)/shard_map/backward/pallas_call | solution.py:1548
  438.5 6.6 %finish.1 = (f32[64,6144]{1,0:T(8,128)}, f32[64,5632]{1,0:T(8,128)}, f32[64,5632]{1,0:T(8,128)}, f32[64,2048]{1,0:T(8,128)}, f32[176,2048]{1,0:T(8,128)}, /*inde...) custom-call(bf16[8,64,768]{2,1,0:T(8,128)(2,1)} %get-tuple-element.5, ...), custom_call_target="tpu_custom_call" | custom-call | tf_op jit(solution)/shard_map/finish/pallas_call | solution.py:1683

commit v9 on v8

--- a/solution.py
+++ b/solution.py
@@ -358,6 +358,13 @@
         )
 
     def greet(self, zs, n):
+        self.call(zs, n)
+        self.met(zs, n)
+
+    def met(self, zs, n):
+        pl.semaphore_wait(pltpu.get_barrier_semaphore(), zs + n - 2)
+
+    def call(self, zs, n):
         barrier = pltpu.get_barrier_semaphore()
         for m in range(1, zs):
             pl.semaphore_signal(
@@ -367,7 +374,6 @@
             pl.semaphore_signal(
                 barrier, inc=1, device_id=(self.z, flip(self.c, m)), device_id_type=MESH
             )
-        pl.semaphore_wait(barrier, zs + n - 2)
 
 
 class DepthGather:
@@ -752,10 +758,15 @@
     def pair_at(i):
         return pl.ds(pl.multiple_of(i * pair, pair), pair)
 
+    wires.call(zs, n)
     wait_out = moves.load(w_out, w_out_v.at[z])
     wait_small = moves.load(small, small_v.at[z, c])
     waits = [moves.load(inputs, raw_v.at[0]), moves.load(cotangent, raw_v.at[1])]
     wait_down = moves.load(w_down, w_down_v.at[z])
+    wait_out.wait()
+    wires.met(zs, n)
+    out_z = DepthGather(wires, lambda i: w_out_v.at[i])
+    DepthGather.start([out_z])
     pack_columns(
         qkv_send,
         [(w_qkv.at[:, i * width : (i + 1) * width], HEAD_DIM, 0, HEAD_DIM) for i in range(3)],
@@ -763,19 +774,15 @@
         zs,
     )
     wait_own_qkv = moves.load(qkv_send.at[c], w_qkv_v.at[z, c])
-    waits[0].wait()
-    by_slot(block_of(wide_x, c), raw_v.at[0])
-    wires.greet(zs, n)
-    wait_out.wait()
-    wait_small.wait()
-    out_z = DepthGather(wires, lambda i: w_out_v.at[i])
-    DepthGather.start([out_z])
     qkv_x = [wires.put(qkv_send.at[flip(c, m)], w_qkv_v.at[z, c], 0, m) for m in range(1, n)]
     for copy in qkv_x:
         copy.start()
+    wait_small.wait()
     small_z = [wires.put(small_v.at[z, c], small_v.at[z, c], m, 0) for m in range(1, zs)]
     for copy in small_z:
         copy.start()
+    waits[0].wait()
+    by_slot(block_of(wide_x, c), raw_v.at[0])
     xs_g = LayerGather(wires, lambda i: block_of(wide_x, i))
     xs_g.start()
     pack_columns(
@@ -968,6 +975,8 @@
     for step, ((at, size), (start, count), parts) in enumerate(zip(halves, spans, gu_z)):
         units, gates = slice(at, at + size), slice(start, start + 2 * count)
         inner = slice(zs * at, zs * (at + size))
+        for _, _, chain in down_sums:
+            chain.hop(1, 3)
         for part in parts:
             part.finish()
 
@@ -1005,6 +1014,7 @@
             if step == 1:
                 down_z[2 + p].hop(1)
                 down_z[p].hop(2)
+                down_sums[p][2].hop(1, 2)
         for distance in (2, 1):
             for chain in chains:
                 chain.start(distance)
@@ -1032,19 +1042,20 @@
 
         lax.fori_loop(0, n // 2, rows_of, 0)
 
-    down_z[2].hop(2)
-    down_z[3].hop(2)
     chains = [chain for _, _, chain in down_sums]
+    for t in (0, 1):
+        chains[t].hop(2, 3)
+        down_z[2 + t].hop(2)
+    for t in (2, 3):
+        chains[t].hop(1, 3)
+    for t in (2, 3):
+        chains[t].hop(1, 2)
+    for t in (2, 3):
+        chains[t].hop(2, 3)
     for t in range(number):
-        chains[t].hop(1, 3)
         down_z[t].finish()
         products(t)
     moves.store(wide_x, y_out)
-    for pair_of in (chains[:2], chains[2:]):
-        for chain in pair_of:
-            chain.hop(1, 2)
-        for chain in pair_of:
-            chain.hop(2, 3)
 
     def back(i, carry):
         for (at, size), (start, count) in zip(halves, spans):
@@ -1226,12 +1237,12 @@
     width = dh_all.shape[-1]
     tokens, seq, local_rows = n * slots * rows, n * rows, slots * rows
     heads = hc // HEAD_DIM
-    depth, gc = ggu_v.shape[1:]
+    wrows, gc = ggu_v.shape[2:]
+    depth = n * wrows
     ffc, qc = gc // 2, 3 * hc
-    wrows = depth // n
     part = wide_v
-    gu_weight = weight_v.at[:, :, 0:gc]
-    qkv_weight, gq_v = weight_v.at[:, :, 0:qc], weight_v.at[:, :, qc : 2 * qc]
+    gu_weight = weight_v.at[:, :, :, 0:gc]
+    qkv_weight, gq_v = weight_v.at[:, :, :, 0:qc], weight_v.at[:, :, :, qc : 2 * qc]
 
     wait_a2 = moves.load(a2_all, wide_v)
     wait_dy = moves.load(cotangent, raw_v)
@@ -1249,18 +1260,20 @@
     wait_dgu.wait()
 
     number = 4
-    size = depth // number
-    step = 2 * size
+    step = depth // 2
+
+    quarter = wrows // number
 
     def scatters(whole, relay, box):
+        rows_of = [slice(p * quarter, (p + 1) * quarter) for p in range(number)]
         return [
             DepthScatter(
                 wires,
-                lambda i, a=p * size: whole.at[i, a : a + size],
-                relay.at[p * size : (p + 1) * size],
-                [box.at[j, p * size : (p + 1) * size] for j in range(3)],
+                lambda i, k=k: whole.at[i, :, k],
+                relay.at[:, k],
+                [box.at[j, :, k] for j in range(3)],
             )
-            for p in range(number)
+            for k in rows_of
         ]
 
     def weigh(sums, whole, left_v, grads, also=None):
@@ -1270,12 +1283,11 @@
             def piece(p, carry, to=to):
                 at = pl.multiple_of(to * depth + p * step, step)
                 left = left_v[:, :, pl.ds(at, step)].reshape(tokens, step)
-                whole[to, pl.ds(pl.multiple_of(p * step, step), step)] = dot(
-                    left, grads(), ((0,), (0,))
-                ).astype(b16)
+                gradient = dot(left, grads(), ((0,), (0,))).astype(b16)
+                whole[to, pl.ds(p * (n // 2), n // 2)] = gradient.reshape(n // 2, wrows, -1)
                 return carry
 
-            lax.fori_loop(0, number // 2, piece, 0)
+            lax.fori_loop(0, 2, piece, 0)
             for part_sum in sums:
                 part_sum.start(mask)
             if mask == 3 and also is not None:
@@ -1318,10 +1330,17 @@
     dh_all[c] = dh.astype(b16)
     dh_g = LayerGather(wires, lambda i: dh_all.at[i])
     dh_g.start()
+    da2_sums.sent()
+    wait_y = moves.load(y_part, part)
     for m in (2, 4, 6):
         dh_g.forward(m)
     for m in (1, 3, 5, 7):
         dh_g.arrived(m)
+    wait_y.wait()
+    y_sums = LayerScatter(
+        wires, lambda i: part.at[i], lambda j: near.at[j], lambda j: far.at[j]
+    )
+    y_sums.start()
 
     go_sums = DepthScatter(
         wires, lambda i: go_v.at[i], go_relay, [go_box.at[j] for j in range(3)]
@@ -1346,6 +1365,8 @@
         )
         return carry
 
+    for m in (6, 4, 2):
+        y_sums.step(m)
     lax.fori_loop(0, n, heads_back, 0)
     dh_g.sent()
     wait_a1 = moves.load(a1_all, dh_all)
@@ -1413,8 +1434,12 @@
         )
         return carry
 
-    da2_sums.sent()
+    by_position(result_out, hidden_v[...] + y_sums.total())
+    for m in (1, 2, 4, 6):
+        pl.semaphore_signal(free, inc=1, device_id=(z, flip(c, m)), device_id_type=MESH)
+    y_sums.sent()
     lax.fori_loop(0, n // 2, normed_one, 0)
+    pl.semaphore_wait(free, 4)
     da1_sums = LayerScatter(
         wires, lambda i: part.at[i], lambda j: near.at[j], lambda j: far.at[j]
     )
@@ -1423,19 +1448,11 @@
         da1_sums.step(m)
 
     for p, part_sum in enumerate(gu_sums):
-        ggu_v[z, p * size : (p + 1) * size] = part_sum.total().astype(b16)
-    gu_x = [
-        wires.put(
-            ggu_v.at[z, pl.ds(pl.multiple_of(flip(c, m) * wrows, wrows), wrows)],
-            gu_rows.at[c],
-            0,
-            m,
-        )
-        for m in range(1, n)
-    ]
+        ggu_v[z, :, p * quarter : (p + 1) * quarter] = part_sum.total().astype(b16)
+    gu_x = [wires.put(ggu_v.at[z, flip(c, m)], gu_rows.at[c], 0, m) for m in range(1, n)]
     for copy in gu_x:
         copy.start()
-    gu_rows[c] = ggu_v[z, pl.ds(pl.multiple_of(c * wrows, wrows), wrows)]
+    gu_rows[c] = ggu_v[z, c]
 
     for part_sum in qkv_sums:
         part_sum.relay()
@@ -1445,10 +1462,6 @@
     by_slot(own_v, raw_v)
     n1, r1 = layer_stats(own_v[...].astype(f32))
     da1 = da1_sums.total()
-    for m in (1, 2, 4, 6):
-        pl.semaphore_signal(free, inc=1, device_id=(z, flip(c, m)), device_id_type=MESH)
-    da1_sums.sent()
-    wait_y = moves.load(y_part, part)
     grad = norm_back(da1, n1, r1, norms[0:1])
     for s in range(slots):
         input_grad_out[:, s, :] += grad[s * rows : (s + 1) * rows]
@@ -1480,14 +1493,6 @@
     for copy in small_v_x:
         copy.start()
 
-    wait_y.wait()
-    pl.semaphore_wait(free, 4)
-    y_sums = LayerScatter(
-        wires, lambda i: part.at[i], lambda j: near.at[j], lambda j: far.at[j]
-    )
-    y_sums.start()
-    for m in (6, 4, 2):
-        y_sums.step(m)
     small_sum = small_v[:, c // 2]
     for m in range(1, n):
         small_v_x[m - 1].wait_recv()
@@ -1499,21 +1504,17 @@
     for copy in gu_x:
         copy.wait_recv()
     moves.store(gu_rows, gu_out)
+    gq_x = []
     for p, part_sum in enumerate(qkv_sums):
-        gq_v[z, p * size : (p + 1) * size] = part_sum.total().astype(b16)
-    gq_x = [
-        wires.put(
-            gq_v.at[z, pl.ds(pl.multiple_of(flip(c, m) * wrows, wrows), wrows)],
-            gq_rows.at[c],
-            0,
-            m,
-        )
-        for m in range(1, n)
-    ]
-    for copy in gq_x:
-        copy.start()
-    gq_rows[c] = gq_v[z, pl.ds(pl.multiple_of(c * wrows, wrows), wrows)]
-    by_position(result_out, hidden_v[...] + y_sums.total())
+        k = slice(p * quarter, (p + 1) * quarter)
+        gq_v[z, :, k] = part_sum.total().astype(b16)
+        copies = [
+            wires.put(gq_v.at[z, flip(c, m), k], gq_rows.at[c, k], 0, m) for m in range(1, n)
+        ]
+        for copy in copies:
+            copy.start()
+        gq_x += copies
+    gq_rows[c] = gq_v[z, c]
     small_sum = small_r[z]
     for m in range(1, zs):
         small_z_x[m - 1].wait_recv()
@@ -1521,7 +1522,7 @@
     small_out[...] = small_sum
     hidden_v[0:wrows] = go_sums.total()
     moves.store(hidden_v.at[0:wrows], grad_out_out)
-    for group in (*gu_sums, go_sums, *qkv_sums, y_sums):
+    for group in (*gu_sums, go_sums, *qkv_sums, da1_sums):
         group.sent()
     for copy in (*gu_x, *small_v_x, *small_z_x):
         copy.wait_send()
@@ -1536,9 +1537,8 @@
     a1_all, a2_all, dgu, w_gu, w_qkv, w_out, qkv, probs, ob, hidden, _, inputs, _ = arrays
     _, slots, rows, hc = ob.shape
     local, width = hidden.shape
-    _, depth, gc = w_gu.shape
+    _, _, wrows, gc = w_gu.shape
     qc = 3 * hc
-    wrows = depth // n
     seq = n * rows
     wide = (n, local, width)
 
@@ -1560,7 +1560,7 @@
         scratch_shapes=[
             pltpu.VMEM(wide, b16),
             buf(dgu),
-            pltpu.VMEM((zs, depth, max(gc, 2 * qc)), b16),
+            pltpu.VMEM((zs, n, wrows, max(gc, 2 * qc)), b16),
             buf(w_out),
             buf(qkv),
             pltpu.VMEM(probs.shape[1:], b16),
@@ -1568,9 +1568,9 @@
             buf(hidden),
             pltpu.VMEM((local, width), b16),
             pltpu.VMEM(inputs.shape, b16),
-            pltpu.VMEM((zs, depth, gc), b16),
-            pltpu.VMEM((depth, gc), b16),
-            pltpu.VMEM((3, depth, gc), b16),
+            pltpu.VMEM((zs, n, wrows, gc), b16),
+            pltpu.VMEM((n, wrows, gc), b16),
+            pltpu.VMEM((3, n, wrows, gc), b16),
             pltpu.VMEM((n // 2, local, width), b16),
             pltpu.VMEM((n // 2 - 1, local, width), b16),
             pltpu.VMEM(wide, b16),
@@ -1580,16 +1580,16 @@
             pltpu.VMEM((3, seq, hc), f32),
             pltpu.VMEM((n, slots, rows, qc), b16),
             pltpu.VMEM((1, qc), f32),
-            pltpu.VMEM((depth, qc), b16),
-            pltpu.VMEM((3, depth, qc), b16),
+            pltpu.VMEM((n, wrows, qc), b16),
+            pltpu.VMEM((3, n, wrows, qc), b16),
             pltpu.VMEM((n, wrows, gc), b16),
             pltpu.VMEM((n, wrows, qc), b16),
             pltpu.VMEM((zs, n // 2, 8, 2 * HEAD_DIM), f32),
             pltpu.VMEM((n, zs, 8, 2 * HEAD_DIM), f32),
             pltpu.VMEM((zs, 8, 2 * HEAD_DIM), f32),
             pltpu.VMEM((zs, 8, 2 * HEAD_DIM), f32),
-            pltpu.SemaphoreType.DMA((96,)),
-            pltpu.SemaphoreType.DMA((96,)),
+            pltpu.SemaphoreType.DMA((128,)),
+            pltpu.SemaphoreType.DMA((128,)),
             pltpu.SemaphoreType.DMA((24,)),
             pltpu.SemaphoreType.REGULAR,
         ],
@@ -1752,8 +1752,7 @@
     wide = (n, local, width)
     grad_out, result, input_grad, gq, gu, sums = backward(
         zs, n, norms, tables, a1.reshape(wide), a2.reshape(wide), dgu,
-        w_gu_c.reshape(zs, n * wrows, 2 * ffc), w_qkv_c.reshape(zs, n * wrows, 3 * hc),
-        w_out_c, qkv, probs, ob, hidden, cotangent, inputs,
+        w_gu_c, w_qkv_c, w_out_c, qkv, probs, ob, hidden, cotangent, inputs,
         y.reshape(wide),
     )
     grad_qkv, grad_gate, grad_up, grad_out, grad_down, result, input_grad, *rows = finish(

time: 454 us -> 448 us (0.987)
  Pallas kernels: 440 us -> 435 us
where the time goes in v9:
time: 448 us; the launch traced here: 440 us
  Pallas kernels  435 us (97%)
    pallas_call x1, Pallas kernels, front(): pl.pallas_call(functools.partial(front_kernel, zs, n, slots), out_shape=[...  251 us
    pallas_call x1, Pallas kernels, backward(): pl.pallas_call(functools.partial(backward_kernel, zs, n), out_shape=[jax....  177 us

profile of v9, /device:TPU:1, one launch (start us, length us, event | category | flops | bytes accessed | tf_op | source)
XLA Modules:
  0.0 439.8 jit_solution(11789891294634102741)
XLA Ops:
  0.6 0.7 convert_element_type.25
  1.3 0.7 convert_element_type.36
  2.0 0.7 convert_element_type.37
  2.6 0.7 convert_element_type.38
  3.3 1.3 add_bitcast_fusion.small
  4.6 251.1 %front.1 = (bf16[4,8,64,768]{3,2,1,0:T(8,128)(2,1)}, bf16[4,64,2048]{2,1,0:T(8,128)(2,1)}, bf16[4,8,64,1408]{3,2,1,0:T(8,128)(2,1)}, bf16[1024,2048]{1,0:T(8,128...) custom-call(s32[1,2]{1,0:T(1,128)} %lengths.1, ...), custom_call_target="tpu_custom_call" | custom-call | tf_op jit(solution)/shard_map/front/pallas_call | solution.py:1143
  255.7 177.2 %backward.1 = (f32[64,2048]{1,0:T(8,128)}, bf16[64,2,2048]{2,1,0:T(2,128)(2,1)}, f32[64,2,2048]{2,1,0:T(2,128)}, bf16[8,64,768]{2,1,0:T(8,128)(2,1)}, bf16[8,64,1408]{2,1,0:T(8,128)(2,1)}, /*index=5*/f32[8,128]{1,0:T(8,128)}) custom-call(f32[8,2048]{1,0:T(8,128)} %get-tuple-element.43.norms, f32[3,8,64,128]{3,2,1,0:T(8,128)} %constant.7.clone.tables, ...), custom_call_target="tpu_custom_call" | custom-call | tf_op jit(solution)/shard_map/backward/pallas_call | solution.py:1548
  432.9 6.6 %finish.1 = (f32[64,6144]{1,0:T(8,128)}, f32[64,5632]{1,0:T(8,128)}, f32[64,5632]{1,0:T(8,128)}, f32[64,2048]{1,0:T(8,128)}, f32[176,2048]{1,0:T(8,128)}, /*inde...) custom-call(bf16[8,64,768]{2,1,0:T(8,128)(2,1)} %get-tuple-element.5, ...), custom_call_target="tpu_custom_call" | custom-call | tf_op jit(solution)/shard_map/finish/pallas_call | solution.py:1683

commit v10 on v9

--- a/solution.py
+++ b/solution.py
@@ -1724,12 +1724,12 @@
 
     nb = b_qkv.shape[0]
     vectors = [v for gain in (gain_one, shift_one, gain_two, shift_two) for v in (gain, gain)]
-    small, at = jnp.zeros(1024, f32), 0
+    small, at = jnp.zeros(1024, jnp.bfloat16), 0
     for vector in (*vectors, b_qkv):
         size = vector.shape[0]
-        small = small + jnp.pad(vector.astype(f32), (at, 1024 - at - size))
+        small = small + jnp.pad(vector, (at, 1024 - at - size))
         at += size
-    small = small.reshape(8, 128)
+    small = small.reshape(8, 128).astype(f32)
 
     angles = np.arange(seq)[:, None] * 10000.0 ** (-2.0 * np.arange(ROTARY // 2) / ROTARY)[None, :]
     cos_t, sin_t = np.cos(angles), np.sin(angles)

time: 448 us -> 446 us (level)
  no operation moved by 1% of the time
where the time goes in v10:
time: 446 us; the launch traced here: 437 us
  Pallas kernels  435 us (98%)
    pallas_call x1, Pallas kernels, front(): pl.pallas_call(functools.partial(front_kernel, zs, n, slots), out_shape=[...  251 us
    pallas_call x1, Pallas kernels, backward(): pl.pallas_call(functools.partial(backward_kernel, zs, n), out_shape=[jax....  177 us

profile of v10, /device:TPU:1, one launch (start us, length us, event | category | flops | bytes accessed | tf_op | source)
XLA Modules:
  0.0 437.3 jit_solution(11878049749310022814)
XLA Ops:
  0.6 1.5 bitcast_convert_fusion.small
  2.1 251.1 %front.1 = (bf16[4,8,64,768]{3,2,1,0:T(8,128)(2,1)}, bf16[4,64,2048]{2,1,0:T(8,128)(2,1)}, bf16[4,8,64,1408]{3,2,1,0:T(8,128)(2,1)}, bf16[1024,2048]{1,0:T(8,128...) custom-call(s32[1,2]{1,0:T(1,128)} %lengths.1, ...), custom_call_target="tpu_custom_call" | custom-call | tf_op jit(solution)/shard_map/front/pallas_call | solution.py:1143
  253.2 177.2 %backward.1 = (f32[64,2048]{1,0:T(8,128)}, bf16[64,2,2048]{2,1,0:T(2,128)(2,1)}, f32[64,2,2048]{2,1,0:T(2,128)}, bf16[8,64,768]{2,1,0:T(8,128)(2,1)}, bf16[8,64,1408]{2,1,0:T(8,128)(2,1)}, /*index=5*/f32[8,128]{1,0:T(8,128)}) custom-call(f32[8,2048]{1,0:T(8,128)} %get-tuple-element.43.norms, f32[3,8,64,128]{3,2,1,0:T(8,128)} %constant.5.clone.tables, ...), custom_call_target="tpu_custom_call" | custom-call | tf_op jit(solution)/shard_map/backward/pallas_call | solution.py:1548
  430.4 6.6 %finish.1 = (f32[64,6144]{1,0:T(8,128)}, f32[64,5632]{1,0:T(8,128)}, f32[64,5632]{1,0:T(8,128)}, f32[64,2048]{1,0:T(8,128)}, f32[176,2048]{1,0:T(8,128)}, /*inde...) custom-call(bf16[8,64,768]{2,1,0:T(8,128)(2,1)} %get-tuple-element.5, ...), custom_call_target="tpu_custom_call" | custom-call | tf_op jit(solution)/shard_map/finish/pallas_call | solution.py:1683

commit v11 on v10

--- a/solution.py
+++ b/solution.py
@@ -865,6 +865,12 @@
         part.forward()
     for part in gu_z:
         DepthGather.start(part)
+    tile = width // number
+    columns = [slice(p * tile, (p + 1) * tile) for p in range(number)]
+    down_z = [ChainGather(wires, lambda i, k=k: w_down_v.at[i, :, k]) for k in columns]
+    wait_down.wait()
+    for chain in down_z:
+        chain.start()
     waits[1].wait()
     by_slot(dy_v.at[c], raw_v.at[1])
     dy_g = LayerGather(wires, lambda i: dy_v.at[i])
@@ -959,12 +965,6 @@
         a2_g.forward(m)
     for part in gu_z[1][1:]:
         part.forward()
-    wait_down.wait()
-    tile = width // number
-    columns = [slice(p * tile, (p + 1) * tile) for p in range(number)]
-    down_z = [ChainGather(wires, lambda i, k=k: w_down_v.at[i, :, k]) for k in columns]
-    for chain in down_z:
-        chain.start()
     for m in (1, 3, 5, 7):
         dy_g.arrived(m)
     for m in (1, 3, 5, 7):

time: 446 us -> 446 us (level)
    pallas_call x1, Pallas kernels: 177 us -> 185 us  [backward(): pl.pallas_call(functools.partial(backward_kernel, zs, n), out_shape=[jax....]
    pallas_call x1, Pallas kernels: 251 us -> 245 us  [front(): pl.pallas_call(functools.partial(front_kernel, zs, n, slots), out_shape=[...]
where the time goes in v11:
time: 446 us; the launch traced here: 439 us
  Pallas kernels  436 us (98%)
    pallas_call x1, Pallas kernels, front(): pl.pallas_call(functools.partial(front_kernel, zs, n, slots), out_shape=[...  245 us
    pallas_call x1, Pallas kernels, backward(): pl.pallas_call(functools.partial(backward_kernel, zs, n), out_shape=[jax....  185 us

profile of v11, /device:TPU:1, one launch (start us, length us, event | category | flops | bytes accessed | tf_op | source)
XLA Modules:
  0.0 438.6 jit_solution(6134626593279010585)
XLA Ops:
  0.6 1.5 bitcast_convert_fusion.small
  2.1 244.8 %front.1 = (bf16[4,8,64,768]{3,2,1,0:T(8,128)(2,1)}, bf16[4,64,2048]{2,1,0:T(8,128)(2,1)}, bf16[4,8,64,1408]{3,2,1,0:T(8,128)(2,1)}, bf16[1024,2048]{1,0:T(8,128...) custom-call(s32[1,2]{1,0:T(1,128)} %lengths.1, ...), custom_call_target="tpu_custom_call" | custom-call | tf_op jit(solution)/shard_map/front/pallas_call | solution.py:1143
  246.9 184.8 %backward.1 = (f32[64,2048]{1,0:T(8,128)}, bf16[64,2,2048]{2,1,0:T(2,128)(2,1)}, f32[64,2,2048]{2,1,0:T(2,128)}, bf16[8,64,768]{2,1,0:T(8,128)(2,1)}, bf16[8,64,1408]{2,1,0:T(8,128)(2,1)}, /*index=5*/f32[8,128]{1,0:T(8,128)}) custom-call(f32[8,2048]{1,0:T(8,128)} %get-tuple-element.43.norms, f32[3,8,64,128]{3,2,1,0:T(8,128)} %constant.5.clone.tables, ...), custom_call_target="tpu_custom_call" | custom-call | tf_op jit(solution)/shard_map/backward/pallas_call | solution.py:1548
  431.7 6.6 %finish.1 = (f32[64,6144]{1,0:T(8,128)}, f32[64,5632]{1,0:T(8,128)}, f32[64,5632]{1,0:T(8,128)}, f32[64,2048]{1,0:T(8,128)}, f32[176,2048]{1,0:T(8,128)}, /*inde...) custom-call(bf16[8,64,768]{2,1,0:T(8,128)(2,1)} %get-tuple-element.5, ...), custom_call_target="tpu_custom_call" | custom-call | tf_op jit(solution)/shard_map/finish/pallas_call | solution.py:1683
